TPU v7x, 32 devices: a whole 2x2x4 slice. The times are simulated.
32 devices in a mesh: segment: 2 (over x), dp: 16 (over z, y, core).
Axes of the slice: x: 2, y: 2, z: 4, core: 2. Of those that a mesh axis runs over, the one named last changes fastest.
Arguments:
- boundary: bfloat16 [2, 2, 16, 512, 768], P('segment', None, 'dp'), may hold values from -6 to 6
- lengths: int32 [2, 16], P(None, 'dp'), may hold values from 20 to 512, as said below
- ln1_gain: float32 [2, 768], P('segment', 'dp'), may hold values from 0.5 to 1.5
- ln1_bias: float32 [2, 768], P('segment', 'dp'), may hold values from -2 to 2
- value_weight: float32 [2, 768, 768], P('segment', 'dp'), may hold values from -0.21875 to 0.21875
- value_bias: float32 [2, 768], P('segment', 'dp'), may hold values from -2 to 2
- out_weight: float32 [2, 768, 768], P('segment', 'dp'), may hold values from -0.625 to 0.625
- out_bias: float32 [2, 768], P('segment', 'dp'), may hold values from -2 to 2
- ln2_gain: float32 [2, 768], P('segment', 'dp'), may hold values from 0.5 to 1.5
- ln2_bias: float32 [2, 768], P('segment', 'dp'), may hold values from -2 to 2
- ffn_in: float32 [2, 768, 3072], P('segment', 'dp'), may hold values from -0.21875 to 0.21875
- ffn_in_bias: float32 [2, 3072], P('segment', 'dp'), may hold values from -2 to 2
- ffn_out: float32 [2, 3072, 768], P('segment', 'dp'), may hold values from -0.15625 to 0.15625
- ffn_out_bias: float32 [2, 768], P('segment', 'dp'), may hold values from -2 to 2
- dense_first: float32 [768, 768], P(('segment', 'dp')), may hold values from -0.21875 to 0.21875
- dense_first_bias: float32 [768], P(('segment', 'dp')), may hold values from -2 to 2
- dense_second: float32 [768, 6144], P(('segment', 'dp')), may hold values from -0.5 to 0.5
- dense_second_bias: float32 [6144], P(('segment', 'dp')), may hold values from -3 to 3
- random_table: float32 [6144, 512], P(('segment', 'dp')), may hold values from -8 to 8
Outputs:
- layer_outputs: bfloat16 [2, 2, 16, 512, 768], P('segment', None, 'dp')
- input_grads: bfloat16 [2, 2, 16, 512, 768], P('segment', None, 'dp')
- grad_ln1_gain: float32 [2, 768], P('segment', 'dp')
- grad_ln1_bias: float32 [2, 768], P('segment', 'dp')
- grad_value_weight: float32 [2, 768, 768], P('segment', 'dp')
- grad_value_bias: float32 [2, 768], P('segment', 'dp')
- grad_out_weight: float32 [2, 768, 768], P('segment', 'dp')
- grad_out_bias: float32 [2, 768], P('segment', 'dp')
- grad_ln2_gain: float32 [2, 768], P('segment', 'dp')
- grad_ln2_bias: float32 [2, 768], P('segment', 'dp')
- grad_ffn_in: float32 [2, 768, 3072], P('segment', 'dp')
- grad_ffn_in_bias: float32 [2, 3072], P('segment', 'dp')
- grad_ffn_out: float32 [2, 3072, 768], P('segment', 'dp')
- grad_ffn_out_bias: float32 [2, 768], P('segment', 'dp')
- grad_dense_first: float32 [768, 768], P(('segment', 'dp'))
- grad_dense_first_bias: float32 [768], P(('segment', 'dp'))
- grad_dense_second: float32 [768, 6144], P(('segment', 'dp'))
- grad_dense_second_bias: float32 [6144], P(('segment', 'dp'))
- grad_random_table: float32 [6144, 512], P(('segment', 'dp'))
Inputs may be any that keep to these rules, and one draw needn't show every extreme that they name: `lengths`: each item's used positions; at least one item has exactly 512.
All inputs are finite; a program needn't handle non-finite values.
Results may differ from a plain program's by a relative error of at most 0.028.
Values may be sent and summed in bfloat16 or wider, within the bound.
A program may use at most 512 MiB of HBM per device.

v0:
```python
import jax
import jax.numpy as jnp
from jax import lax
from jax.sharding import PartitionSpec as P

D = 768
HEADS = 12
HEAD_DIM = 64
SLOTS = 512


EPSILON = 1e-05
GELU_SCALE = 0.7978845608028654


def passed_along(x, axis, by):
    devices = lax.axis_size(axis)
    pairs = [(i, i + by) for i in range(devices) if 0 <= i + by < devices]
    return lax.ppermute(x, axis, pairs)


def to_half(value):
    return value.astype(jnp.bfloat16)


def widen(value):
    return value.astype(jnp.float32)


def product(left, right):
    return jnp.dot(left, right, preferred_element_type=jnp.float32)


def transpose_left(left, right):
    return lax.dot_general(
        left, right, (((0,), (0,)), ((), ())), preferred_element_type=jnp.float32
    )


def transpose_right(left, right):
    return lax.dot_general(
        left, right, (((1,), (1,)), ((), ())), preferred_element_type=jnp.float32
    )


def column_sums(value):
    return jnp.sum(widen(value), axis=0)


def float_zeros(tree):
    return jax.tree.map(lambda piece: jnp.zeros(piece.shape, jnp.float32), tree)


def layer_norm(rows, gain, shift):
    centre = rows - jnp.mean(rows, axis=-1, keepdims=True)
    spread = jnp.mean(centre * centre, axis=-1, keepdims=True)
    return centre * lax.rsqrt(spread + EPSILON) * gain + shift


def smooth_gate(value):
    return 0.5 * value * (1.0 + jnp.tanh(GELU_SCALE * (value + 0.044715 * value * value * value)))


def probabilities(logits, lengths):
    places = lax.broadcasted_iota(jnp.int32, logits.shape, 3)
    valid = places < lengths[:, None, None, None]
    masked = jnp.where(valid, logits, -1e30)
    top = jnp.max(masked, axis=3, keepdims=True)
    expo = jnp.where(valid, jnp.exp(masked - top), 0.0)
    return expo / jnp.sum(expo, axis=3, keepdims=True)


def dense_front(normed_half, synth):
    pre_gate = product(normed_half, synth[0]) + widen(synth[1])
    return (pre_gate, to_half(smooth_gate(pre_gate)))


def forward_layer(rows, lengths, common, synth, dense_flag):
    (
        gain_one,
        bias_one,
        value_w,
        value_b,
        out_w,
        out_b,
        gain_two,
        bias_two,
        inner_w,
        inner_b,
        outer_w,
        outer_b,
    ) = common
    items = rows.shape[0]
    flat = rows.reshape(items * SLOTS, D)
    normed_half = to_half(layer_norm(flat, widen(gain_one), widen(bias_one)))
    values_half = to_half(product(normed_half, value_w) + widen(value_b))

    def dense_logits(operand):
        pre_gate, gated = dense_front(operand, synth)
        flat_logits = product(gated, synth[2]) + widen(synth[3])
        return flat_logits.reshape(items, SLOTS, HEADS, SLOTS).transpose(0, 2, 1, 3)

    def random_logits(operand):
        table = widen(synth[4]).reshape(HEADS, SLOTS, SLOTS)
        return table[None]

    logits = lax.cond(dense_flag, dense_logits, random_logits, normed_half)
    probs = probabilities(logits, lengths)
    probs_half = to_half(probs)
    heads_half = values_half.reshape(items, SLOTS, HEADS, HEAD_DIM)
    mixed = jnp.einsum(
        "ihqk,ikhd->iqhd", probs_half, heads_half, preferred_element_type=jnp.float32
    )
    mixed_half = to_half(mixed.reshape(items * SLOTS, D))
    hidden = flat + product(mixed_half, out_w) + widen(out_b)
    normed_two = to_half(layer_norm(hidden, widen(gain_two), widen(bias_two)))
    inner = product(normed_two, inner_w) + widen(inner_b)
    active_half = to_half(smooth_gate(inner))
    output = hidden + product(active_half, outer_w) + widen(outer_b)
    saved = (
        flat,
        normed_half,
        heads_half,
        probs,
        probs_half,
        mixed_half,
        hidden,
        normed_two,
        inner,
        active_half,
    )
    return (output.reshape(items, SLOTS, D), saved)


def backward_layer(rows, lengths, cotangent, common, synth, dense_flag):
    (
        gain_one,
        bias_one,
        value_w,
        value_b,
        out_w,
        out_b,
        gain_two,
        bias_two,
        inner_w,
        inner_b,
        outer_w,
        outer_b,
    ) = common
    output, saved = forward_layer(rows, lengths, common, synth, dense_flag)
    (
        flat,
        normed_half,
        heads_half,
        probs,
        probs_half,
        mixed_half,
        hidden,
        normed_two,
        inner,
        active_half,
    ) = saved
    items = rows.shape[0]
    upstream = cotangent.reshape(items * SLOTS, D)
    upstream_half = to_half(upstream)
    grad_outer_w = transpose_left(active_half, upstream_half)
    grad_outer_b = column_sums(upstream_half)
    unused, gate_back = jax.vjp(smooth_gate, inner)
    inner_half = to_half(gate_back(transpose_right(upstream_half, outer_w))[0])
    grad_inner_w = transpose_left(normed_two, inner_half)
    grad_inner_b = column_sums(inner_half)
    unused, norm_two_back = jax.vjp(layer_norm, hidden, widen(gain_two), widen(bias_two))
    hidden_part, grad_gain_two, grad_bias_two = norm_two_back(transpose_right(inner_half, inner_w))
    grad_hidden = upstream + hidden_part
    hidden_half = to_half(grad_hidden)
    grad_out_w = transpose_left(mixed_half, hidden_half)
    grad_out_b = column_sums(hidden_half)
    grad_mixed = to_half(transpose_right(hidden_half, out_w)).reshape(items, SLOTS, HEADS, HEAD_DIM)
    grad_probs = jnp.einsum(
        "iqhd,ikhd->ihqk", grad_mixed, heads_half, preferred_element_type=jnp.float32
    )
    grad_values = jnp.einsum(
        "ihqk,iqhd->ikhd", probs_half, grad_mixed, preferred_element_type=jnp.float32
    )
    values_half = to_half(grad_values.reshape(items * SLOTS, D))
    grad_logits = probs * (grad_probs - jnp.sum(probs * grad_probs, axis=3, keepdims=True))

    def dense_back(operand):
        normed_in, logit_grads = operand
        pre_gate, gated = dense_front(normed_in, synth)
        flat_grads = to_half(
            logit_grads.transpose(0, 2, 1, 3).reshape(items * SLOTS, HEADS * SLOTS)
        )
        grad_second = transpose_left(gated, flat_grads)
        grad_second_b = column_sums(flat_grads)
        unused_value, front_back = jax.vjp(smooth_gate, pre_gate)
        pre_half = to_half(front_back(transpose_right(flat_grads, synth[2]))[0])
        grad_first = transpose_left(normed_in, pre_half)
        grad_first_b = column_sums(pre_half)
        table_zero = jnp.zeros(synth[4].shape, jnp.float32)
        return (
            grad_first,
            grad_first_b,
            grad_second,
            grad_second_b,
            table_zero,
            transpose_right(pre_half, synth[0]),
        )

    def random_back(operand):
        normed_in, logit_grads = operand
        table_grad = jnp.sum(logit_grads, axis=0).reshape(HEADS * SLOTS, SLOTS)
        blanks = float_zeros((synth[0], synth[1], synth[2], synth[3]))
        return (
            blanks[0],
            blanks[1],
            blanks[2],
            blanks[3],
            table_grad,
            jnp.zeros((items * SLOTS, D), jnp.float32),
        )

    synth_grads = lax.cond(dense_flag, dense_back, random_back, (normed_half, grad_logits))
    grad_value_w = transpose_left(normed_half, values_half)
    grad_value_b = column_sums(values_half)
    grad_normed = transpose_right(values_half, value_w) + synth_grads[5]
    unused, norm_one_back = jax.vjp(layer_norm, flat, widen(gain_one), widen(bias_one))
    flat_part, grad_gain_one, grad_bias_one = norm_one_back(grad_normed)
    grad_rows = (grad_hidden + flat_part).reshape(items, SLOTS, D)
    common_grads = (
        grad_gain_one,
        grad_bias_one,
        grad_value_w,
        grad_value_b,
        grad_out_w,
        grad_out_b,
        grad_gain_two,
        grad_bias_two,
        grad_inner_w,
        grad_inner_b,
        grad_outer_w,
        grad_outer_b,
    )
    return (grad_rows, common_grads, synth_grads[:5])


def per_device(
    boundary,
    lengths,
    ln1_gain,
    ln1_bias,
    value_weight,
    value_bias,
    out_weight,
    out_bias,
    ln2_gain,
    ln2_bias,
    ffn_in,
    ffn_in_bias,
    ffn_out,
    ffn_out_bias,
    dense_first,
    dense_first_bias,
    dense_second,
    dense_second_bias,
    random_table,
):
    micro = boundary.shape[1]
    first_segment = lax.axis_index("segment") == 0
    masters = (
        ln1_gain,
        ln1_bias,
        value_weight,
        value_bias,
        out_weight,
        out_bias,
        ln2_gain,
        ln2_bias,
        ffn_in,
        ffn_in_bias,
        ffn_out,
        ffn_out_bias,
    )
    synth_masters = (dense_first, dense_first_bias, dense_second, dense_second_bias, random_table)
    halves = tuple((to_half(w) for w in masters))
    synth_halves = tuple((to_half(w) for w in synth_masters))
    gathered = (
        lax.all_gather(halves[0], "dp", axis=1, tiled=True),
        lax.all_gather(halves[1], "dp", axis=1, tiled=True),
        lax.all_gather(halves[2], "dp", axis=1, tiled=True),
        lax.all_gather(halves[3], "dp", axis=1, tiled=True),
        lax.all_gather(halves[4], "dp", axis=1, tiled=True),
        lax.all_gather(halves[5], "dp", axis=1, tiled=True),
        lax.all_gather(halves[6], "dp", axis=1, tiled=True),
        lax.all_gather(halves[7], "dp", axis=1, tiled=True),
        lax.all_gather(halves[8], "dp", axis=1, tiled=True),
        lax.all_gather(halves[9], "dp", axis=1, tiled=True),
        lax.all_gather(halves[10], "dp", axis=1, tiled=True),
        lax.all_gather(halves[11], "dp", axis=1, tiled=True),
    )
    common = tuple((piece[0] for piece in gathered))
    synth = (
        lax.all_gather(synth_halves[0], ("segment", "dp"), axis=0, tiled=True),
        lax.all_gather(synth_halves[1], ("segment", "dp"), axis=0, tiled=True),
        lax.all_gather(synth_halves[2], ("segment", "dp"), axis=0, tiled=True),
        lax.all_gather(synth_halves[3], ("segment", "dp"), axis=0, tiled=True),
        lax.all_gather(synth_halves[4], ("segment", "dp"), axis=0, tiled=True),
    )
    received = jnp.zeros(boundary.shape[2:], jnp.bfloat16)
    inputs_kept = []
    outputs_kept = []
    for tick in range(micro + 1):
        own = boundary[0, min(tick, micro - 1)]
        layer_in = jnp.where(first_segment, own, received)
        lens = jnp.where(first_segment, lengths[min(tick, micro - 1)], lengths[max(tick - 1, 0)])
        active = jnp.where(first_segment, tick < micro, tick >= 1)

        def run_forward(operand):
            return forward_layer(widen(operand[0]), operand[1], common, synth, first_segment)[0]

        def skip_forward(operand):
            return jnp.zeros(operand[0].shape, jnp.float32)

        result = to_half(lax.cond(active, run_forward, skip_forward, (layer_in, lens)))
        inputs_kept.append(layer_in)
        outputs_kept.append(result)
        if tick < micro:
            received = passed_along(result, "segment", 1)
    regathered = (
        lax.all_gather(halves[0], "dp", axis=1, tiled=True),
        lax.all_gather(halves[1], "dp", axis=1, tiled=True),
        lax.all_gather(halves[2], "dp", axis=1, tiled=True),
        lax.all_gather(halves[3], "dp", axis=1, tiled=True),
        lax.all_gather(halves[4], "dp", axis=1, tiled=True),
        lax.all_gather(halves[5], "dp", axis=1, tiled=True),
        lax.all_gather(halves[6], "dp", axis=1, tiled=True),
        lax.all_gather(halves[7], "dp", axis=1, tiled=True),
        lax.all_gather(halves[8], "dp", axis=1, tiled=True),
        lax.all_gather(halves[9], "dp", axis=1, tiled=True),
        lax.all_gather(halves[10], "dp", axis=1, tiled=True),
        lax.all_gather(halves[11], "dp", axis=1, tiled=True),
    )
    back_common = tuple((piece[0] for piece in regathered))
    back_synth = (
        lax.all_gather(synth_halves[0], ("segment", "dp"), axis=0, tiled=True),
        lax.all_gather(synth_halves[1], ("segment", "dp"), axis=0, tiled=True),
        lax.all_gather(synth_halves[2], ("segment", "dp"), axis=0, tiled=True),
        lax.all_gather(synth_halves[3], ("segment", "dp"), axis=0, tiled=True),
        lax.all_gather(synth_halves[4], ("segment", "dp"), axis=0, tiled=True),
    )
    common_total = float_zeros(back_common)
    synth_total = float_zeros(back_synth)
    sent_back = jnp.zeros(boundary.shape[2:], jnp.bfloat16)
    grads_kept = []
    for tick in range(micro + 1):
        own = boundary[0, min(tick, micro - 1)]
        cotangent = widen(jnp.where(first_segment, sent_back, own))
        rows = jnp.where(
            first_segment, inputs_kept[max(tick - 1, 0)], inputs_kept[min(tick + 1, micro)]
        )
        lens = jnp.where(first_segment, lengths[max(tick - 1, 0)], lengths[min(tick, micro - 1)])
        active = jnp.where(first_segment, tick >= 1, tick < micro)

        def run_backward(operand):
            return backward_layer(
                widen(operand[0]), operand[1], operand[2], back_common, back_synth, first_segment
            )

        def skip_backward(operand):
            return (
                jnp.zeros(operand[2].shape, jnp.float32),
                float_zeros(back_common),
                float_zeros(back_synth),
            )

        grad_rows, grad_common, grad_synth = lax.cond(
            active, run_backward, skip_backward, (rows, lens, cotangent)
        )
        grad_half = to_half(grad_rows)
        grads_kept.append(grad_half)
        if tick < micro:
            sent_back = passed_along(grad_half, "segment", -1)
        common_total = tuple((total + grad for total, grad in zip(common_total, grad_common)))
        synth_total = tuple((total + grad for total, grad in zip(synth_total, grad_synth)))
    lifted = tuple((piece[None] for piece in common_total))
    common_out = (
        lax.psum_scatter(lifted[0], "dp", scatter_dimension=1, tiled=True),
        lax.psum_scatter(lifted[1], "dp", scatter_dimension=1, tiled=True),
        lax.psum_scatter(lifted[2], "dp", scatter_dimension=1, tiled=True),
        lax.psum_scatter(lifted[3], "dp", scatter_dimension=1, tiled=True),
        lax.psum_scatter(lifted[4], "dp", scatter_dimension=1, tiled=True),
        lax.psum_scatter(lifted[5], "dp", scatter_dimension=1, tiled=True),
        lax.psum_scatter(lifted[6], "dp", scatter_dimension=1, tiled=True),
        lax.psum_scatter(lifted[7], "dp", scatter_dimension=1, tiled=True),
        lax.psum_scatter(lifted[8], "dp", scatter_dimension=1, tiled=True),
        lax.psum_scatter(lifted[9], "dp", scatter_dimension=1, tiled=True),
        lax.psum_scatter(lifted[10], "dp", scatter_dimension=1, tiled=True),
        lax.psum_scatter(lifted[11], "dp", scatter_dimension=1, tiled=True),
    )
    synth_out = (
        lax.psum_scatter(synth_total[0], ("segment", "dp"), scatter_dimension=0, tiled=True),
        lax.psum_scatter(synth_total[1], ("segment", "dp"), scatter_dimension=0, tiled=True),
        lax.psum_scatter(synth_total[2], ("segment", "dp"), scatter_dimension=0, tiled=True),
        lax.psum_scatter(synth_total[3], ("segment", "dp"), scatter_dimension=0, tiled=True),
        lax.psum_scatter(synth_total[4], ("segment", "dp"), scatter_dimension=0, tiled=True),
    )
    layer_outputs = jnp.stack(
        [jnp.where(first_segment, outputs_kept[m], outputs_kept[m + 1]) for m in range(micro)]
    )[None]
    input_grads = jnp.stack(
        [jnp.where(first_segment, grads_kept[m + 1], grads_kept[m]) for m in range(micro)]
    )[None]
    return (
        layer_outputs,
        input_grads,
        common_out[0],
        common_out[1],
        common_out[2],
        common_out[3],
        common_out[4],
        common_out[5],
        common_out[6],
        common_out[7],
        common_out[8],
        common_out[9],
        common_out[10],
        common_out[11],
        synth_out[0],
        synth_out[1],
        synth_out[2],
        synth_out[3],
        synth_out[4],
    )


def solution(mesh):
    return jax.shard_map(
        per_device,
        mesh=mesh,
        in_specs=(
            P("segment", None, "dp", None, None),
            P(None, "dp"),
            P("segment", "dp"),
            P("segment", "dp"),
            P("segment", "dp", None),
            P("segment", "dp"),
            P("segment", "dp", None),
            P("segment", "dp"),
            P("segment", "dp"),
            P("segment", "dp"),
            P("segment", "dp", None),
            P("segment", "dp"),
            P("segment", "dp", None),
            P("segment", "dp"),
            P(("segment", "dp"), None),
            P(("segment", "dp")),
            P(("segment", "dp"), None),
            P(("segment", "dp")),
            P(("segment", "dp"), None),
        ),
        out_specs=(
            P("segment", None, "dp", None, None),
            P("segment", None, "dp", None, None),
            P("segment", "dp"),
            P("segment", "dp"),
            P("segment", "dp", None),
            P("segment", "dp"),
            P("segment", "dp", None),
            P("segment", "dp"),
            P("segment", "dp"),
            P("segment", "dp"),
            P("segment", "dp", None),
            P("segment", "dp"),
            P("segment", "dp", None),
            P("segment", "dp"),
            P(("segment", "dp"), None),
            P(("segment", "dp")),
            P(("segment", "dp"), None),
            P(("segment", "dp")),
            P(("segment", "dp"), None),
        ),
        check_vma=False,
    )
```

profile of v0, /device:TPU:0, one launch (start us, length us, event | category | flops | bytes accessed | tf_op | source)
XLA Modules:
  0.0 2359.6 jit_solution(8320902983907864866)
XLA Ops:
  21.1 42.3 %all-reduce.13 = (bf16[768]{0:T(1024)(128)(2,1)S(1)}, bf16[6144]{0:T(1024)(128)(2,1)S(1)}) all-reduce(bf16[768]{0:T(1024)(128)(2,1)S(1)} %dynamic-update-slice.3, bf16[6144]{0:T(1024)(128)(2,1)S(1)} %dynamic-update-slice.4), channel_id=1, replica_groups=mesh['segment'=2,'dp'=16] {'segment','dp'}, use_global_device_ids=true, to_apply=%add.3 | all-reduce | flops 6912 | bytes 27648
  63.4 59.3 %all-reduce.14 = (bf16[768]{0:T(1024)(128)(2,1)S(1)}, bf16[768]{0:T(1024)(128)(2,1)S(1)}, bf16[768]{0:T(1024)(128)(2,1)}, bf16[768]{0:T(1024)(128)(2,1)S(1)}, bf...) all-reduce(bf16[768]{0:T(1024)(128)(2,1)S(1)} %dynamic-update-slice, ...), channel_id=1, replica_groups=mesh['segment'=2,'dp'=16] {'dp'}, use_global_device_ids=true, to_apply=%add | all-reduce | flops 8448 | bytes 33792 | tf_op jit(solution)/shard_map/squeeze | solution.py:301
  124.3 24.6 %all-gather.12.cloned.1.call-done = bf16[768,768]{1,0:T(8,128)(2,1)} async-done(((bf16[24,768]{1,0:T(8,128)(2,1)}), bf16[768,768]{1,0:T(8,128)(2,1)}) %all-gather.12.cloned.1.call-update) | async-done | bytes 1179664 | tf_op jit(solution)/shard_map/all_gather | solution.py:303
  148.9 55.0 %all-gather.18.cloned.1.call-done = bf16[1,768,3072]{2,1,0:T(8,128)(2,1)} async-done(((bf16[1,48,3072]{2,1,0:T(8,128)(2,1)}), bf16[1,768,3072]{2,1,0:T(8,128)(2,1)}) %all-gather.18.cloned.1.call-update) | async-done | bytes 4718608 | tf_op jit(solution)/shard_map/all_gather | solution.py:296
  203.9 54.7 %all-gather.20.cloned.1.call-done = bf16[1,3072,768]{2,1,0:T(8,128)(2,1)} async-done(((bf16[1,192,768]{2,1,0:T(8,128)(2,1)}), bf16[1,3072,768]{2,1,0:T(8,128)(2,1)}) %all-gather.20.cloned.1.call-update) | async-done | bytes 4718608 | tf_op jit(solution)/shard_map/all_gather | solution.py:298
  258.6 71.5 %all-gather.10.cloned.1.call-done = bf16[6144,512]{1,0:T(8,128)(2,1)} async-done(((bf16[192,512]{1,0:T(8,128)(2,1)}), bf16[6144,512]{1,0:T(8,128)(2,1)}) %all-gather.10.cloned.1.call-update) | async-done | bytes 6291472 | tf_op jit(solution)/shard_map/all_gather | solution.py:307
  330.1 84.0 %all-gather.14.cloned.1.call-done = bf16[768,6144]{1,0:T(8,128)(2,1)} async-done(((bf16[24,6144]{1,0:T(8,128)(2,1)}), bf16[768,6144]{1,0:T(8,128)(2,1)}) %all-gather.14.cloned.1.call-update) | async-done | bytes 9437200 | tf_op jit(solution)/shard_map/all_gather | solution.py:305
  414.1 56.8 %conditional.13 = (bf16[1,512,768]{2,1,0:T(8,128)(2,1)S(1)}) conditional(s32[]{:T(128)} %convert_element_type.780, () %tuple.113, (bf16[1,512,768]{2,1,0:T(8,128)(2,1)S(1)}, bf16[768]{0:T(1024)(128)(2,1)S(1)}, bf16[768]{0:T(1024)(128)(2,1)S(1)}, bf16[768,768]{1,0:T(8,128)(2,1)}, bf16[768]{0:T(1024)(128)(2,1)}, /*index=5*/s32[1]{0:T(128)}, ...), branch_computations={%region_0.1_spmd, %region_1.10_spmd} | conditional | flops 11956917248 | bytes 173783360 | solution.py:324
  419.1 25.1 %conditional = (f32[1,12,512,512]{2,3,1,0:T(8,128)}) conditional(s32[]{:T(128)} %convert_element_type.569, bf16[6144,512]{1,0:T(8,128)(2,1)} %get-tuple-element.392, (bf16[512,768]{1,0:T(8,128)(2,1)S(1)}, bf16[768,768]{1,0:T(8,128)(2,1)}, bf16[768]{0:T(1024)(128)(2,1)S(1)}, bf16[768,6144]{1,0:T(8,128)(2,1)}, bf16[6144]{0:T(1024)(128)(2,1)S(1)}) %tuple.84), branch_computations={%region_4.4_spmd, %region_5.5_spmd} | conditional | flops 5442903040 | bytes 49221128 | solution.py:107
  419.1 12.3 convolution_add_fusion
  431.4 12.6 copy.120
  496.0 26.5 %conditional.14 = (f32[1,12,512,512]{2,3,1,0:T(8,128)}) conditional(s32[]{:T(128)} %convert_element_type.780, bf16[6144,512]{1,0:T(8,128)(2,1)} %all-gather.10.cloned.1.call-done, (bf16[512,768]{1,0:T(8,128)(2,1)}, bf16[768,768]{1,0:T(8,128)(2,1)}, bf16[768]{0:T(1024)(128)(2,1)S(1)}, bf16[768,6144]{1,0:T(8,128)(2,1)}, ...), branch_computations={%region_12.13_spmd, %region_13.14_spmd} | conditional | flops 5442903040 | bytes 49221128 | solution.py:107
  497.3 12.5 convolution_add_fusion.1
  509.8 12.6 copy.124
  539.3 11.0 fusion.386
  554.8 40.9 %conditional.16 = (f32[768]{0:T(1024)}, f32[768]{0:T(1024)}, f32[768,768]{1,0:T(8,128)}, f32[768]{0:T(1024)}, f32[768,768]{1,0:T(8,128)}, /*index=5*/f32[768]{0:...) conditional(s32[]{:T(128)} %convert_element_type.820, ...), branch_computations={%region_28.29_spmd, %region_29.55_spmd} | conditional | flops 34057216000 | bytes 637375040 | solution.py:376
  600.6 24.8 %conditional.17 = (f32[1,12,512,512]{2,3,1,0:T(8,128)}) conditional(s32[]{:T(128)} %convert_element_type.780, bf16[6144,512]{1,0:T(8,128)(2,1)} %all-gather.10.cloned.1.call-done, (bf16[512,768]{1,0:T(8,128)(2,1)S(1)}, bf16[768,768]{1,0:T(8,128)(2,1)}, bf16[768]{0:T(1024)(128)(2,1)S(1)}, bf16[768,6144]{1,0:T(8,128)(2,1)}, ...), branch_computations={%region_57.58_spmd, %region_58.59_spmd} | conditional | flops 5442903040 | bytes 49221128 | solution.py:107
  600.6 12.2 convolution_add_fusion.6
  612.8 12.6 copy.138
  648.3 64.0 %collective-permute-done.2 = bf16[1,512,768]{2,1,0:T(8,128)(2,1)} collective-permute-done((bf16[1,512,768]{2,1,0:T(8,128)(2,1)}, bf16[1,512,768]{2,1,0:T(8,128)(2,1)}, u32[]{:S(2)}, u32[]{:S(2)}) %collective-permute-start.2) | collective-permute-done | bytes 786464 | tf_op jit(solution)/shard_map/ppermute | solution.py:19
  755.2 11.7 bitcast_multiply_fusion.4
  766.8 43.0 %conditional.18 = (f32[768]{0:T(1024)S(1)}, f32[768,6144]{1,0:T(8,128)}, f32[6144]{0:T(1024)S(1)}, f32[6144,512]{1,0:T(8,128)}, f32[512,768]{1,0:T(8,128)}, /*index=5*/f32[768,768]{1,0:T(8,128)}) conditional(s32[]{:T(128)} %convert_element_type.780, (f32[1,12,512,512]{2,3,1,0:T(8,128)}) %tuple.143, (bf16[512,768]{1,0:T(8,128)(2,1)S(1)}, ...), branch_computations={%region_66.67_spmd, %region_67.70_spmd} | conditional | flops 11499202560 | bytes 132991688 | solution.py:223
  776.8 11.5 convert_reduce_fusion.10
  818.9 19.1 collective-permute-done.3
  839.3 203.2 %conditional.19 = (f32[768]{0:T(1024)}, f32[768]{0:T(1024)}, f32[768,768]{1,0:T(8,128)}, f32[768]{0:T(1024)}, f32[768,768]{1,0:T(8,128)}, /*index=5*/f32[768]{0:...) conditional(s32[]{:T(128)} %convert_element_type.780, ...), branch_computations={%region_72.73_spmd, %region_73.99_spmd} | conditional | flops 34056429568 | bytes 611297856 | solution.py:376
  845.5 26.7 %conditional.4 = (f32[1,12,512,512]{2,3,1,0:T(8,128)}) conditional(s32[]{:T(128)} %convert_element_type.684, bf16[6144,512]{1,0:T(8,128)(2,1)} %get-tuple-element.501, (bf16[512,768]{1,0:T(8,128)(2,1)}, bf16[768,768]{1,0:T(8,128)(2,1)}, bf16[768]{0:T(1024)(128)(2,1)S(1)}, bf16[768,6144]{1,0:T(8,128)(2,1)}, bf16[6144]{0:T(1024)(128)(2,1)S(1)}) %tuple.97), branch_computations={%region_76.76_spmd, %region_77.77_spmd} | conditional | flops 5442903040 | bytes 49221128 | solution.py:107
  846.8 12.5 convolution_add_fusion.8
  859.2 12.6 copy.141
  904.6 11.7 convert_reduce_fusion.13
  926.7 12.0 fusion.245
  938.8 12.3 bitcast_multiply_fusion.2
  951.1 46.7 %conditional.5 = (f32[768,768]{0,1:T(8,128)}, f32[768]{0:T(1024)}, f32[768,6144]{1,0:T(8,128)}, f32[6144]{0:T(1024)}, f32[6144,512]{1,0:T(8,128)}, /*index=5*/f32[512,768]{1,0:T(8,128)}) conditional(s32[]{:T(128)} %convert_element_type.684, (f32[1,12,512,512]{2,3,1,0:T(8,128)}) %tuple.138, (bf16[512,768]{1,0:T(8,128)(2,1)}, ...), branch_computations={%region_85.85_spmd, %region_86.88_spmd} | conditional | flops 11499202560 | bytes 125127336 | solution.py:223
  963.1 12.0 convert_reduce_fusion.12
  1110.6 18.7 add_add_fusion.5
  1129.4 25.5 %add_add_fusion.4 = f32[768,6144]{1,0:T(8,128)} fusion(f32[768,6144]{1,0:T(8,128)} %get-tuple-element.615, f32[768,6144]{1,0:T(8,128)} %get-tuple-element.613, f32[768,6144]{1,0:T(8,128)} %get-tuple-element.614), kind=kLoop, calls=%fused_computation.426 | loop fusion | flops 9437184 | bytes 75497472 | tf_op jit(solution)/shard_map/add | solution.py:384
  1160.2 39.4 %all-reduce.12 = (f32[768]{0:T(1024)S(1)}, f32[6144]{0:T(1024)S(1)}) all-reduce(f32[768]{0:T(1024)S(1)} %add_add_fusion.11, f32[6144]{0:T(1024)S(1)} %add_add_fusion.9), channel_id=15, replica_groups=mesh['segment'=2,'dp'=16] {'segment','dp'}, use_global_device_ids=true, to_apply=%region_120.121.clone | all-reduce | flops 6912 | bytes 55296
  1216.3 57.2 %reduce-scatter.52.cloned.1.call-done = f32[48,1]{1,0:T(8,128)} async-done(((f32[768,1]{1,0:T(8,128)}), f32[48,1]{1,0:T(8,128)}) %reduce-scatter.52.cloned.1.call-update) | async-done | bytes 208
  1274.9 56.7 %reduce-scatter.54.cloned.1.call-done = f32[48,1]{1,0:T(8,128)} async-done(((f32[768,1]{1,0:T(8,128)}), f32[48,1]{1,0:T(8,128)}) %reduce-scatter.54.cloned.1.call-update) | async-done | bytes 208
  1332.9 57.2 %reduce-scatter.56.cloned.1.call-done = f32[48,1]{1,0:T(8,128)} async-done(((f32[768,1]{1,0:T(8,128)}), f32[48,1]{1,0:T(8,128)}) %reduce-scatter.56.cloned.1.call-update) | async-done | bytes 208
  1391.4 56.7 %reduce-scatter.60.cloned.1.call-done = f32[48,1]{1,0:T(8,128)} async-done(((f32[768,1]{1,0:T(8,128)}), f32[48,1]{1,0:T(8,128)}) %reduce-scatter.60.cloned.1.call-update) | async-done | bytes 208
  1449.4 61.1 %reduce-scatter.58.cloned.1.call-done = f32[192,1]{1,0:T(8,128)} async-done(((f32[3072,1]{1,0:T(8,128)}), f32[192,1]{1,0:T(8,128)}) %reduce-scatter.58.cloned.1.call-update) | async-done | bytes 784
  1512.0 102.2 %reduce-scatter.40.cloned.1.call-done = f32[24,768]{1,0:T(8,128)} async-done(((f32[768,768]{1,0:T(8,128)}), f32[24,768]{1,0:T(8,128)}) %reduce-scatter.40.cloned.1.call-update) | async-done | bytes 73744 | tf_op jit(solution)/shard_map/reduce_scatter | solution.py:401
  1614.3 66.7 %reduce-scatter.32.cloned.1.call-done = f32[1,48,768]{2,1,0:T(8,128)} async-done(((f32[1,768,768]{2,1,0:T(8,128)}), f32[1,48,768]{2,1,0:T(8,128)}) %reduce-scatter.32.cloned.1.call-update) | async-done | bytes 147472 | tf_op jit(solution)/shard_map/reduce_scatter | solution.py:389
  1681.0 66.2 %reduce-scatter.34.cloned.1.call-done = f32[1,48,768]{2,1,0:T(8,128)} async-done(((f32[1,768,768]{2,1,0:T(8,128)}), f32[1,48,768]{2,1,0:T(8,128)}) %reduce-scatter.34.cloned.1.call-update) | async-done | bytes 147472 | tf_op jit(solution)/shard_map/reduce_scatter | solution.py:391
  1747.2 115.7 %reduce-scatter.36.cloned.1.call-done = f32[1,48,3072]{2,1,0:T(8,128)} async-done(((f32[1,768,3072]{2,1,0:T(8,128)}), f32[1,48,3072]{2,1,0:T(8,128)}) %reduce-scatter.36.cloned.1.call-update) | async-done | bytes 589840 | tf_op jit(solution)/shard_map/reduce_scatter | solution.py:395
  1862.8 115.6 %reduce-scatter.38.cloned.1.call-done = f32[1,192,768]{2,1,0:T(8,128)} async-done(((f32[1,3072,768]{2,1,0:T(8,128)}), f32[1,192,768]{2,1,0:T(8,128)}) %reduce-scatter.38.cloned.1.call-update) | async-done | bytes 589840 | tf_op jit(solution)/shard_map/reduce_scatter | solution.py:397
  1978.4 162.8 %reduce-scatter.44.cloned.1.call-done = f32[192,512]{1,0:T(8,128)} async-done(((f32[6144,512]{1,0:T(8,128)}), f32[192,512]{1,0:T(8,128)}) %reduce-scatter.44.cloned.1.call-update) | async-done | bytes 393232 | tf_op jit(solution)/shard_map/reduce_scatter | solution.py:405
  2141.2 211.2 %reduce-scatter.42.cloned.1.call-done = f32[24,6144]{1,0:T(8,128)} async-done(((f32[768,6144]{1,0:T(8,128)}), f32[24,6144]{1,0:T(8,128)}) %reduce-scatter.42.cloned.1.call-update) | async-done | bytes 589840 | tf_op jit(solution)/shard_map/reduce_scatter | solution.py:403
  (671 shorter events, 462.4 us)
Async XLA Ops:
  7.2 117.1 %all-gather.8.cloned.1.call-start = ((), (), s32[]{:S(2)}) async-start(), calls=%async_computation.15 | async-start | bytes 1253376 | tf_op jit(solution)/shard_map/all_gather | solution.py:290
  8.9 115.4 %all-gather.16.cloned.1.call-start = ((), (), s32[]{:S(2)}) async-start(), calls=%async_computation.19 | async-start | bytes 1253376 | tf_op jit(solution)/shard_map/all_gather | solution.py:292
  10.5 138.4 %all-gather.12.cloned.1.call-start = ((), (), s32[]{:S(2)}) async-start(), calls=%async_computation.17 | async-start | bytes 1216512 | tf_op jit(solution)/shard_map/all_gather | solution.py:303
  12.1 191.8 %all-gather.18.cloned.1.call-start = ((), (), s32[]{:S(2)}) async-start(), calls=%async_computation.20 | async-start | bytes 5013504 | tf_op jit(solution)/shard_map/all_gather | solution.py:296
  14.2 108.5 %copy-start.212 = (s32[2,1]{0,1:T(1,128)S(1)}, s32[2,1]{0,1:T(1,128)}, u32[]{:S(2)}) copy-start(s32[2,1]{0,1:T(1,128)} %param.46) | copy-start | bytes 28
  14.2 109.1 %copy-start.16 = (bf16[1,2,1,512,768]{4,3,2,1,0:T(8,128)(2,1)S(1)}, bf16[1,2,1,512,768]{4,3,2,1,0:T(8,128)(2,1)}, u32[]{:S(2)}) copy-start(bf16[1,2,1,512,768]{4,3,2,1,0:T(8,128)(2,1)} %param.45) | copy-start | bytes 4718596
  14.2 244.4 %all-gather.20.cloned.1.call-start = ((), (), s32[]{:S(2)}) async-start(), calls=%async_computation.21 | async-start | bytes 5013504 | tf_op jit(solution)/shard_map/all_gather | solution.py:298
  15.1 315.0 %all-gather.10.cloned.1.call-start = ((), (), s32[]{:S(2)}) async-start(), calls=%async_computation.16 | async-start | bytes 6488064 | tf_op jit(solution)/shard_map/all_gather | solution.py:307
  15.8 398.3 %all-gather.14.cloned.1.call-start = ((), (), s32[]{:S(2)}) async-start(), calls=%async_computation.18 | async-start | bytes 9732096 | tf_op jit(solution)/shard_map/all_gather | solution.py:305
  16.7 1187.3 %reduce-scatter.46.cloned.1.call-start = ((), (), s32[]{:S(2)}) async-start(), calls=%async_computation.29 | async-start | bytes 417792
  63.4 537.0 %copy-start.70 = (bf16[6144]{0:T(1024)(128)(2,1)}, bf16[6144]{0:T(1024)(128)(2,1)S(1)}, u32[]{:S(2)}) copy-start(bf16[6144]{0:T(1024)(128)(2,1)S(1)} %get-tuple-element.836) | copy-start | bytes 36868
  122.7 291.4 %copy-start.106 = (bf16[768]{0:T(1024)(128)(2,1)}, bf16[768]{0:T(1024)(128)(2,1)S(1)}, u32[]{:S(2)}) copy-start(bf16[768]{0:T(1024)(128)(2,1)S(1)} %get-tuple-element.837) | copy-start | bytes 4612
  122.7 291.4 %copy-start.110 = (bf16[768]{0:T(1024)(128)(2,1)}, bf16[768]{0:T(1024)(128)(2,1)S(1)}, u32[]{:S(2)}) copy-start(bf16[768]{0:T(1024)(128)(2,1)S(1)} %get-tuple-element.838) | copy-start | bytes 4612
  122.7 291.4 %copy-start.116 = (bf16[768]{0:T(1024)(128)(2,1)}, bf16[768]{0:T(1024)(128)(2,1)S(1)}, u32[]{:S(2)}) copy-start(bf16[768]{0:T(1024)(128)(2,1)S(1)} %get-tuple-element.840) | copy-start | bytes 4612
  470.9 18.8 collective-permute-start
  491.2 63.6 %copy-start.8 = (bf16[1,512,768]{2,1,0:T(8,128)(2,1)}, bf16[1,512,768]{2,1,0:T(8,128)(2,1)S(1)}, u32[]{:S(2)}) copy-start(bf16[1,512,768]{2,1,0:T(8,128)(2,1)S(1)} %get-tuple-element.883) | copy-start | bytes 2359300
  550.3 46.7 %collective-permute-start.1 = (bf16[1,512,768]{2,1,0:T(8,128)(2,1)}, bf16[1,512,768]{2,1,0:T(8,128)(2,1)}, u32[]{:S(2)}, u32[]{:S(2)}) collective-permute-start(bf16[1,512,768]{2,1,0:T(8,128)(2,1)} %fusion.386), channel_id=1, source_target_pairs={{0,16},{1,17},{2,18},{3,19},{4,20},{5,21},{6,22},{7,23},{8,24},{9,... | collective-permute-start | bytes 2359304 | tf_op jit(solution)/shard_map/ppermute | solution.py:19
  595.7 116.6 %collective-permute-start.2 = (bf16[1,512,768]{2,1,0:T(8,128)(2,1)}, bf16[1,512,768]{2,1,0:T(8,128)(2,1)}, u32[]{:S(2)}, u32[]{:S(2)}) collective-permute-start(bf16[1,512,768]{2,1,0:T(8,128)(2,1)} %get-tuple-element.580), channel_id=1, source_target_pairs={{16,0},{17,1},{18,2},{19,3},{20,4},{21,5},{22,6},{23,7},{24,8},{25... | collective-permute-start | bytes 2359304 | tf_op jit(solution)/shard_map/ppermute | solution.py:19
  599.6 215.3 %copy-start.6 = (bf16[1,512,768]{2,1,0:T(8,128)(2,1)}, bf16[1,512,768]{2,1,0:T(8,128)(2,1)S(1)}, u32[]{:S(2)}) copy-start(bf16[1,512,768]{2,1,0:T(8,128)(2,1)S(1)} %get-tuple-element.880) | copy-start | bytes 2359300
  599.7 37.5 %copy-start.98 = (f32[512]{0:T(512)}, f32[512]{0:T(512)S(1)}, u32[]{:S(2)}) copy-start(f32[512]{0:T(512)S(1)} %broadcast_multiply_fusion.9) | copy-start | bytes 6148
  600.1 37.1 %copy-start.131 = (f32[512]{0:T(512)}, f32[512]{0:T(512)S(1)}, u32[]{:S(2)}) copy-start(f32[512]{0:T(512)S(1)} %fusion.410) | copy-start | bytes 6148
  647.9 83.4 %copy-start.30 = (f32[512,768]{1,0:T(8,128)}, f32[512,768]{1,0:T(8,128)S(1)}, u32[]{:S(2)}) copy-start(f32[512,768]{1,0:T(8,128)S(1)} %get-tuple-element.921) | copy-start | bytes 4718596
  647.9 64.4 %copy-start.17 = (bf16[1,2,1,512,768]{4,3,2,1,0:T(8,128)(2,1)S(1)}, bf16[1,2,1,512,768]{4,3,2,1,0:T(8,128)(2,1)}, u32[]{:S(2)}) copy-start(bf16[1,2,1,512,768]{4,3,2,1,0:T(8,128)(2,1)} %param.45) | copy-start | bytes 4718596
  647.9 83.4 %copy-start.144 = (f32[512]{0:T(512)}, f32[512]{0:T(512)S(1)}, u32[]{:S(2)}) copy-start(f32[512]{0:T(512)S(1)} %broadcast_multiply_fusion.8) | copy-start | bytes 6148
  648.2 66.1 %copy-start.172 = (f32[768]{0:T(1024)S(1)}, f32[768]{0:T(1024)}, u32[]{:S(2)}) copy-start(f32[768]{0:T(1024)} %convert_element_type.812) | copy-start | bytes 9220
  648.2 66.1 %copy-start.195 = (f32[768]{0:T(1024)S(1)}, f32[768]{0:T(1024)}, u32[]{:S(2)}) copy-start(f32[768]{0:T(1024)} %convert_element_type.813) | copy-start | bytes 9220
  648.3 83.0 %copy-start.186 = (f32[512]{0:T(512)}, f32[512]{0:T(512)S(1)}, u32[]{:S(2)}) copy-start(f32[512]{0:T(512)S(1)} %fusion.411) | copy-start | bytes 6148
  766.8 43.0 %copy-start.85 = (f32[768]{0:T(1024)S(1)}, f32[768]{0:T(1024)}, u32[]{:S(2)}) copy-start(f32[768]{0:T(1024)} %copy-done.83) | copy-start | bytes 9220
  766.8 43.1 %copy-start.99 = (f32[512]{0:T(512)S(1)}, f32[512]{0:T(512)}, u32[]{:S(2)}) copy-start(f32[512]{0:T(512)} %copy-done.98) | copy-start | bytes 6148
  816.9 21.1 collective-permute-start.3
  898.9 21.0 copy-start.34
  898.9 20.9 copy-start.148
  1044.2 161.0 %reduce-scatter.48.cloned.1.call-start = ((), (), s32[]{:S(2)}) async-start(), calls=%async_computation.30 | async-start | bytes 417792
  1045.9 169.1 %reduce-scatter.50.cloned.1.call-start = ((), (), s32[]{:S(2)}) async-start(), calls=%async_computation.31 | async-start | bytes 417792
  1047.6 225.9 %reduce-scatter.52.cloned.1.call-start = ((), (), s32[]{:S(2)}) async-start(), calls=%async_computation.32 | async-start | bytes 417792
  1049.3 282.2 %reduce-scatter.54.cloned.1.call-start = ((), (), s32[]{:S(2)}) async-start(), calls=%async_computation.33 | async-start | bytes 417792
  1051.0 339.0 %reduce-scatter.56.cloned.1.call-start = ((), (), s32[]{:S(2)}) async-start(), calls=%async_computation.34 | async-start | bytes 417792
  1052.7 395.4 %reduce-scatter.60.cloned.1.call-start = ((), (), s32[]{:S(2)}) async-start(), calls=%async_computation.36 | async-start | bytes 417792
  1054.4 456.1 %reduce-scatter.58.cloned.1.call-start = ((), (), s32[]{:S(2)}) async-start(), calls=%async_computation.35 | async-start | bytes 1671168
  1056.9 557.3 %reduce-scatter.40.cloned.1.call-start = ((), (), s32[]{:S(2)}) async-start(), calls=%async_computation.26 | async-start | bytes 2433024 | tf_op jit(solution)/shard_map/reduce_scatter | solution.py:401
  1062.1 618.9 %reduce-scatter.32.cloned.1.call-start = ((), (), s32[]{:S(2)}) async-start(), calls=%async_computation.22 | async-start | bytes 2506752 | tf_op jit(solution)/shard_map/reduce_scatter | solution.py:389
  1068.8 678.4 %reduce-scatter.34.cloned.1.call-start = ((), (), s32[]{:S(2)}) async-start(), calls=%async_computation.23 | async-start | bytes 2506752 | tf_op jit(solution)/shard_map/reduce_scatter | solution.py:391
  1075.2 787.6 %reduce-scatter.36.cloned.1.call-start = ((), (), s32[]{:S(2)}) async-start(), calls=%async_computation.24 | async-start | bytes 10027008 | tf_op jit(solution)/shard_map/reduce_scatter | solution.py:395
  1092.3 886.1 %reduce-scatter.38.cloned.1.call-start = ((), (), s32[]{:S(2)}) async-start(), calls=%async_computation.25 | async-start | bytes 10027008 | tf_op jit(solution)/shard_map/reduce_scatter | solution.py:397
  1110.4 1030.9 %reduce-scatter.44.cloned.1.call-start = ((), (), s32[]{:S(2)}) async-start(), calls=%async_computation.28 | async-start | bytes 12976128 | tf_op jit(solution)/shard_map/reduce_scatter | solution.py:405
  1129.4 1223.0 %reduce-scatter.42.cloned.1.call-start = ((), (), s32[]{:S(2)}) async-start(), calls=%async_computation.27 | async-start | bytes 19464192 | tf_op jit(solution)/shard_map/reduce_scatter | solution.py:403
  1157.0 43.7 %copy-start.42 = (bf16[1,512,768]{2,1,0:T(8,128)(2,1)S(1)}, bf16[1,512,768]{2,1,0:T(8,128)(2,1)}, u32[]{:S(2)}) copy-start(bf16[1,512,768]{2,1,0:T(8,128)(2,1)} %copy-done.41) | copy-start | bytes 2359300
  1158.6 43.4 %copy-start.40 = (bf16[1,1,512,768]{3,2,1,0:T(8,128)(2,1)S(1)}, bf16[1,1,512,768]{3,2,1,0:T(8,128)(2,1)}, u32[]{:S(2)}) copy-start(bf16[1,1,512,768]{3,2,1,0:T(8,128)(2,1)} %get-tuple-element.875) | copy-start | bytes 2359300
  (161 other events, 977.6 us)
Sparse Core Ops, SparseCore 0:
  10.9 41.1 all-gather.7
  54.9 37.2 all-gather.15
  95.7 53.1 all-gather.11
  151.6 52.2 all-gather.17
  206.6 51.9 all-gather.19
  261.9 68.1 all-gather.9
  333.6 80.5 all-gather.13
  1044.3 54.1 reduce-scatter.45
  1102.4 54.5 reduce-scatter.47
  1160.4 54.5 reduce-scatter.49
  1218.9 54.5 reduce-scatter.51
  1276.9 54.6 reduce-scatter.53
  1335.5 54.5 reduce-scatter.55
  1393.4 54.6 reduce-scatter.59
  1452.1 58.4 reduce-scatter.57
  1516.2 98.0 reduce-scatter.39
  1618.9 61.9 reduce-scatter.31
  1685.2 61.9 reduce-scatter.33
  1752.4 110.3 reduce-scatter.35
  1867.3 111.0 reduce-scatter.37
  1986.1 155.1 reduce-scatter.43
  2148.2 204.1 reduce-scatter.41
where the time goes:
time: 2370 us; the launch traced here: 2360 us
  waiting for transfers between devices  1520 us (64%)
  matrix products  283 us (12%)
  other arithmetic  222 us (9%)
  local copies, waits for them, and re-layouts  160 us (7%)
  blocking collectives  141 us (6%)
    unnamed x30, waiting for transfers between devices  298 us
    reduce_scatter x1, waiting for transfers between devices, per_device(): lax.psum_scatter(synth_total[2], ('segment', 'dp'), scatter_dimension=0,...  211 us
    reduce_scatter x1, waiting for transfers between devices, per_device(): lax.psum_scatter(synth_total[4], ('segment', 'dp'), scatter_dimension=0,...  163 us
    reduce_scatter x1, waiting for transfers between devices, per_device(): lax.psum_scatter(lifted[8], 'dp', scatter_dimension=1, tiled=True)  116 us
    reduce_scatter x1, waiting for transfers between devices, per_device(): lax.psum_scatter(lifted[10], 'dp', scatter_dimension=1, tiled=True)  116 us
    reduce_scatter x1, waiting for transfers between devices, per_device(): lax.psum_scatter(synth_total[0], ('segment', 'dp'), scatter_dimension=0,...  102 us
    dot_general x18, matrix products, product(): return jnp.dot(left, right, preferred_element_type=jnp.float32)  95.6 us
    ppermute x4, waiting for transfers between devices, passed_along(): return lax.ppermute(x, axis, pairs)  90.9 us
  transfers between devices with their start and end apart: 26, of which 21 were waited for; matrix products, arithmetic and copies ran while one was open for 10% of the time, Pallas kernels for 0%

commit v1 on v0

v1 whole, which is shorter than its diff:
```python
import functools
import math
from typing import Any, NamedTuple

import jax
import jax.numpy as jnp
from jax import lax
from jax.experimental import pallas as pl
from jax.experimental.pallas import tpu as pltpu
from jax.sharding import PartitionSpec as P

MESH = pl.DeviceIdType.MESH
HEADS = 12
EPSILON = 1e-05
GELU_SCALE = 0.7978845608028654
AXES = ("segment", "dp")


def half(value):
    return value.astype(jnp.bfloat16)


def wide(value):
    return value.astype(jnp.float32)


def mm(left, right):
    return jnp.dot(left, right, preferred_element_type=jnp.float32)


def mm_tn(left, right):
    return lax.dot_general(left, right, (((0,), (0,)), ((), ())), preferred_element_type=jnp.float32)


def mm_nt(left, right):
    return lax.dot_general(left, right, (((1,), (1,)), ((), ())), preferred_element_type=jnp.float32)


class Place:
    def __init__(self, nz):
        self.nz = nz
        self.x = lax.axis_index("segment")
        d = lax.axis_index("dp")
        self.c = d % 2
        self.y = (d // 2) % 2
        self.z = d // 4
        par = self.z % 2
        self.q = par * ((self.z + 1) // 2) + (1 - par) * ((nz - self.z // 2) % nz)

    def z_at(self, q):
        nz = self.nz
        upper = ((q + nz - 1) % nz) // (nz // 2)
        return (1 - upper) * (2 * q - 1) + upper * ((2 * (nz - q)) % (2 * nz))

    def ring_z(self, back):
        return self.z_at((self.q + 2 * self.nz - back) % self.nz)

    def device(self, x=None, z=None, y=None, c=None):
        x = self.x if x is None else x
        z = self.z if z is None else z
        y = self.y if y is None else y
        c = self.c if c is None else c
        return (x, (z * 2 + y) * 2 + c)

    def other(self, axis):
        return self.device(**{axis: 1 - getattr(self, axis)})

    def succ(self):
        return self.device(z=self.z_at((self.q + 1) % self.nz))

    def pred(self):
        return self.device(z=self.ring_z(1))


def greet(place):
    barrier = pltpu.get_barrier_semaphore()
    peers = [place.other("x"), place.other("y"), place.other("c"), place.succ(), place.pred()]
    for peer in peers:
        pl.semaphore_signal(barrier, inc=1, device_id=peer, device_id_type=MESH)
    pl.semaphore_wait(barrier, len(peers))


def block_of(ref, place, c, z, x=None, y=None):
    xs = pl.ds(0, 2) if x is None else x
    ys = pl.ds(0, 2) if y is None else y
    return ref.at[xs, z, ys, c]


def gather_kernel(orders, nz, *refs):
    n = len(orders)
    ins, outs = refs[:n], refs[n : 2 * n]
    send, recv, local = refs[2 * n :]
    place = Place(nz)
    greet(place)
    started = []

    def put(i, k, src, dst, device):
        copy = pltpu.make_async_remote_copy(
            src_ref=src,
            dst_ref=dst,
            send_sem=send.at[i, k],
            recv_sem=recv.at[i, k],
            device_id=device,
            device_id_type=MESH,
        )
        copy.start()
        started.append(copy)
        return copy

    copies = [dict() for _ in orders]

    def stage(i, t):
        first, second, third = orders[i]
        out, mine = outs[i], copies[i]

        def shard(z, **at):
            return block_of(out, place, place.c, z, **at)

        def own(axis, z):
            return shard(z, **{axis: getattr(place, axis)})

        one = shard(place.z, x=place.x, y=place.y)
        if t == 0:
            mine["own"] = pltpu.make_async_copy(ins[i], one, local.at[i])
            mine["own"].start()
        if second == "z":
            if t == 0:
                mine["p"] = put(i, 0, ins[i], one, place.other(first))
                return
            if t == 1:
                mine["own"].wait()
                mine["p"].wait_recv()
            elif t <= nz:
                mine["z", t - 1].wait_recv()
            if t <= nz:
                z = place.ring_z(t - 1)
                block = own(third, z)
                if t < nz:
                    mine["z", t] = put(i, t, block, block, place.succ())
                mine["l", t] = put(i, nz + t, block, block, place.other(third))
                mine["c", t] = put(i, 2 * nz + t, block, block, place.other("c"))
            if t >= 2:
                mine["l", t - 1].wait_recv()
                z = place.ring_z(t - 2)
                block = shard(z, **{third: 1 - getattr(place, third)})
                mine["d", t - 1] = put(i, 3 * nz + t - 1, block, block, place.other("c"))
        else:
            if t <= nz - 1:
                if t > 0:
                    mine["z", t].wait_recv()
                z = place.ring_z(t)
                src = ins[i] if t == 0 else shard(z, x=place.x, y=place.y)
                dst = shard(z, x=place.x, y=place.y)
                if t < nz - 1:
                    mine["z", t + 1] = put(i, t, src, dst, place.succ())
                mine["p", t + 1] = put(i, nz + t, src, dst, place.other(second))
            if 1 <= t <= nz:
                if t == 1:
                    mine["own"].wait()
                mine["p", t].wait_recv()
                block = own(third, place.ring_z(t - 1))
                mine["l", t] = put(i, 2 * nz + t, block, block, place.other(third))
                mine["c", t] = put(i, 3 * nz + t, block, block, place.other("c"))
            if t >= 2:
                mine["l", t - 1].wait_recv()
                block = shard(place.ring_z(t - 2), **{third: 1 - getattr(place, third)})
                mine["d", t - 1] = put(i, 4 * nz + t - 1, block, block, place.other("c"))

    stages = nz + 2
    for t in range(stages + n - 1):
        for i in range(n):
            if 0 <= t - i < stages:
                stage(i, t - i)
    for mine in copies:
        for key, copy in mine.items():
            if key[0] in "cd":
                copy.wait_recv()
    for copy in started:
        copy.wait_send()


def gather_all(shards, orders, mesh):
    nx, ndp = mesh.shape["segment"], mesh.shape["dp"]
    if nx != 2 or ndp % 8:
        return [lax.all_gather(s, AXES, axis=0) for s in shards]
    nz, n = ndp // 4, len(shards)
    slots = 5 * nz + 2
    outs = pl.pallas_call(
        functools.partial(gather_kernel, orders, nz),
        out_shape=[jax.ShapeDtypeStruct((2, nz, 2, 2) + s.shape, s.dtype) for s in shards],
        in_specs=[pl.BlockSpec(memory_space=pl.ANY)] * n,
        out_specs=[pl.BlockSpec(memory_space=pl.ANY)] * n,
        scratch_shapes=[
            pltpu.SemaphoreType.DMA((n, slots)),
            pltpu.SemaphoreType.DMA((n, slots)),
            pltpu.SemaphoreType.DMA((n,)),
        ],
        compiler_params=pltpu.CompilerParams(collective_id=0, has_side_effects=True),
        name="gather_weights",
    )(*shards)
    return [o.reshape((nx * ndp,) + s.shape) for o, s in zip(outs, shards)]


def add_to(dst, src):
    lead = dst.shape[:-2]

    def one(j, carry):
        at = (j // 2, j % 2) if len(lead) == 2 else (j,)[: len(lead)]
        at = at + (slice(None), slice(None))
        dst[at] = dst[at] + src[at]
        return carry

    if lead:
        lax.fori_loop(0, math.prod(lead), one, 0)
    else:
        dst[...] = dst[...] + src[...]


def scatter_kernel(orders, nz, *refs):
    n = len(orders)
    ins, outs = refs[:n], refs[n : 2 * n]
    accs, stages, firsts, rings, lasts = (refs[(2 + j) * n : (3 + j) * n] for j in range(5))
    send, recv, local = refs[7 * n :]
    place = Place(nz)
    greet(place)
    started = []

    def put(i, k, src, dst, device):
        copy = pltpu.make_async_remote_copy(
            src_ref=src,
            dst_ref=dst,
            send_sem=send.at[i, k],
            recv_sem=recv.at[i, k],
            device_id=device,
            device_id_type=MESH,
        )
        copy.start()
        started.append(copy)
        return copy

    live = [dict() for _ in orders]

    def load(i, k):
        copy = pltpu.make_async_copy(
            block_of(ins[i], place, place.c, place.ring_z(k)), stages[i].at[k % 2], local.at[i, k % 2]
        )
        copy.start()
        live[i]["o", k] = copy

    def stage(i, s):
        first, second, third = orders[i]
        acc, mine = accs[i], live[i]
        early, ring, late = firsts[i], rings[i], lasts[i]

        def part(k, flip=0, flip2=None):
            own = {axis: getattr(place, axis) for axis in "xy"}
            own[first] = own[first] + flip * (1 - 2 * own[first])
            if flip2 is None:
                own["xy".replace(first, "")] = pl.ds(0, 2)
            else:
                other = "xy".replace(first, "")
                own[other] = own[other] + flip2 * (1 - 2 * own[other])
            return acc.at[k - 1, own["x"], own["y"]]

        if s == 0:
            for k in range(1, nz + 1):
                src = block_of(ins[i], place, 1 - place.c, place.ring_z(k))
                mine["c", k] = put(i, k, src, acc.at[k - 1], place.other("c"))
            load(i, 1)
            load(i, 2)
        if 1 <= s <= nz:
            k = s
            mine["c", k].wait_recv()
            mine["o", k].wait()
            add_to(acc.at[k - 1], stages[i].at[k % 2])
            if k + 2 <= nz:
                load(i, k + 2)
            mine["p", k] = put(i, nz + k, part(k, 1), early.at[k - 1], place.other(first))
        if 2 <= s <= nz + 1:
            k = s - 1
            mine["p", k].wait_recv()
            add_to(part(k), early.at[k - 1])
        if second == "z":
            if s == 2:
                mine["z", 1] = put(i, 2 * nz + 1, part(1), ring.at[0], place.succ())
            if 3 <= s <= nz + 1:
                t = s - 2
                mine["z", t].wait_recv()
                add_to(ring.at[t - 1], part(t + 1))
                if t < nz - 1:
                    mine["z", t + 1] = put(i, 2 * nz + t + 1, ring.at[t - 1], ring.at[t], place.succ())
                else:
                    there = 1 - getattr(place, third)
                    mine["l"] = put(i, 3 * nz + 1, ring.at[t - 1, there], late, place.other(third))
            if s == nz + 2:
                mine["l"].wait_recv()
                outs[i][...] = wide(ring[nz - 2, getattr(place, third)]) + wide(late[...])
        else:
            if 2 <= s <= nz + 1:
                k = s - 1
                mine["l", k] = put(i, 3 * nz + k, part(k, 0, 1), late.at[k - 1], place.other(second))
            if 3 <= s <= nz + 2:
                k = s - 2
                mine["l", k].wait_recv()
                add_to(part(k, 0, 0), late.at[k - 1])
                if k == 1:
                    mine["z", 1] = put(i, 2 * nz + 1, part(1, 0, 0), ring.at[0], place.succ())
                else:
                    t = k - 1
                    mine["z", t].wait_recv()
                    if t < nz - 1:
                        add_to(ring.at[t - 1], part(t + 1, 0, 0))
                        mine["z", t + 1] = put(i, 2 * nz + t + 1, ring.at[t - 1], ring.at[t], place.succ())
                    else:
                        outs[i][...] = wide(ring[t - 1]) + wide(part(nz, 0, 0)[...])

    stages_of = nz + 3
    for t in range(stages_of + n - 1):
        for i in range(n):
            if 0 <= t - i < stages_of:
                stage(i, t - i)
    for copy in started:
        copy.wait_send()


def scatter_all(grads, orders, mesh):
    nx, ndp = mesh.shape["segment"], mesh.shape["dp"]
    if nx != 2 or ndp != 16:
        return [wide(lax.psum_scatter(g, AXES, scatter_dimension=0, tiled=False)) for g in grads]
    nz, n = ndp // 4, len(grads)

    def scratch(lead):
        return [pltpu.VMEM(lead(o) + g.shape[1:], g.dtype) for o, g in zip(orders, grads)]

    slots = 4 * nz + 2
    return pl.pallas_call(
        functools.partial(scatter_kernel, orders, nz),
        out_shape=[jax.ShapeDtypeStruct(g.shape[1:], jnp.float32) for g in grads],
        in_specs=[pl.BlockSpec(memory_space=pl.ANY)] * n,
        out_specs=[pl.BlockSpec(memory_space=pltpu.VMEM)] * n,
        scratch_shapes=scratch(lambda o: (nz, 2, 2))
        + scratch(lambda o: (2, 2, 2))
        + scratch(lambda o: (nz, 2))
        + scratch(lambda o: (nz - 1, 2) if o[1] == "z" else (nz - 1,))
        + scratch(lambda o: () if o[1] == "z" else (nz,))
        + [
            pltpu.SemaphoreType.DMA((n, slots)),
            pltpu.SemaphoreType.DMA((n, slots)),
            pltpu.SemaphoreType.DMA((n, 2)),
        ],
        compiler_params=pltpu.CompilerParams(
            collective_id=1, has_side_effects=True, vmem_limit_bytes=62 * 2**20
        ),
        name="sum_gradients",
    )(*[g.reshape((2, nz, 2, 2) + g.shape[1:]) for g in grads])


def norm_parts(rows):
    centre = rows - jnp.mean(rows, axis=-1, keepdims=True)
    inv = lax.rsqrt(jnp.mean(centre * centre, axis=-1, keepdims=True) + EPSILON)
    return centre * inv, inv


def norm_back(grad, normal, inv, gain):
    m = grad * gain
    part = inv * (
        m - jnp.mean(m, axis=-1, keepdims=True) - normal * jnp.mean(m * normal, axis=-1, keepdims=True)
    )
    return part, jnp.sum(grad * normal, axis=0), jnp.sum(grad, axis=0)


def sums(value):
    return jnp.sum(wide(value), axis=0)


def gelu(t):
    return 0.5 * t * (1.0 + jnp.tanh(GELU_SCALE * (t + 0.044715 * t * t * t)))


def gelu_slope(t):
    th = jnp.tanh(GELU_SCALE * (t + 0.044715 * t * t * t))
    return 0.5 * (1.0 + th) + 0.5 * t * (1.0 - th * th) * GELU_SCALE * (1.0 + 3 * 0.044715 * t * t)


def softmax(logits, length):
    valid = lax.broadcasted_iota(jnp.int32, logits.shape, 2) < length
    masked = jnp.where(valid, logits, -1e30)
    expo = jnp.where(valid, jnp.exp(masked - jnp.max(masked, axis=2, keepdims=True)), 0.0)
    return expo / jnp.sum(expo, axis=2, keepdims=True)


class Layer(NamedTuple):
    ln1_gain: Any
    ln1_bias: Any
    value_weight: Any
    value_bias: Any
    out_weight: Any
    out_bias: Any
    ln2_gain: Any
    ln2_bias: Any
    ffn_in: Any
    ffn_in_bias: Any
    ffn_out: Any
    ffn_out_bias: Any


class Synth(NamedTuple):
    first: Any
    first_bias: Any
    second: Any
    second_bias: Any
    table: Any


def forward(rows, length, w, synth, dense):
    slots, d = rows.shape
    n1, r1 = norm_parts(rows)
    a = half(n1 * w.ln1_gain + w.ln1_bias)
    v = half(mm(a, w.value_weight) + w.value_bias)
    if dense:
        f = mm(a, synth.first) + synth.first_bias
        p = half(gelu(f))
        logits = mm(p, synth.second) + synth.second_bias
        logits = logits.reshape(slots, HEADS, slots).transpose(1, 0, 2)
    else:
        f = p = None
        logits = wide(synth.table).reshape(HEADS, slots, slots)
    probs = half(softmax(logits, length))
    heads = v.reshape(slots, HEADS, d // HEADS)
    mixed = jnp.einsum("hqk,khd->qhd", probs, heads, preferred_element_type=jnp.float32)
    c = half(mixed.reshape(slots, d))
    hid = rows + mm(c, w.out_weight) + w.out_bias
    n2, r2 = norm_parts(hid)
    b = half(n2 * w.ln2_gain + w.ln2_bias)
    z = mm(b, w.ffn_in) + w.ffn_in_bias
    q = half(gelu(z))
    y = hid + mm(q, w.ffn_out) + w.ffn_out_bias
    return half(y), (n1, r1, a, f, p, probs, v, c, n2, r2, b, half(gelu_slope(z)), q)


def backward(g, saved, w, synth, dense):
    n1, r1, a, f, p, probs, v, c, n2, r2, b, slope, q = saved
    slots, d = g.shape
    gy = half(g)
    gz = half(mm_nt(gy, w.ffn_out) * slope)
    part, g_gain2, g_bias2 = norm_back(mm_nt(gz, w.ffn_in), n2, r2, w.ln2_gain)
    ghid = wide(g) + part
    gatt = half(ghid)
    gc = half(mm_nt(gatt, w.out_weight)).reshape(slots, HEADS, d // HEADS)
    heads = v.reshape(slots, HEADS, d // HEADS)
    dprobs = jnp.einsum("qhd,khd->hqk", gc, heads, preferred_element_type=jnp.float32)
    gv = half(
        jnp.einsum("hqk,qhd->khd", probs, gc, preferred_element_type=jnp.float32).reshape(slots, d)
    )
    probs = wide(probs)
    dlogits = probs * (dprobs - jnp.sum(probs * dprobs, axis=2, keepdims=True))
    ga = mm_nt(gv, w.value_weight)
    if dense:
        gb = half(dlogits.transpose(1, 0, 2).reshape(slots, HEADS * slots))
        gf = half(mm_nt(gb, synth.second) * gelu_slope(f))
        ga = ga + mm_nt(gf, synth.first)
        g_synth = Synth(mm_tn(a, gf), sums(gf), mm_tn(p, gb), sums(gb), None)
    else:
        g_synth = Synth(None, None, None, None, dlogits.reshape(HEADS * slots, slots))
    part, g_gain1, g_bias1 = norm_back(ga, n1, r1, w.ln1_gain)
    g_layer = Layer(
        g_gain1,
        g_bias1,
        mm_tn(a, gv),
        sums(gv),
        mm_tn(c, gatt),
        sums(gatt),
        g_gain2,
        g_bias2,
        mm_tn(b, gz),
        sums(gz),
        mm_tn(q, gy),
        sums(gy),
    )
    return half(ghid + part), g_layer, g_synth


def is_matrix(k):
    return k < 12 and k in (2, 4, 8, 10) or k in (12, 14, 16)


MATRICES = (2, 8, 10, 14, 16, 4, 12)
VECTORS = tuple(k for k in range(17) if not is_matrix(k))
ORDERS = ("zxy", "zxy", "xzy", "yzx", "yzx", "zxy", "yzx", "xzy")
SUM_ORDERS = tuple(o[::-1] for o in ORDERS)


def per_device(mesh, boundary, lengths, *parts):
    nx, ndp = mesh.shape["segment"], mesh.shape["dp"]
    devices = nx * ndp
    s = lax.axis_index("segment")
    first = s == 0
    swap = [(0, 1), (1, 0)]
    own = boundary[0, :, 0]
    received = lax.ppermute(jnp.where(first, own[1], own[0]), "segment", swap)
    rows = jnp.where(first, own[0], received)
    cotangent = jnp.where(first, received, own[1])
    length = jnp.where(first, lengths[0, 0], lengths[1, 0])

    flat = jnp.concatenate([parts[k].reshape(-1) for k in VECTORS])
    sizes = [parts[k].size for k in VECTORS]
    lanes = -(-flat.size // 2048) * 16
    packed = half(jnp.pad(flat, (0, lanes * 128 - flat.size)).reshape(lanes, 128))
    shards = [half(parts[k].reshape(parts[k].shape[-2:])) for k in MATRICES] + [packed]
    gathered = gather_all(shards, ORDERS, mesh)

    full = {}
    for k, g in zip(MATRICES, gathered):
        full[k] = g.reshape((nx, ndp * g.shape[1]) + g.shape[2:]) if k < 12 else g.reshape(-1, g.shape[2])
    vec = wide(gathered[-1].reshape(devices, lanes * 128))
    at = 0
    for k, size in zip(VECTORS, sizes):
        piece = vec[:, at : at + size]
        at += size
        full[k] = piece.reshape(nx, ndp * size) if k < 12 else piece.reshape(devices * size)
    layers = [Layer(*[full[k][j] for k in range(12)]) for j in range(2)]
    synth = Synth(*[full[k] for k in range(12, 17)])

    out0, saved0 = forward(wide(rows), length, layers[0], synth, True)
    out1, saved1 = forward(wide(out0), length, layers[1], synth, False)
    gin1, layer1, synth1 = backward(cotangent, saved1, layers[1], synth, False)
    gin0, layer0, synth0 = backward(gin1, saved0, layers[0], synth, True)

    def swapped(for_first, for_second):
        got = lax.ppermute(jnp.where(first, for_second, for_first), "segment", swap)
        return jnp.stack([jnp.where(first, for_first, got), jnp.where(first, got, for_second)])[None, :, None]

    layer_outputs = swapped(out0, out1)
    input_grads = swapped(gin0, gin1)

    grads = [jnp.stack([half(g0), half(g1)]) if is_matrix(k) else jnp.stack([g0, g1]) for k, (g0, g1) in enumerate(zip(layer0, layer1))]
    grads += list(synth0[:4]) + [synth1.table]
    lists = [half(grads[k]).reshape((devices,) + parts[k].shape[-2:]) for k in MATRICES]
    vec = jnp.concatenate([grads[k].reshape(devices, -1) for k in VECTORS], axis=1)
    vec = jnp.pad(vec, ((0, 0), (0, lanes * 128 - vec.shape[1]))).reshape(devices, lanes, 128)
    summed = scatter_all(lists + [vec], SUM_ORDERS, mesh)
    result = {k: g.reshape(parts[k].shape) for k, g in zip(MATRICES, summed)}
    vec = summed[-1].reshape(-1)
    at = 0
    for k, size in zip(VECTORS, sizes):
        result[k] = vec[at : at + size].reshape(parts[k].shape)
        at += size
    return (layer_outputs, input_grads) + tuple(result[k] for k in range(17))


def solution(mesh):
    layer = [P("segment", "dp")] * 12
    layer[2] = layer[4] = layer[8] = layer[10] = P("segment", "dp", None)
    both = P(AXES)
    rows = P(AXES, None)
    boundary = P("segment", None, "dp", None, None)
    weights = tuple(layer) + (rows, both, rows, both, rows)
    return jax.shard_map(
        functools.partial(per_device, mesh),
        mesh=mesh,
        in_specs=(boundary, P(None, "dp")) + weights,
        out_specs=(boundary, boundary) + weights,
        check_vma=False,
    )
```

time: 2370 us -> 751 us (0.32)
  waiting for transfers between devices: 1520 us -> 0.01 us
  Pallas kernels: 0 us -> 410 us
  blocking collectives: 141 us -> 0 us
  other arithmetic: 222 us -> 81.4 us
  matrix products: 283 us -> 157 us
  local copies, waits for them, and re-layouts: 160 us -> 89.1 us
    reduce_scatter x7 -> x0, waiting for transfers between devices: 840 us -> none  [the longest x1 211 us: per_device(): lax.psum_scatter(synth_total[2], ('segment', 'dp'), scatter_dimension=0,...]
    pallas_call x0 -> x2, Pallas kernels: none -> 410 us  [the longest x1 206 us: gather_all(): pl.pallas_call(functools.partial(gather_kernel, orders, nz), out_shape=[j...]
    unnamed x30 -> x0, waiting for transfers between devices: 298 us -> none
    all_gather x7 -> x0, waiting for transfers between devices: 290 us -> none  [the longest x1 84 us: per_device(): lax.all_gather(synth_halves[2], ('segment', 'dp'), axis=0, tiled=True)]
    dot_general x50 -> x35, matrix products: 283 us -> 146 us  [the longest x10 44.6 us: mm_nt(): lax.dot_general(left, right, (((1,), (1,)), ((), ())), preferred_element_...]
    ppermute x4 -> x3, waiting for transfers between devices: 90.9 us -> 0.01 us  [the longest x2 0.01 us: swapped(): got = lax.ppermute(jnp.where(first, for_second, for_first), 'segment', swap)]
    unnamed x2 -> x0, blocking collectives: 81.6 us -> none
    squeeze x1 -> x0, blocking collectives: 59.3 us -> none  [per_device(): common = tuple((piece[0] for piece in gathered))]
  transfers between devices with their start and end apart: 26 -> 3, of which waited for: 21 -> 0; matrix products, arithmetic and copies ran while one was open for 10% -> 14% of each run, Pallas kernels for 0% -> 55%
where the time goes in v1:
time: 751 us; the launch traced here: 746 us
  Pallas kernels  410 us (55%)
  matrix products  157 us (21%)
  local copies, waits for them, and re-layouts  89.1 us (12%)
  other arithmetic  81.4 us (11%)
    pallas_call x1, Pallas kernels, gather_all(): pl.pallas_call(functools.partial(gather_kernel, orders, nz), out_shape=[j...  206 us
    pallas_call x1, Pallas kernels, scatter_all(): pl.pallas_call(functools.partial(scatter_kernel, orders, nz), out_shape=[...  204 us
    dot_general x10, matrix products, mm_nt(): lax.dot_general(left, right, (((1,), (1,)), ((), ())), preferred_element_...  44.6 us
    dot_general x10, matrix products, mm_tn(): lax.dot_general(left, right, (((0,), (0,)), ((), ())), preferred_element_...  40.6 us
    dot_general x10, matrix products, mm(): return jnp.dot(left, right, preferred_element_type=jnp.float32)  37.4 us
    another operation x4, other arithmetic, per_device(): jnp.stack([half(g0), half(g1)])  21.2 us
    slice x6, local copies, waits for them, and re-layouts, per_device(): layers = [Layer(*[full[k][j] for k in range(12)]) for j in range(2)]  20.8 us
    convert_element_type x8, other arithmetic, half(): return value.astype(jnp.bfloat16)  18.5 us
  transfers between devices with their start and end apart: 3, of which 0 were waited for; matrix products, arithmetic and copies ran while one was open for 14% of the time, Pallas kernels for 55%

profile of v1, /device:TPU:0, one launch (start us, length us, event | category | flops | bytes accessed | tf_op | source)
XLA Modules:
  0.0 745.6 jit_solution(7578136788478089858)
XLA Ops:
  0.8 2.5 bitcast_select_fusion.1
  3.3 2.9 collective-permute-start
  13.3 205.5 %gather_weights.1 = (bf16[2,4,2,2,48,768]{5,4,3,2,1,0:T(8,128)(2,1)}, bf16[2,4,2,2,48,3072]{5,4,3,2,1,0:T(8,128)(2,1)}, bf16[2,4,2,2,192,768]{5,4,3,2,1,0:T(8,12...) custom-call(bf16[48,768]{1,0:T(8,128)(2,1)} %get-tuple-element.193.r, ...), custom_call_target="tpu_custom_call" | custom-call | tf_op jit(solution)/shard_map/gather_weights/pallas_call | solution.py:188
  218.8 4.3 select_reduce_fusion.1
  223.4 3.8 select_reduce_fusion
  240.5 9.2 %fusion.76 = (bf16[1,4,2,2,48,3072]{5,4,3,2,1,0:T(8,128)(2,1)}, bf16[1,4,2,2,48,3072]{5,4,3,2,1,0:T(8,128)(2,1)}) fusion(bf16[2,4,2,2,48,3072]{5,4,3,2,1,0:T(8,128)(2,1)} %get-tuple-element.40), kind=kLoop, calls=%fused_computation.205 | loop fusion | bytes 18874368 | tf_op jit(solution)/shard_map/slice | solution.py:521
  249.7 9.6 %copy.61 = f32[12,512,512]{1,2,0:T(8,128)} copy(bf16[12,512,512]{2,1,0:T(8,128)(2,1)} %bitcast.208) | data formatting | bytes 18874368 | tf_op jit(solution)/shard_map/convert_element_type | solution.py:24
  260.9 8.5 %fusion.77 = (bf16[1,4,2,2,192,768]{5,4,3,2,1,0:T(8,128)(2,1)}, bf16[1,4,2,2,192,768]{5,4,3,2,1,0:T(8,128)(2,1)}) fusion(bf16[2,4,2,2,192,768]{5,4,3,2,1,0:T(8,128)(2,1)} %get-tuple-element.41), kind=kLoop, calls=%fused_computation.206 | loop fusion | bytes 18874368 | tf_op jit(solution)/shard_map/slice | solution.py:521
  269.4 3.1 convert_reduce_fusion.6
  274.5 2.2 convolution_add_fusion.2
  278.0 11.8 %convolution_add_fusion = f32[512,6144]{1,0:T(8,128)} fusion(bf16[768,6144]{1,0:T(8,128)(2,1)} %bitcast.285, f32[6144]{0:T(1024)S(1)} %copy-done.49, f32[512,768]{1,0:T(8,128)S(1)} %convolution_add_fusion.2), kind=kOutput, calls=%fused_computation.26 | convolution fusion | flops 4838522880 | bytes 23617536 | tf_op jit(solution)/shard_map/dot_general | solution.py:28
  289.7 12.6 %copy.58 = f32[512,6144]{0,1:T(8,128)} copy(f32[512,6144]{1,0:T(8,128)} %convolution_add_fusion) | data formatting | bytes 25165824 | tf_op jit(solution)/shard_map/add | solution.py:423
  302.3 6.5 bitcast_reduce_fusion
  310.4 10.3 %divide_convert_fusion.1 = (bf16[12,512,512]{1,2,0:T(8,128)(2,1)}, f32[12,512]{1,0:T(8,128)S(1)}) fusion(f32[12,512,512]{1,2,0:T(8,128)} %copy.61, f32[12,512]{1,0:T(8,128)S(1)} %copy-done.45, f32[12,512]{1,0:T(8,128)S(1)} %copy-done.44, pred[512]{0:T(512)(128)(4,1)S(1)} %iota_compare_fusion, f32[12,512]{1,0:T(8,128)S(1)} %bitcast_reduce_fusion, ...), kind=kLoop, calls=%fused_computation.14 | loop fusion | flops 28305408 | bytes 31556096 | tf_op jit(solution)/shard_map/convert_element_type | solution.py:20
  320.8 3.9 divide_convert_fusion.2
  330.2 2.7 fusion.67
  333.0 4.0 convert_reduce_fusion.3
  338.8 4.2 convolution_convert_fusion.14
  344.7 4.9 fusion.68
  349.6 5.7 convolution_convert_fusion.1
  355.3 6.2 convert_reduce_fusion.1
  361.5 3.1 multiply_reduce_fusion.1
  364.6 4.8 convolution_convert_fusion.3
  373.6 2.3 copy.63
  375.9 5.9 convert_reduce_fusion.10
  381.9 11.2 %fusion.1 = bf16[12,512,512]{1,2,0:T(8,128)(2,1)} fusion(bf16[12,512,512]{1,2,0:T(8,128)(2,1)} %get-tuple-element.158, bf16[512,12,64]{0,2,1:T(8,128)(2,1)} %bitcast.250, bf16[512,12,64]{0,2,1:T(8,128)(2,1)} %bitcast.218), kind=kOutput, calls=%fused_computation.3 | convolution fusion | flops 824187392 | bytes 14155776 | tf_op jit(solution)/shard_map/sub | solution.py:456
  393.1 3.1 fusion.39
  398.1 8.8 %convert_reduce_fusion.2 = (f32[3072]{0:T(1024)S(1)}, bf16[512,3072]{1,0:T(8,128)(2,1)S(1)}) fusion(f32[512,3072]{1,0:T(8,128)} %copy-done.84, f32[3072]{0:T(1024)S(1)} %copy-done.57, bf16[512,768]{1,0:T(8,128)(2,1)S(1)} %get-tuple-element.108, bf16[3072,768]{1,0:T(8,128)(2,1)} %bitcast.241), kind=kOutput, calls=%fused_computation.41 | convolution fusion | flops 2453664768 | bytes 14966784 | tf_op jit(solution)/shard_map/dot_general | solution.py:36
  406.9 5.5 convolution_convert_fusion.2
  412.5 3.1 multiply_reduce_fusion.2
  415.6 5.2 convolution_convert_fusion.4
  420.8 2.2 convolution_convert_fusion.8
  427.8 2.3 copy.65
  430.1 5.2 convert_reduce_fusion.11
  437.5 2.1 convolution_convert_fusion.9
  439.6 6.6 multiply_reduce_fusion
  446.3 8.1 %convert_reduce_fusion = (f32[12,512]{1,0:T(8,128)S(1)}, bf16[512,12,512]{0,2,1:T(8,128)(2,1)S(1)}) fusion(f32[512,12]{0,1:T(8,128)S(1)} %bitcast.278, f32[12,512,512]{1,2,0:T(8,128)} %get-tuple-element.174, f32[512,12]{0,1:T(8,128)S(1)} %bitcast.274, f32[512,12]{0,1:T(8,128)S(1)} %bitcast.273, f32[512,12,512]{0,2,1:T(8,128)S(1)} %bitcast.205, ...), kind=kLoop, calls=%fused_computation.11 | loop fusion | flops 34596864 | bytes 31556096 | tf_op jit(solution)/shard_map/reduce_sum | solution.py:373
  454.5 10.5 %convert_reduce_fusion.7 = (f32[768]{0:T(1024)S(1)}, bf16[512,768]{1,0:T(8,128)(2,1)}) fusion(f32[512,768]{1,0:T(8,128)S(1)} %copy-done.86, bf16[512,6144]{0,1:T(8,128)(2,1)S(1)} %bitcast.221, bf16[768,6144]{1,0:T(8,128)(2,1)} %bitcast.286), kind=kOutput, calls=%fused_computation.105 | convolution fusion | flops 4840094720 | bytes 18091008 | tf_op jit(solution)/shard_map/dot_general | solution.py:36
  465.0 8.2 %convolution_convert_fusion = bf16[768,6144]{1,0:T(8,128)(2,1)} fusion(bf16[512,6144]{0,1:T(8,128)(2,1)S(1)} %bitcast.222, f32[512,768]{1,0:T(8,128)S(1)} %copy-done.86), kind=kOutput, calls=%fused_computation.18 | convolution fusion | flops 4840095744 | bytes 17301504 | tf_op jit(solution)/shard_map/dot_general | solution.py:32
  473.3 8.1 %broadcast_select_fusion.1 = (bf16[512,768]{1,0:T(8,128)(2,1)}, bf16[512,768]{1,0:T(8,128)(2,1)}) fusion(bf16[512,768]{1,0:T(8,128)(2,1)S(1)} %copy-done.6, pred[]{:T(512)S(6)} %eq.3, f32[768]{0:T(1024)S(1)} %copy-done.62, f32[512,768]{1,0:T(8,128)S(1)} %copy-done.15, bf16[3072,768]{1,0:T(8,128)(2,1)S(1)} %bitcast.232, f32[512,3072]{1,0:T(8,128)} %copy-done.83, ...), kind=kOutput, calls=%fused_computation.151 | convolution fusion | flops 2433220608 | bytes 14957569 | tf_op jit(solution)/shard_map/dot_general | solution.py:28
  482.3 4.4 fusion.48
  487.1 3.6 broadcast_select_fusion
  492.7 8.3 %pad_maximum_fusion.1.refs_2_ = bf16[2,4,2,2,192,768]{5,4,3,2,1,0:T(8,128)(2,1)} fusion(bf16[1,4,2,2,192,768]{5,4,3,2,1,0:T(8,128)(2,1)} %bitcast.225, bf16[1,4,2,2,192,768]{5,4,3,2,1,0:T(8,128)(2,1)} %bitcast.233), kind=kLoop, calls=%fused_computation.25 | loop fusion | flops 4718592 | bytes 18874368 | tf_op jit(solution)/shard_map/stack | solution.py:536
  501.0 8.3 %pad_maximum_fusion.refs_1_ = bf16[2,4,2,2,48,3072]{5,4,3,2,1,0:T(8,128)(2,1)} fusion(bf16[1,4,2,2,48,3072]{5,4,3,2,1,0:T(8,128)(2,1)} %bitcast.226, bf16[1,4,2,2,48,3072]{5,4,3,2,1,0:T(8,128)(2,1)} %bitcast.234), kind=kLoop, calls=%fused_computation.24 | loop fusion | flops 4718592 | bytes 18874368 | tf_op jit(solution)/shard_map/stack | solution.py:536
  509.2 3.0 pad_maximum_fusion.3.refs_5_
  514.0 8.7 %copy.69 = bf16[12,512,512]{2,1,0:T(8,128)(2,1)} copy(bf16[12,512,512]{1,2,0:T(8,128)(2,1)} %fusion.1) | data formatting | bytes 12582912 | tf_op jit(solution)/shard_map/convert_element_type | solution.py:20
  523.5 3.1 convolution_convert_fusion.5
  526.7 204.0 %sum_gradients.1 = (f32[48,768]{1,0:T(8,128)}, f32[48,3072]{1,0:T(8,128)}, f32[192,768]{1,0:T(8,128)}, f32[24,6144]{1,0:T(8,128)}, f32[192,512]{1,0:T(8,128)}, /...) custom-call(bf16[2,4,2,2,48,768]{5,4,3,2,1,0:T(8,128)(2,1)} %pad_maximum_fusion.2.refs_0_, ...), custom_call_target="tpu_custom_call" | custom-call | tf_op jit(solution)/shard_map/sum_gradients/pallas_call | solution.py:336
  (355 shorter events, 67.6 us)
Async XLA Ops:
  0.7 7.5 %copy-start.73 = (f32[1,48]{1,0:T(1,128)S(1)}, f32[1,48]{1,0:T(1,128)}, u32[]{:S(2)}) copy-start(f32[1,48]{1,0:T(1,128)} %param.24) | copy-start | bytes 580
  0.7 7.5 %copy-start.74 = (f32[1,48]{1,0:T(1,128)S(1)}, f32[1,48]{1,0:T(1,128)}, u32[]{:S(2)}) copy-start(f32[1,48]{1,0:T(1,128)} %param.22) | copy-start | bytes 580
  0.7 7.5 %copy-start.75 = (f32[1,48]{1,0:T(1,128)S(1)}, f32[1,48]{1,0:T(1,128)}, u32[]{:S(2)}) copy-start(f32[1,48]{1,0:T(1,128)} %param.27) | copy-start | bytes 580
  0.7 7.5 %copy-start.76 = (f32[1,48]{1,0:T(1,128)S(1)}, f32[1,48]{1,0:T(1,128)}, u32[]{:S(2)}) copy-start(f32[1,48]{1,0:T(1,128)} %param.26) | copy-start | bytes 580
  0.8 7.5 %copy-start.77 = (f32[1,48]{1,0:T(1,128)S(1)}, f32[1,48]{1,0:T(1,128)}, u32[]{:S(2)}) copy-start(f32[1,48]{1,0:T(1,128)} %param.32) | copy-start | bytes 580
  0.8 7.5 %copy-start.78 = (f32[1,48]{1,0:T(1,128)S(1)}, f32[1,48]{1,0:T(1,128)}, u32[]{:S(2)}) copy-start(f32[1,48]{1,0:T(1,128)} %param.28) | copy-start | bytes 580
  0.8 8.2 %copy-start.47 = (f32[24,768]{1,0:T(8,128)S(1)}, f32[24,768]{1,0:T(8,128)}, u32[]{:S(2)}) copy-start(f32[24,768]{1,0:T(8,128)} %param.33) | copy-start | bytes 221188
  0.8 8.8 %copy-start.38 = (f32[192,512]{1,0:T(8,128)S(1)}, f32[192,512]{1,0:T(8,128)}, u32[]{:S(2)}) copy-start(f32[192,512]{1,0:T(8,128)} %param.37) | copy-start | bytes 1179652
  0.8 9.5 %copy-start.32 = (f32[1,48,3072]{2,1,0:T(8,128)S(1)}, f32[1,48,3072]{2,1,0:T(8,128)}, u32[]{:S(2)}) copy-start(f32[1,48,3072]{2,1,0:T(8,128)} %param.29) | copy-start | bytes 1769476
  0.8 10.3 %copy-start.33 = (f32[1,192,768]{2,1,0:T(8,128)S(1)}, f32[1,192,768]{2,1,0:T(8,128)}, u32[]{:S(2)}) copy-start(f32[1,192,768]{2,1,0:T(8,128)} %param.31) | copy-start | bytes 1769476
  3.3 8.5 %copy-start.34 = (f32[24,6144]{1,0:T(8,128)S(1)}, f32[24,6144]{1,0:T(8,128)}, u32[]{:S(2)}) copy-start(f32[24,6144]{1,0:T(8,128)} %param.35) | copy-start | bytes 1769476
  3.3 266.1 %collective-permute-start = (bf16[512,768]{1,0:T(8,128)(2,1)}, bf16[512,768]{1,0:T(8,128)(2,1)}, u32[]{:S(2)}, u32[]{:S(2)}) collective-permute-start(bf16[512,768]{1,0:T(8,128)(2,1)} %bitcast_select_fusion.1), channel_id=1, source_target_pairs={{0,16},{16,0},{1,17},{17,1},{2,18},{18,2},{3,19},{19,3},{4,20},{20... | collective-permute-start | bytes 2359304 | tf_op jit(solution)/shard_map/ppermute | solution.py:500
  223.4 15.8 %copy-start.22 = (bf16[2,4,2,2,48,768]{5,4,3,2,1,0:T(8,128)(2,1)S(1)}, bf16[2,4,2,2,48,768]{5,4,3,2,1,0:T(8,128)(2,1)}, u32[]{:S(2)}) copy-start(bf16[2,4,2,2,48,768]{5,4,3,2,1,0:T(8,128)(2,1)} %get-tuple-element.36) | copy-start | bytes 7077892
  231.7 42.4 %copy-start.53 = (f32[768]{0:T(1024)}, f32[768]{0:T(1024)S(1)}, u32[]{:S(2)}) copy-start(f32[768]{0:T(1024)S(1)} %mul.348) | copy-start | bytes 9220
  240.5 32.4 %copy-start.23 = (bf16[1,4,2,2,48,768]{5,4,3,2,1,0:T(8,128)(2,1)}, bf16[1,4,2,2,48,768]{5,4,3,2,1,0:T(8,128)(2,1)S(1)}, u32[]{:S(2)}) copy-start(bf16[1,4,2,2,48,768]{5,4,3,2,1,0:T(8,128)(2,1)S(1)} %get-tuple-element.128) | copy-start | bytes 3538948
  249.7 9.6 %copy-start.21 = (bf16[2,4,2,2,48,768]{5,4,3,2,1,0:T(8,128)(2,1)S(1)}, bf16[2,4,2,2,48,768]{5,4,3,2,1,0:T(8,128)(2,1)}, u32[]{:S(2)}) copy-start(bf16[2,4,2,2,48,768]{5,4,3,2,1,0:T(8,128)(2,1)} %get-tuple-element.39) | copy-start | bytes 7077892
  260.9 8.5 %copy-start.13 = (bf16[1,2,1,512,768]{4,3,2,1,0:T(8,128)(2,1)S(1)}, bf16[1,2,1,512,768]{4,3,2,1,0:T(8,128)(2,1)}, u32[]{:S(2)}) copy-start(bf16[1,2,1,512,768]{4,3,2,1,0:T(8,128)(2,1)} %param.19) | copy-start | bytes 4718596
  272.5 54.9 %copy-start.7 = (bf16[512,768]{1,0:T(8,128)(2,1)}, bf16[512,768]{1,0:T(8,128)(2,1)S(1)}, u32[]{:S(2)}) copy-start(bf16[512,768]{1,0:T(8,128)(2,1)S(1)} %get-tuple-element.124) | copy-start | bytes 2359300
  289.7 19.1 %copy-start.45 = (f32[12,512]{1,0:T(8,128)S(1)}, f32[12,512]{1,0:T(8,128)}, u32[]{:S(2)}) copy-start(f32[12,512]{1,0:T(8,128)} %div.81) | copy-start | bytes 73732
  302.3 8.2 %copy-start = (f32[512,6144]{0,1:T(8,128)S(1)}, f32[512,6144]{0,1:T(8,128)}, u32[]{:S(2)}) copy-start(f32[512,6144]{0,1:T(8,128)} %copy.58) | copy-start | bytes 37748740
  302.3 8.2 %copy-start.44 = (f32[12,512]{1,0:T(8,128)S(1)}, f32[12,512]{1,0:T(8,128)}, u32[]{:S(2)}) copy-start(f32[12,512]{1,0:T(8,128)} %sub.142) | copy-start | bytes 73732
  320.8 8.0 %slice-start.9 = ((s8[4718592]{0:T(1024)(128)(4,1)}), s8[4194304]{0:T(1024)(128)(4,1)S(1)}, s32[]{:S(2)}) async-start(s8[4718592]{0:T(1024)(128)(4,1)} %bitcast.235), calls=%async_computation.9 | async-start | bytes 8388608
  337.1 56.0 %copy-start.4 = (bf16[512,768]{1,0:T(8,128)(2,1)}, bf16[512,768]{1,0:T(8,128)(2,1)S(1)}, u32[]{:S(2)}) copy-start(bf16[512,768]{1,0:T(8,128)(2,1)S(1)} %get-tuple-element.165) | copy-start | bytes 2359300
  344.0 25.4 %copy-start.14 = (f32[512,768]{1,0:T(8,128)}, f32[512,768]{1,0:T(8,128)S(1)}, u32[]{:S(2)}) copy-start(f32[512,768]{1,0:T(8,128)S(1)} %get-tuple-element.167) | copy-start | bytes 4718596
  344.7 10.6 %slice-start.5 = ((s8[4718592]{0:T(1024)(128)(4,1)}), s8[4194304]{0:T(1024)(128)(4,1)S(1)}, s32[]{:S(2)}) async-start(s8[4718592]{0:T(1024)(128)(4,1)} %bitcast.227), calls=%async_computation.5 | async-start | bytes 8388608
  349.5 5.7 copy-start.83
  349.6 5.7 slice-start.6
  349.6 11.9 %slice-start.15 = ((s8[4718592]{0:T(1024)(128)(4,1)}), s8[4194304]{0:T(1024)(128)(4,1)S(1)}, s32[]{:S(2)}) async-start(s8[4718592]{0:T(1024)(128)(4,1)} %bitcast.246), calls=%async_computation.15 | async-start | bytes 8388608
  355.3 6.2 slice-start.16
  393.0 19.4 %slice-start.11 = ((s8[4718592]{0:T(1024)(128)(4,1)}), s8[4194304]{0:T(1024)(128)(4,1)S(1)}, s32[]{:S(2)}) async-start(s8[4718592]{0:T(1024)(128)(4,1)} %bitcast.238), calls=%async_computation.11 | async-start | bytes 8388608
  396.1 10.8 %slice-start.17 = ((s8[6291456]{0:T(1024)(128)(4,1)}), s8[4194304]{0:T(1024)(128)(4,1)S(1)}, s32[]{:S(2)}) async-start(s8[6291456]{0:T(1024)(128)(4,1)} %bitcast.289), calls=%async_computation.17 | async-start | bytes 8388608
  398.1 8.9 %slice-start.18 = ((s8[6291456]{0:T(1024)(128)(4,1)}), s8[2097152]{0:T(1024)(128)(4,1)S(1)}, s32[]{:S(2)}) async-start(s8[6291456]{0:T(1024)(128)(4,1)} %bitcast.289), calls=%async_computation.18 | async-start | bytes 4194304
  398.1 14.4 %slice-start.12 = ((s8[4718592]{0:T(1024)(128)(4,1)}), s8[524288]{0:T(1024)(128)(4,1)S(1)}, s32[]{:S(2)}) async-start(s8[4718592]{0:T(1024)(128)(4,1)} %bitcast.238), calls=%async_computation.12 | async-start | bytes 1048576
  430.1 9.5 %slice-start.3 = ((s8[6291456]{0:T(1024)(128)(4,1)}), s8[4194304]{0:T(1024)(128)(4,1)S(1)}, s32[]{:S(2)}) async-start(s8[6291456]{0:T(1024)(128)(4,1)} %bitcast.206), calls=%async_computation.3 | async-start | bytes 8388608
  437.5 8.8 %slice-start = ((s8[12582912]{0:T(1024)(128)(4,1)}), s8[4194304]{0:T(1024)(128)(4,1)S(1)}, s32[]{:S(2)}) async-start(s8[12582912]{0:T(1024)(128)(4,1)} %bitcast.203), calls=%async_computation | async-start | bytes 8388608
  439.6 6.6 slice-start.1
  439.6 6.6 slice-start.2
  446.3 8.2 %copy-start.86 = (f32[512,768]{1,0:T(8,128)S(1)}, f32[512,768]{1,0:T(8,128)}, u32[]{:S(2)}) copy-start(f32[512,768]{1,0:T(8,128)} %copy-done.85) | copy-start | bytes 4718596
  446.3 27.0 %slice-start.7 = ((s8[4718592]{0:T(1024)(128)(4,1)}), s8[4194304]{0:T(1024)(128)(4,1)S(1)}, s32[]{:S(2)}) async-start(s8[4718592]{0:T(1024)(128)(4,1)} %bitcast.230), calls=%async_computation.7 | async-start | bytes 8388608
  454.4 18.8 %slice-start.8 = ((s8[4718592]{0:T(1024)(128)(4,1)}), s8[524288]{0:T(1024)(128)(4,1)S(1)}, s32[]{:S(2)}) async-start(s8[4718592]{0:T(1024)(128)(4,1)} %bitcast.230), calls=%async_computation.8 | async-start | bytes 1048576
  465.0 8.2 %copy-start.52 = (f32[768]{0:T(1024)S(1)}, f32[768]{0:T(1024)}, u32[]{:S(2)}) copy-start(f32[768]{0:T(1024)} %get-tuple-element.109) | copy-start | bytes 9220
  465.0 8.3 %copy-start.6 = (bf16[512,768]{1,0:T(8,128)(2,1)S(1)}, bf16[512,768]{1,0:T(8,128)(2,1)}, u32[]{:S(2)}) copy-start(bf16[512,768]{1,0:T(8,128)(2,1)} %copy-done.4) | copy-start | bytes 2359300
  465.0 8.3 %copy-start.15 = (f32[512,768]{1,0:T(8,128)S(1)}, f32[512,768]{1,0:T(8,128)}, u32[]{:S(2)}) copy-start(f32[512,768]{1,0:T(8,128)} %copy-done.14) | copy-start | bytes 4718596
  465.0 8.3 %copy-start.62 = (f32[768]{0:T(1024)S(1)}, f32[768]{0:T(1024)}, u32[]{:S(2)}) copy-start(f32[768]{0:T(1024)} %add.298) | copy-start | bytes 9220
  482.2 252.7 %collective-permute-start.1 = (bf16[512,768]{1,0:T(8,128)(2,1)}, bf16[512,768]{1,0:T(8,128)(2,1)}, u32[]{:S(2)}, u32[]{:S(2)}) collective-permute-start(bf16[512,768]{1,0:T(8,128)(2,1)} %get-tuple-element.168), channel_id=1, source_target_pairs={{0,16},{16,0},{1,17},{17,1},{2,18},{18,2},{3,19},{19,3},{4,20},{20... | collective-permute-start | bytes 2359304 | tf_op jit(solution)/shard_map/ppermute | solution.py:530
  490.7 246.7 %collective-permute-start.2 = (bf16[512,768]{1,0:T(8,128)(2,1)}, bf16[512,768]{1,0:T(8,128)(2,1)}, u32[]{:S(2)}, u32[]{:S(2)}) collective-permute-start(bf16[512,768]{1,0:T(8,128)(2,1)} %get-tuple-element.115), channel_id=1, source_target_pairs={{0,16},{16,0},{1,17},{17,1},{2,18},{18,2},{3,19},{19,3},{4,20},{20... | collective-permute-start | bytes 2359304 | tf_op jit(solution)/shard_map/ppermute | solution.py:530
  501.0 8.3 %copy-start.18 = (bf16[768,768]{1,0:T(8,128)(2,1)S(1)}, bf16[768,768]{1,0:T(8,128)(2,1)}, u32[]{:S(2)}) copy-start(bf16[768,768]{1,0:T(8,128)(2,1)} %convolution_convert_fusion.6) | copy-start | bytes 3538948
  514.0 9.5 %copy-start.9 = (bf16[512,768]{1,0:T(8,128)(2,1)S(1)}, bf16[512,768]{1,0:T(8,128)(2,1)}, u32[]{:S(2)}) copy-start(bf16[512,768]{1,0:T(8,128)(2,1)} %copy-done.7) | copy-start | bytes 2359300
  (61 other events, 200.9 us)

commit v2 on v1

--- a/solution.py
+++ b/solution.py
@@ -355,137 +355,428 @@
     )(*[g.reshape((2, nz, 2, 2) + g.shape[1:]) for g in grads])
 
 
+ROWS = 256
+GAIN1, BIAS1, VALUE_B, OUT_B, GAIN2, BIAS2, OUTER_B, FIRST_B = range(8)
+
+
+def chunks(rows, size=ROWS):
+    return [slice(at, at + size) for at in range(0, rows, size)]
+
+
 def norm_parts(rows):
     centre = rows - jnp.mean(rows, axis=-1, keepdims=True)
     inv = lax.rsqrt(jnp.mean(centre * centre, axis=-1, keepdims=True) + EPSILON)
     return centre * inv, inv
 
 
-def norm_back(grad, normal, inv, gain):
-    m = grad * gain
-    part = inv * (
-        m - jnp.mean(m, axis=-1, keepdims=True) - normal * jnp.mean(m * normal, axis=-1, keepdims=True)
-    )
-    return part, jnp.sum(grad * normal, axis=0), jnp.sum(grad, axis=0)
+def row_loop(rows, body, init):
+    return lax.fori_loop(0, rows // 128, lambda j, c: body(pl.ds(pl.multiple_of(j * 128, 128), 128), c), init)
+
+
+def norm_into(read, write, gain, shift, rows):
+    def body(r, carry):
+        write[r, :] = half(norm_parts(read(r))[0] * gain + shift)
+        return carry
+
+    row_loop(rows, body, 0)
+
+
+def norm_back(read, grad, gain, rows, done):
+    def body(r, carry):
+        normal, inv = norm_parts(read(r))
+        m_hat = grad(r)
+        m = m_hat * gain
+        part = inv * (
+            m - jnp.mean(m, axis=-1, keepdims=True) - normal * jnp.mean(m * normal, axis=-1, keepdims=True)
+        )
+        done(r, part)
+        return carry[0] + sums(m_hat * normal), carry[1] + sums(m_hat)
+
+    zero = jnp.zeros_like(gain)
+    return row_loop(rows, body, (zero, zero))
 
 
 def sums(value):
-    return jnp.sum(wide(value), axis=0)
-
-
-def gelu(t):
-    return 0.5 * t * (1.0 + jnp.tanh(GELU_SCALE * (t + 0.044715 * t * t * t)))
-
-
-def gelu_slope(t):
-    th = jnp.tanh(GELU_SCALE * (t + 0.044715 * t * t * t))
-    return 0.5 * (1.0 + th) + 0.5 * t * (1.0 - th * th) * GELU_SCALE * (1.0 + 3 * 0.044715 * t * t)
-
-
-def softmax(logits, length):
-    valid = lax.broadcasted_iota(jnp.int32, logits.shape, 2) < length
-    masked = jnp.where(valid, logits, -1e30)
-    expo = jnp.where(valid, jnp.exp(masked - jnp.max(masked, axis=2, keepdims=True)), 0.0)
-    return expo / jnp.sum(expo, axis=2, keepdims=True)
-
-
-class Layer(NamedTuple):
-    ln1_gain: Any
-    ln1_bias: Any
-    value_weight: Any
-    value_bias: Any
-    out_weight: Any
-    out_bias: Any
-    ln2_gain: Any
-    ln2_bias: Any
-    ffn_in: Any
-    ffn_in_bias: Any
-    ffn_out: Any
-    ffn_out_bias: Any
-
-
-class Synth(NamedTuple):
+    return jnp.sum(wide(value), axis=0, keepdims=True)
+
+
+def gelu_both(t):
+    square = t * t
+    s = 0.5 + 0.5 * jnp.tanh(t * (GELU_SCALE + GELU_SCALE * 0.044715 * square))
+    value = t * s
+    slope = s + value * (1.0 - s) * (2 * GELU_SCALE + 6 * GELU_SCALE * 0.044715 * square)
+    return value, slope
+
+
+def forward_kernel(dense, pairs, parts, length_ref, x_ref, vec_ref, value_ref, out_ref, *refs):
+    if dense:
+        first_ref, first_b, second_ref, second_b, *refs = refs
+        inner_ref, inner_b, outer_ref, y_ref, a_ref, v_ref, probs_ref, c_ref, hid_ref, b_ref, q_ref, slope_ref, *refs = refs
+        p_ref, first_slope, acc = refs
+    else:
+        table_ref, *refs = refs
+        inner_ref, inner_b, outer_ref, y_ref, a_ref, v_ref, probs_ref, c_ref, hid_ref, b_ref, q_ref, slope_ref, acc = refs
+    i = pl.program_id(0)
+    rows, width = x_ref.shape
+    head = width // HEADS
+
+    def vec(k):
+        return vec_ref[0, k : k + 1, :]
+
+    @pl.when(i == 0)
+    def _():
+        norm_into(lambda r: wide(x_ref[r, :]), a_ref, vec(GAIN1), vec(BIAS1), rows)
+        for r in chunks(rows):
+            v_ref[r] = half(mm(a_ref[r], value_ref[0]) + vec(VALUE_B))
+            if dense:
+                value, slope = gelu_both(mm(a_ref[r], first_ref[...]) + first_b[...])
+                p_ref[r] = half(value)
+                first_slope[r] = half(slope)
+
+    @pl.when(i < pairs)
+    def _():
+        at = pl.ds(pl.multiple_of(i * 2 * head, 2 * head), 2 * head)
+        v = v_ref[:, at]
+        slots = probs_ref.shape[2]
+        hidden_keys = lax.broadcasted_iota(jnp.int32, (1, slots), 1) >= length_ref[0]
+        shut = jnp.where(hidden_keys, -1e30, 0.0)
+        lower = lax.broadcasted_iota(jnp.int32, (1, 2 * head), 1) < head
+        for r in chunks(rows):
+            mixed = []
+            for h in range(2):
+                if dense:
+                    cols = slice(h * slots, (h + 1) * slots)
+                    logits = mm(p_ref[r], second_ref[:, cols]) + jnp.where(hidden_keys, -1e30, second_b[:, cols])
+                else:
+                    logits = wide(table_ref[h * slots + r.start : h * slots + r.stop, :]) + shut
+                expo = jnp.exp(logits - jnp.max(logits, axis=1, keepdims=True))
+                probs = half(expo * (1.0 / jnp.sum(expo, axis=1, keepdims=True)))
+                probs_ref[h, r] = probs
+                mixed.append(mm(probs, v))
+            c_ref[r, at] = half(jnp.where(lower, mixed[0], mixed[1]))
+
+    @pl.when(i == pairs - 1)
+    def _():
+        for r in chunks(rows):
+            hid_ref[r] = wide(x_ref[r]) + mm(c_ref[r], out_ref[0]) + vec(OUT_B)
+        norm_into(lambda r: hid_ref[r, :], b_ref, vec(GAIN2), vec(BIAS2), rows)
+
+    @pl.when(i >= pairs)
+    def _():
+        for r in chunks(rows):
+            value, slope = gelu_both(mm(b_ref[r], inner_ref[0]) + inner_b[0])
+            q = half(value)
+            q_ref[r] = q
+            slope_ref[r] = half(slope)
+            more = mm(q, outer_ref[0])
+
+            @pl.when(i == pairs)
+            def _():
+                acc[r] = more
+
+            @pl.when(i > pairs)
+            def _():
+                acc[r] += more
+
+    @pl.when(i == pairs + parts - 1)
+    def _():
+        for r in chunks(rows):
+            y_ref[r] = half(hid_ref[r] + acc[r] + vec(OUTER_B))
+
+
+def backward_kernel(dense, layer, pairs, parts, *refs):
+    g_ref, x_ref, hid_ref, b_ref, c_ref, a_ref, v_ref, q_ref, slope_ref, probs_ref, vec_ref, *refs = refs
+    inner_ref, outer_ref, out_ref, value_ref, *refs = refs
+    if dense:
+        p_ref, first_slope, first_ref, second_ref, *refs = refs
+    if layer == 0:
+        refs = refs[6:]
+    gx_ref, g_outer, g_inner, g_out, g_value, g_vec, g_inner_b, *refs = refs
+    if dense:
+        g_first, g_second, g_second_b, *refs = refs
+    else:
+        g_table, *refs = refs
+    acc, ghid, gatt, gc_ref, gv_ref, db, *refs = refs
+    i = pl.program_id(0)
+    rows, width = x_ref.shape
+    head = width // HEADS
+
+    def vec(k):
+        return vec_ref[0, k : k + 1, :]
+
+    def put(k, value):
+        g_vec[0, k : k + 1, :] = value
+
+    @pl.when(i < parts)
+    def _():
+        gy = g_ref[...]
+        for r in chunks(rows):
+            gz = half(mm_nt(g_ref[r], outer_ref[0]) * wide(slope_ref[r]))
+            db[0, r] = gz
+            more = mm_nt(gz, inner_ref[0])
+
+            @pl.when(i == 0)
+            def _():
+                acc[r] = more
+
+            @pl.when(i > 0)
+            def _():
+                acc[r] += more
+
+        gz = db[0]
+        g_outer[0] = half(mm_tn(q_ref[...], gy))
+        g_inner[0] = half(mm_tn(b_ref[...], gz))
+        g_inner_b[0] = sums(gz)
+
+    @pl.when(i == parts - 1)
+    def _():
+        def done(r, part):
+            total = wide(g_ref[r, :]) + part
+            ghid[r, :] = total
+            gatt[r, :] = half(total)
+
+        gain, shift = norm_back(lambda r: hid_ref[r, :], lambda r: acc[r, :], vec(GAIN2), rows, done)
+        put(GAIN2, gain)
+        put(BIAS2, shift)
+        put(OUTER_B, sums(g_ref[...]))
+        put(OUT_B, sums(gatt[...]))
+        g_out[0] = half(mm_tn(c_ref[...], gatt[...]))
+        for r in chunks(rows):
+            gc_ref[r] = half(mm_nt(gatt[r], out_ref[0]))
+
+    @pl.when(i >= parts)
+    def _():
+        at = pl.ds(pl.multiple_of((i - parts) * 2 * head, 2 * head), 2 * head)
+        slots = probs_ref.shape[2]
+        lower = lax.broadcasted_iota(jnp.int32, (1, 2 * head), 1) < head
+        v, gc = v_ref[:, at], gc_ref[:, at]
+        values = []
+        for h in range(2):
+            mine = lower if h == 0 else jnp.logical_not(lower)
+            v_own = jnp.where(mine, v, jnp.zeros_like(v))
+            cols = slice(h * slots, (h + 1) * slots)
+            for r in chunks(rows):
+                probs = wide(probs_ref[h, r])
+                weighed = probs * mm_nt(gc_ref[r, at], v_own)
+                grad = half(weighed - probs * jnp.sum(weighed, axis=1, keepdims=True))
+                db[h, r] = grad
+                if not dense:
+                    g_table[h * slots + r.start : h * slots + r.stop, :] = grad
+            values.append(mm_tn(probs_ref[h], gc))
+            if dense:
+                grad = db[h]
+                g_second[:, cols] = half(mm_tn(p_ref[...], grad))
+                g_second_b[:, cols] = sums(grad)
+                for r in chunks(rows):
+                    more = mm_nt(db[h, r], second_ref[:, cols])
+                    if h == 0:
+
+                        @pl.when(i == parts)
+                        def _():
+                            acc[r] = more
+
+                        @pl.when(i > parts)
+                        def _():
+                            acc[r] += more
+
+                    else:
+                        acc[r] += more
+        gv_ref[:, at] = half(jnp.where(lower, values[0], values[1]))
+
+    @pl.when(i == pairs + parts - 1)
+    def _():
+        gv = gv_ref[...]
+        put(VALUE_B, sums(gv))
+        g_value[0] = half(mm_tn(a_ref[...], gv))
+        if dense:
+            for r in chunks(rows):
+                gatt[r] = half(acc[r] * wide(first_slope[r]))
+            gf = gatt[...]
+            put(FIRST_B, sums(gf))
+            g_first[...] = half(mm_tn(a_ref[...], gf))
+        else:
+            put(FIRST_B, jnp.zeros((1, width), jnp.float32))
+        for r in chunks(rows):
+            ga = mm_nt(gv_ref[r], value_ref[0])
+            if dense:
+                ga = ga + mm_nt(gatt[r], first_ref[...])
+            acc[r] = ga
+
+        def done(r, part):
+            gx_ref[r, :] = half(ghid[r, :] + part)
+
+        gain, shift = norm_back(lambda r: wide(x_ref[r, :]), lambda r: acc[r, :], vec(GAIN1), rows, done)
+        put(GAIN1, gain)
+        put(BIAS1, shift)
+
+
+class Weights(NamedTuple):
+    vectors: Any
+    value: Any
+    out: Any
+    inner: Any
+    inner_b: Any
+    outer: Any
     first: Any
-    first_bias: Any
+    first_b: Any
     second: Any
-    second_bias: Any
+    second_b: Any
     table: Any
 
 
-def forward(rows, length, w, synth, dense):
-    slots, d = rows.shape
-    n1, r1 = norm_parts(rows)
-    a = half(n1 * w.ln1_gain + w.ln1_bias)
-    v = half(mm(a, w.value_weight) + w.value_bias)
+def whole(shape, *at):
+    at = tuple(at)
+    block = (1,) * len(at) + tuple(shape[len(at) :])
+    return pl.BlockSpec(block, lambda i: at + (0,) * (len(shape) - len(at)), pipeline_mode=pl.Buffered(1))
+
+
+def whole_out(shape, *at):
+    at = tuple(at)
+    block = (1,) * len(at) + tuple(shape[len(at) :])
+    return pl.BlockSpec(block, lambda i: at + (0,) * (len(shape) - len(at)))
+
+
+class Saved(NamedTuple):
+    a: Any
+    v: Any
+    probs: Any
+    c: Any
+    hid: Any
+    b: Any
+    q: Any
+    slope: Any
+    p: Any = None
+    first_slope: Any = None
+
+
+def sizes_of(x, w):
+    rows, width = x.shape
+    parts = w.inner.shape[2] // 512
+    return rows, width, HEADS // 2, parts, w.inner.shape[2] // parts
+
+
+def forward(x, length, w, layer):
+    dense = layer == 0
+    rows, width, pairs, parts, part = sizes_of(x, w)
+    slots = rows
+
+    def pair(i):
+        return jnp.minimum(i, pairs - 1)
+
+    def piece(i):
+        return jnp.maximum(i - pairs, 0)
+
+    ins = [length, x, w.vectors, w.value, w.out]
+    specs = [pl.BlockSpec(memory_space=pltpu.SMEM), whole(x.shape), whole(w.vectors.shape, layer)]
+    specs += [whole(w.value.shape, layer), whole(w.out.shape, layer)]
     if dense:
-        f = mm(a, synth.first) + synth.first_bias
-        p = half(gelu(f))
-        logits = mm(p, synth.second) + synth.second_bias
-        logits = logits.reshape(slots, HEADS, slots).transpose(1, 0, 2)
+        ins += [w.first, w.first_b, w.second, w.second_b]
+        specs += [
+            whole(w.first.shape),
+            whole(w.first_b.shape),
+            pl.BlockSpec((width, 2 * slots), lambda i: (0, pair(i))),
+            pl.BlockSpec((1, 2 * slots), lambda i: (0, pair(i))),
+        ]
     else:
-        f = p = None
-        logits = wide(synth.table).reshape(HEADS, slots, slots)
-    probs = half(softmax(logits, length))
-    heads = v.reshape(slots, HEADS, d // HEADS)
-    mixed = jnp.einsum("hqk,khd->qhd", probs, heads, preferred_element_type=jnp.float32)
-    c = half(mixed.reshape(slots, d))
-    hid = rows + mm(c, w.out_weight) + w.out_bias
-    n2, r2 = norm_parts(hid)
-    b = half(n2 * w.ln2_gain + w.ln2_bias)
-    z = mm(b, w.ffn_in) + w.ffn_in_bias
-    q = half(gelu(z))
-    y = hid + mm(q, w.ffn_out) + w.ffn_out_bias
-    return half(y), (n1, r1, a, f, p, probs, v, c, n2, r2, b, half(gelu_slope(z)), q)
-
-
-def backward(g, saved, w, synth, dense):
-    n1, r1, a, f, p, probs, v, c, n2, r2, b, slope, q = saved
-    slots, d = g.shape
-    gy = half(g)
-    gz = half(mm_nt(gy, w.ffn_out) * slope)
-    part, g_gain2, g_bias2 = norm_back(mm_nt(gz, w.ffn_in), n2, r2, w.ln2_gain)
-    ghid = wide(g) + part
-    gatt = half(ghid)
-    gc = half(mm_nt(gatt, w.out_weight)).reshape(slots, HEADS, d // HEADS)
-    heads = v.reshape(slots, HEADS, d // HEADS)
-    dprobs = jnp.einsum("qhd,khd->hqk", gc, heads, preferred_element_type=jnp.float32)
-    gv = half(
-        jnp.einsum("hqk,qhd->khd", probs, gc, preferred_element_type=jnp.float32).reshape(slots, d)
-    )
-    probs = wide(probs)
-    dlogits = probs * (dprobs - jnp.sum(probs * dprobs, axis=2, keepdims=True))
-    ga = mm_nt(gv, w.value_weight)
+        ins += [w.table]
+        specs += [pl.BlockSpec((2 * slots, slots), lambda i: (pair(i), 0))]
+    ins += [w.inner, w.inner_b, w.outer]
+    specs += [
+        pl.BlockSpec((1, width, part), lambda i: (layer, 0, piece(i))),
+        pl.BlockSpec((1, 1, part), lambda i: (layer, 0, piece(i))),
+        pl.BlockSpec((1, part, width), lambda i: (layer, piece(i), 0)),
+    ]
+    wide_half = jax.ShapeDtypeStruct((rows, width), jnp.bfloat16)
+    hidden = jax.ShapeDtypeStruct((rows, part * parts), jnp.bfloat16)
+    outs = [wide_half] * 3 + [jax.ShapeDtypeStruct((2 * pairs, rows, slots), jnp.bfloat16), wide_half]
+    outs += [jax.ShapeDtypeStruct((rows, width), jnp.float32), wide_half, hidden, hidden]
+    row_block = whole_out((rows, width))
+    hidden_block = pl.BlockSpec((rows, part), lambda i: (0, piece(i)))
+    out_specs = [row_block] * 3 + [pl.BlockSpec((2, rows, slots), lambda i: (pair(i), 0, 0))]
+    out_specs += [row_block] * 3 + [hidden_block] * 2
     if dense:
-        gb = half(dlogits.transpose(1, 0, 2).reshape(slots, HEADS * slots))
-        gf = half(mm_nt(gb, synth.second) * gelu_slope(f))
-        ga = ga + mm_nt(gf, synth.first)
-        g_synth = Synth(mm_tn(a, gf), sums(gf), mm_tn(p, gb), sums(gb), None)
+        outs += [wide_half] * 2
+        out_specs += [row_block] * 2
+    y, *saved = pl.pallas_call(
+        functools.partial(forward_kernel, dense, pairs, parts),
+        grid=(pairs + parts,),
+        out_shape=outs,
+        in_specs=specs,
+        out_specs=out_specs,
+        scratch_shapes=[pltpu.VMEM((rows, width), jnp.float32)],
+        compiler_params=pltpu.CompilerParams(vmem_limit_bytes=56 * 2**20),
+        name=f"forward_{layer}",
+    )(*ins)
+    return y, Saved(*saved)
+
+
+def backward(g, x, saved, w, layer, before):
+    dense = layer == 0
+    rows, width, pairs, parts, part = sizes_of(x, w)
+    slots = rows
+
+    def pair(i):
+        return jnp.maximum(i - parts, 0)
+
+    def piece(i):
+        return jnp.minimum(i, parts - 1)
+
+    hidden_block = pl.BlockSpec((rows, part), lambda i: (0, piece(i)))
+    ins = [g, x, saved.hid, saved.b, saved.c, saved.a, saved.v, saved.q, saved.slope, saved.probs, w.vectors]
+    specs = [whole((rows, width))] * 7 + [hidden_block] * 2
+    specs += [pl.BlockSpec((2, rows, slots), lambda i: (pair(i), 0, 0)), whole(w.vectors.shape, layer)]
+    ins += [w.inner, w.outer, w.out, w.value]
+    inner_block = pl.BlockSpec((1, width, part), lambda i: (layer, 0, piece(i)))
+    outer_block = pl.BlockSpec((1, part, width), lambda i: (layer, piece(i), 0))
+    specs += [inner_block, outer_block, whole(w.out.shape, layer), whole(w.value.shape, layer)]
+    second_block = pl.BlockSpec((width, 2 * slots), lambda i: (0, pair(i)))
+    if dense:
+        ins += [saved.p, saved.first_slope, w.first, w.second]
+        specs += [whole((rows, width))] * 2 + [whole(w.first.shape), second_block]
+    aliases = {}
+    if before is not None:
+        aliases = {len(ins) + j: 1 + j for j in range(6)}
+        ins += list(before)
+        specs += [pl.BlockSpec(memory_space=pl.ANY)] * 6
+
+    def like(shape, dtype=jnp.bfloat16):
+        return jax.ShapeDtypeStruct(shape, dtype)
+
+    outs = [like((rows, width)), like(w.outer.shape), like(w.inner.shape), like(w.out.shape), like(w.value.shape)]
+    outs += [like((2, 8, width), jnp.float32), like(w.inner_b.shape, jnp.float32)]
+    out_specs = [whole_out((rows, width)), outer_block, inner_block]
+    out_specs += [whole_out(w.out.shape, layer), whole_out(w.value.shape, layer), whole_out((2, 8, width), layer)]
+    out_specs += [pl.BlockSpec((1, 1, part), lambda i: (layer, 0, piece(i)))]
+    if dense:
+        outs += [like(w.first.shape), like(w.second.shape), like(w.second_b.shape, jnp.float32)]
+        out_specs += [whole_out(w.first.shape), second_block, pl.BlockSpec((1, 2 * slots), lambda i: (0, pair(i)))]
     else:
-        g_synth = Synth(None, None, None, None, dlogits.reshape(HEADS * slots, slots))
-    part, g_gain1, g_bias1 = norm_back(ga, n1, r1, w.ln1_gain)
-    g_layer = Layer(
-        g_gain1,
-        g_bias1,
-        mm_tn(a, gv),
-        sums(gv),
-        mm_tn(c, gatt),
-        sums(gatt),
-        g_gain2,
-        g_bias2,
-        mm_tn(b, gz),
-        sums(gz),
-        mm_tn(q, gy),
-        sums(gy),
-    )
-    return half(ghid + part), g_layer, g_synth
-
-
-def is_matrix(k):
-    return k < 12 and k in (2, 4, 8, 10) or k in (12, 14, 16)
+        outs += [like(w.table.shape)]
+        out_specs += [pl.BlockSpec((2 * slots, slots), lambda i: (pair(i), 0))]
+    gx, *grads = pl.pallas_call(
+        functools.partial(backward_kernel, dense, layer, pairs, parts),
+        grid=(pairs + parts,),
+        out_shape=outs,
+        in_specs=specs,
+        out_specs=out_specs,
+        scratch_shapes=[
+            pltpu.VMEM((rows, width), jnp.float32),
+            pltpu.VMEM((rows, width), jnp.float32),
+            pltpu.VMEM((rows, width), jnp.bfloat16),
+            pltpu.VMEM((rows, width), jnp.bfloat16),
+            pltpu.VMEM((rows, width), jnp.bfloat16),
+            pltpu.VMEM((2, rows, slots), jnp.bfloat16),
+        ],
+        input_output_aliases=aliases,
+        compiler_params=pltpu.CompilerParams(vmem_limit_bytes=60 * 2**20),
+        name=f"backward_{layer}",
+    )(*ins)
+    return gx, grads[:6], grads[6:]
 
 
 MATRICES = (2, 8, 10, 14, 16, 4, 12)
-VECTORS = tuple(k for k in range(17) if not is_matrix(k))
+ROW_VECTORS = (0, 1, 3, 5, 6, 7, 11)
+VECTORS = ROW_VECTORS + (9, 13, 15)
 ORDERS = ("zxy", "zxy", "xzy", "yzx", "yzx", "zxy", "yzx", "xzy")
 SUM_ORDERS = tuple(o[::-1] for o in ORDERS)
 
@@ -493,14 +784,13 @@
 def per_device(mesh, boundary, lengths, *parts):
     nx, ndp = mesh.shape["segment"], mesh.shape["dp"]
     devices = nx * ndp
-    s = lax.axis_index("segment")
-    first = s == 0
+    first = lax.axis_index("segment") == 0
     swap = [(0, 1), (1, 0)]
     own = boundary[0, :, 0]
     received = lax.ppermute(jnp.where(first, own[1], own[0]), "segment", swap)
     rows = jnp.where(first, own[0], received)
     cotangent = jnp.where(first, received, own[1])
-    length = jnp.where(first, lengths[0, 0], lengths[1, 0])
+    length = jnp.where(first, lengths[0], lengths[1])
 
     flat = jnp.concatenate([parts[k].reshape(-1) for k in VECTORS])
     sizes = [parts[k].size for k in VECTORS]
@@ -513,18 +803,30 @@
     for k, g in zip(MATRICES, gathered):
         full[k] = g.reshape((nx, ndp * g.shape[1]) + g.shape[2:]) if k < 12 else g.reshape(-1, g.shape[2])
     vec = wide(gathered[-1].reshape(devices, lanes * 128))
-    at = 0
-    for k, size in zip(VECTORS, sizes):
-        piece = vec[:, at : at + size]
-        at += size
-        full[k] = piece.reshape(nx, ndp * size) if k < 12 else piece.reshape(devices * size)
-    layers = [Layer(*[full[k][j] for k in range(12)]) for j in range(2)]
-    synth = Synth(*[full[k] for k in range(12, 17)])
-
-    out0, saved0 = forward(wide(rows), length, layers[0], synth, True)
-    out1, saved1 = forward(wide(out0), length, layers[1], synth, False)
-    gin1, layer1, synth1 = backward(cotangent, saved1, layers[1], synth, False)
-    gin0, layer0, synth0 = backward(gin1, saved0, layers[0], synth, True)
+    count, size = len(ROW_VECTORS), sizes[0]
+    bounds = [count * size]
+    for k in VECTORS[count:]:
+        bounds.append(bounds[-1] + parts[k].size)
+    vectors = vec[:, : bounds[0]].reshape(nx, ndp, count, size).transpose(0, 2, 1, 3).reshape(nx, count, -1)
+    inner_b, first_b, second_b = (vec[:, lo:hi] for lo, hi in zip(bounds, bounds[1:]))
+    w = Weights(
+        vectors,
+        full[2],
+        full[4],
+        full[8],
+        inner_b.reshape(nx, 1, -1),
+        full[10],
+        full[12],
+        first_b.reshape(1, -1),
+        full[14],
+        second_b.reshape(1, -1),
+        full[16],
+    )
+
+    out0, saved0 = forward(rows, length, w, 0)
+    out1, saved1 = forward(out0, length, w, 1)
+    gin1, both, synth1 = backward(cotangent, out0, saved1, w, 1, None)
+    gin0, both, synth0 = backward(gin1, rows, saved0, w, 0, both)
 
     def swapped(for_first, for_second):
         got = lax.ppermute(jnp.where(first, for_second, for_first), "segment", swap)
@@ -533,10 +835,13 @@
     layer_outputs = swapped(out0, out1)
     input_grads = swapped(gin0, gin1)
 
-    grads = [jnp.stack([half(g0), half(g1)]) if is_matrix(k) else jnp.stack([g0, g1]) for k, (g0, g1) in enumerate(zip(layer0, layer1))]
-    grads += list(synth0[:4]) + [synth1.table]
-    lists = [half(grads[k]).reshape((devices,) + parts[k].shape[-2:]) for k in MATRICES]
-    vec = jnp.concatenate([grads[k].reshape(devices, -1) for k in VECTORS], axis=1)
+    g_outer, g_inner, g_out, g_value, g_vec, g_inner_b = both
+    g_first, g_second, g_second_b = synth0
+    matrices = (g_value, g_inner, g_outer, g_second, synth1[0], g_out, g_first)
+    lists = [g.reshape((devices,) + parts[k].shape[-2:]) for k, g in zip(MATRICES, matrices)]
+    vec = [g_vec[:, :count].reshape(nx, count, ndp, size).transpose(0, 2, 1, 3).reshape(devices, count * size)]
+    vec += [g.reshape(devices, -1) for g in (g_inner_b, g_vec[0, FIRST_B], g_second_b)]
+    vec = jnp.concatenate(vec, axis=1)
     vec = jnp.pad(vec, ((0, 0), (0, lanes * 128 - vec.shape[1]))).reshape(devices, lanes, 128)
     summed = scatter_all(lists + [vec], SUM_ORDERS, mesh)
     result = {k: g.reshape(parts[k].shape) for k, g in zip(MATRICES, summed)}

time: 751 us -> 618 us (0.82)
  Pallas kernels: 410 us -> 570 us
  matrix products: 157 us -> 0 us
  local copies, waits for them, and re-layouts: 89.1 us -> 20.3 us
  other arithmetic: 81.4 us -> 18.3 us
    pallas_call x0 -> x4, Pallas kernels: none -> 161 us  [the longest x2 92.2 us: backward(): pl.pallas_call(functools.partial(backward_kernel, dense, layer, pairs, pa...]
    dot_general x35 -> x0, matrix products: 146 us -> none  [the longest x10 44.6 us: mm_nt(): lax.dot_general(left, right, (((1,), (1,)), ((), ())), preferred_element_...]
    add x15 -> x0, local copies, waits for them, and re-layouts: 21.9 us -> none  [the longest x2 13.3 us: forward(): logits = mm(p, synth.second) + synth.second_bias]
    another operation x15 -> x3, other arithmetic: 21.3 us -> 0.03 us  [the longest x4 21.2 us: per_device(): jnp.stack([half(g0), half(g1)])]
    reduce_sum x10 -> x0, other arithmetic: 19.5 us -> none  [the longest x5 14.4 us: sums(): return jnp.sum(wide(value), axis=0)]
    slice x9 -> x6, local copies, waits for them, and re-layouts: 21.5 us -> 2.12 us  [the longest x1 1.31 us: per_device(): length = jnp.where(first, lengths[0], lengths[1])]
    convert_element_type x6 -> x1, local copies, waits for them, and re-layouts: 14.5 us -> 0.6 us  [half(): return value.astype(jnp.bfloat16)]
    convert_element_type x8 -> x6, other arithmetic: 18.5 us -> 6.26 us  [half(): return value.astype(jnp.bfloat16)]
  transfers between devices with their start and end apart: 3 -> 3, of which waited for: 0 -> 0; matrix products, arithmetic and copies ran while one was open for 14% -> 4% of each run, Pallas kernels for 55% -> 81%
where the time goes in v2:
time: 618 us; the launch traced here: 617 us
  Pallas kernels  570 us (92%)
  local copies, waits for them, and re-layouts  20.3 us (3%)
  other arithmetic  18.3 us (3%)
    pallas_call x1, Pallas kernels, gather_all(): pl.pallas_call(functools.partial(gather_kernel, orders, nz), out_shape=[j...  205 us
    pallas_call x1, Pallas kernels, scatter_all(): pl.pallas_call(functools.partial(scatter_kernel, orders, nz), out_shape=[...  204 us
    pallas_call x2, Pallas kernels, backward(): pl.pallas_call(functools.partial(backward_kernel, dense, layer, pairs, pa...  92.2 us
    pallas_call x2, Pallas kernels, forward(): pl.pallas_call(functools.partial(forward_kernel, dense, pairs, parts), gr...  69.2 us
  transfers between devices with their start and end apart: 3, of which 0 were waited for; matrix products, arithmetic and copies ran while one was open for 4% of the time, Pallas kernels for 81%

profile of v2, /device:TPU:0, one launch (start us, length us, event | category | flops | bytes accessed | tf_op | source)
XLA Modules:
  0.0 617.4 jit_solution(4331083699093733440)
XLA Ops:
  0.8 1.6 bitcast_select_fusion.1
  2.4 3.0 collective-permute-start
  5.4 0.7 convert_bitcast_fusion.1.refs_1_
  6.1 0.7 convert_element_type.48.refs_3_
  6.9 0.7 convert_element_type.49.refs_4_
  7.6 0.6 convert_element_type.52.refs_6_
  8.4 0.1 concatenate.7
  8.5 0.6 pad_bitcast_fusion.refs_7_
  9.1 1.6 convert_bitcast_fusion.2
  10.7 1.8 convert_bitcast_fusion.refs_2_
  12.5 204.9 %gather_weights.1 = (bf16[2,4,2,2,48,768]{5,4,3,2,1,0:T(8,128)(2,1)}, bf16[2,4,2,2,48,3072]{5,4,3,2,1,0:T(8,128)(2,1)}, bf16[2,4,2,2,192,768]{5,4,3,2,1,0:T(8,12...) custom-call(bf16[48,768]{1,0:T(8,128)(2,1)} %get-tuple-element.191.r, ...), custom_call_target="tpu_custom_call" | custom-call | tf_op jit(solution)/shard_map/gather_weights/pallas_call | solution.py:188
  217.4 0.9 copy.61
  218.3 0.6 slice.84
  219.0 0.9 reshape.161
  219.9 0.7 copy.56
  220.6 1.6 reshape.184.vec_ref.refs_10_
  222.2 0.7 reshape.163.refs_1_
  223.0 0.7 reshape.164.refs_3_
  223.7 0.7 reshape.165.refs_5_.refs_2_
  224.4 1.3 fusion.3
  227.0 1.3 bitcast_select_fusion
  228.3 40.0 %forward_0.1 = (bf16[512,768]{1,0:T(8,128)(2,1)}, bf16[512,768]{1,0:T(8,128)(2,1)}, bf16[512,768]{1,0:T(8,128)(2,1)}, bf16[12,512,512]{2,1,0:T(8,128)(2,1)}, bf1...) custom-call(s32[1]{0:T(128)S(6)} %select_n.50.length_ref, ...), custom_call_target="tpu_custom_call" | custom-call | tf_op jit(solution)/shard_map/forward_0/pallas_call | solution.py:700
  268.3 29.2 %forward_1.1 = (bf16[512,768]{1,0:T(8,128)(2,1)}, bf16[512,768]{1,0:T(8,128)(2,1)}, bf16[512,768]{1,0:T(8,128)(2,1)}, bf16[12,512,512]{2,1,0:T(8,128)(2,1)}, bf1...) custom-call(s32[1]{0:T(128)S(6)} %select_n.50.length_ref, ...), custom_call_target="tpu_custom_call" | custom-call | tf_op jit(solution)/shard_map/forward_1/pallas_call | solution.py:700
  297.6 2.1 broadcast_select_fusion.1
  299.7 38.0 %backward_1.1 = (bf16[512,768]{1,0:T(8,128)(2,1)}, bf16[2,3072,768]{2,1,0:T(8,128)(2,1)}, bf16[2,768,3072]{2,1,0:T(8,128)(2,1)}, bf16[2,768,768]{2,1,0:T(8,128)(...) custom-call(bf16[512,768]{1,0:T(8,128)(2,1)} %get-tuple-element.165., ...), custom_call_target="tpu_custom_call" | custom-call | tf_op jit(solution)/shard_map/backward_1/pallas_call | solution.py:756
  337.7 54.2 %backward_0.1 = (bf16[512,768]{1,0:T(8,128)(2,1)}, bf16[2,3072,768]{2,1,0:T(8,128)(2,1)}, bf16[2,768,3072]{2,1,0:T(8,128)(2,1)}, bf16[2,768,768]{2,1,0:T(8,128)(...) custom-call(bf16[512,768]{1,0:T(8,128)(2,1)} %get-tuple-element.91.r, ...), custom_call_target="tpu_custom_call", output_to_operand_aliasing={{1}: (19, {}), {2}: (20, {}), {3}: (21, {}), {4}: (22, {}),... | custom-call | tf_op jit(solution)/shard_map/backward_0/pallas_call | solution.py:756
  391.9 1.0 broadcast_select_fusion
  392.9 3.1 collective-permute-start.2
  396.1 0.5 broadcast.20
  396.6 0.7 reduce.8
  397.7 0.1 reshape.166
  398.0 0.1 fusion
  398.1 0.8 copy.59
  398.8 203.9 %sum_gradients.1 = (f32[48,768]{1,0:T(8,128)}, f32[48,3072]{1,0:T(8,128)}, f32[192,768]{1,0:T(8,128)}, f32[24,6144]{1,0:T(8,128)}, f32[192,512]{1,0:T(8,128)}, /...) custom-call(bf16[2,4,2,2,48,768]{5,4,3,2,1,0:T(8,128)(2,1)} %bitcast.121, ...), custom_call_target="tpu_custom_call" | custom-call | tf_op jit(solution)/shard_map/sum_gradients/pallas_call | solution.py:336
  602.7 1.4 fusion.2
  604.1 1.3 slice.96
  605.4 1.5 slice_bitcast_fusion
  606.9 1.3 select_bitcast_fusion.3
  608.2 1.3 maximum_bitcast_fusion
  609.5 1.3 select_bitcast_fusion.1
  610.9 1.3 maximum_bitcast_fusion.1
  612.2 0.7 copy.75
  612.9 0.7 copy.76
  613.5 0.8 copy.77
  614.3 0.8 copy.78
  615.2 0.6 copy.79
  615.8 0.8 copy.80
  616.6 0.7 copy.81
  (79 shorter events, 0.9 us)
Async XLA Ops:
  0.7 4.7 copy-start.5
  0.7 5.4 copy-start.6
  0.7 6.2 %copy-start.10 = (f32[192,512]{1,0:T(8,128)S(1)}, f32[192,512]{1,0:T(8,128)}, u32[]{:S(2)}) copy-start(f32[192,512]{1,0:T(8,128)} %param.37) | copy-start | bytes 1179652
  0.7 6.9 %copy-start.16 = (f32[24,768]{1,0:T(8,128)S(1)}, f32[24,768]{1,0:T(8,128)}, u32[]{:S(2)}) copy-start(f32[24,768]{1,0:T(8,128)} %param.33) | copy-start | bytes 221188
  0.7 7.5 %copy-start.27 = (f32[1,48]{1,0:T(1,128)S(1)}, f32[1,48]{1,0:T(1,128)}, u32[]{:S(2)}) copy-start(f32[1,48]{1,0:T(1,128)} %param.21) | copy-start | bytes 580
  0.7 7.5 %copy-start.25 = (f32[1,192]{1,0:T(1,128)S(1)}, f32[1,192]{1,0:T(1,128)}, u32[]{:S(2)}) copy-start(f32[1,192]{1,0:T(1,128)} %param.30) | copy-start | bytes 2308
  0.7 7.5 %copy-start.28 = (f32[24]{0:T(128)S(1)}, f32[24]{0:T(128)}, u32[]{:S(2)}) copy-start(f32[24]{0:T(128)} %param.34) | copy-start | bytes 292
  0.7 7.5 %copy-start.26 = (f32[192]{0:T(256)S(1)}, f32[192]{0:T(256)}, u32[]{:S(2)}) copy-start(f32[192]{0:T(256)} %param.36) | copy-start | bytes 2308
  0.7 7.5 %copy-start.19 = (f32[1,48]{1,0:T(1,128)S(1)}, f32[1,48]{1,0:T(1,128)}, u32[]{:S(2)}) copy-start(f32[1,48]{1,0:T(1,128)} %param.24) | copy-start | bytes 580
  0.8 7.5 %copy-start.20 = (f32[1,48]{1,0:T(1,128)S(1)}, f32[1,48]{1,0:T(1,128)}, u32[]{:S(2)}) copy-start(f32[1,48]{1,0:T(1,128)} %param.22) | copy-start | bytes 580
  0.8 7.5 %copy-start.21 = (f32[1,48]{1,0:T(1,128)S(1)}, f32[1,48]{1,0:T(1,128)}, u32[]{:S(2)}) copy-start(f32[1,48]{1,0:T(1,128)} %param.27) | copy-start | bytes 580
  0.8 7.5 %copy-start.22 = (f32[1,48]{1,0:T(1,128)S(1)}, f32[1,48]{1,0:T(1,128)}, u32[]{:S(2)}) copy-start(f32[1,48]{1,0:T(1,128)} %param.26) | copy-start | bytes 580
  0.8 7.5 %copy-start.23 = (f32[1,48]{1,0:T(1,128)S(1)}, f32[1,48]{1,0:T(1,128)}, u32[]{:S(2)}) copy-start(f32[1,48]{1,0:T(1,128)} %param.32) | copy-start | bytes 580
  0.8 7.5 %copy-start.24 = (f32[1,48]{1,0:T(1,128)S(1)}, f32[1,48]{1,0:T(1,128)}, u32[]{:S(2)}) copy-start(f32[1,48]{1,0:T(1,128)} %param.28) | copy-start | bytes 580
  2.4 224.6 %collective-permute-start = (bf16[512,768]{1,0:T(8,128)(2,1)S(1)}, bf16[512,768]{1,0:T(8,128)(2,1)S(1)}, u32[]{:S(2)}, u32[]{:S(2)}) collective-permute-start(bf16[512,768]{1,0:T(8,128)(2,1)S(1)} %bitcast_select_fusion.1), channel_id=1, source_target_pairs={{0,16},{16,0},{1,17},{17,1},{2,18},{18,2},{3,19},{19,3},{4,20},{20... | collective-permute-start | bytes 2359304 | tf_op jit(solution)/shard_map/ppermute | solution.py:790
  6.9 220.1 %copy-start.3 = (bf16[1,2,1,512,768]{4,3,2,1,0:T(8,128)(2,1)S(1)}, bf16[1,2,1,512,768]{4,3,2,1,0:T(8,128)(2,1)}, u32[]{:S(2)}) copy-start(bf16[1,2,1,512,768]{4,3,2,1,0:T(8,128)(2,1)} %param.19) | copy-start | bytes 4718596
  268.3 29.3 %copy-start = (bf16[512,768]{1,0:T(8,128)(2,1)S(1)}, bf16[512,768]{1,0:T(8,128)(2,1)}, u32[]{:S(2)}) copy-start(bf16[512,768]{1,0:T(8,128)(2,1)} %get-tuple-element.80.x_ref.refs_1_) | copy-start | bytes 2359300
  299.7 307.2 %collective-permute-start.1 = (bf16[512,768]{1,0:T(8,128)(2,1)}, bf16[512,768]{1,0:T(8,128)(2,1)}, u32[]{:S(2)}, u32[]{:S(2)}) collective-permute-start(bf16[512,768]{1,0:T(8,128)(2,1)} %broadcast_select_fusion.1), channel_id=1, source_target_pairs={{0,16},{16,0},{1,17},{17,1},{2,18},{18,2},{3,19},{19,3},{4,20},{20... | collective-permute-start | bytes 2359304 | tf_op jit(solution)/shard_map/ppermute | solution.py:832
  337.7 54.3 %copy-start.2 = (bf16[512,768]{1,0:T(8,128)(2,1)S(1)}, bf16[512,768]{1,0:T(8,128)(2,1)}, u32[]{:S(2)}) copy-start(bf16[512,768]{1,0:T(8,128)(2,1)} %get-tuple-element.91.refs_0_) | copy-start | bytes 2359300
  391.9 4.7 copy-start.18
  391.9 5.5 copy-start.12
  391.9 5.6 copy-start.15
  392.9 216.6 %collective-permute-start.2 = (bf16[512,768]{1,0:T(8,128)(2,1)}, bf16[512,768]{1,0:T(8,128)(2,1)}, u32[]{:S(2)}, u32[]{:S(2)}) collective-permute-start(bf16[512,768]{1,0:T(8,128)(2,1)} %broadcast_select_fusion), channel_id=1, source_target_pairs={{0,16},{16,0},{1,17},{17,1},{2,18},{18,2},{3,19},{19,3},{4,20},{20... | collective-permute-start | bytes 2359304 | tf_op jit(solution)/shard_map/ppermute | solution.py:832
  398.8 208.1 %copy-start.1 = (bf16[512,768]{1,0:T(8,128)(2,1)S(1)}, bf16[512,768]{1,0:T(8,128)(2,1)}, u32[]{:S(2)}) copy-start(bf16[512,768]{1,0:T(8,128)(2,1)} %get-tuple-element.80.x_ref.refs_1_) | copy-start | bytes 2359300
  608.2 1.3 copy-start.4
  610.8 1.3 copy-start.14
  610.9 2.0 copy-start.13
  610.9 2.7 copy-start.9
  610.9 3.5 copy-start.8
  610.9 4.3 copy-start.17
  610.9 4.9 copy-start.7
  612.2 4.4 copy-start.11

commit v3 on v2

--- a/solution.py
+++ b/solution.py
@@ -86,7 +86,8 @@
     return ref.at[xs, z, ys, c]
 
 
-def gather_kernel(orders, nz, *refs):
+def gather_kernel(plan, nz, *refs):
+    orders, starts = zip(*plan)
     n = len(orders)
     ins, outs = refs[:n], refs[n : 2 * n]
     send, recv, local = refs[2 * n :]
@@ -167,10 +168,10 @@
                 mine["d", t - 1] = put(i, 4 * nz + t - 1, block, block, place.other("c"))
 
     stages = nz + 2
-    for t in range(stages + n - 1):
+    for t in range(stages + max(starts)):
         for i in range(n):
-            if 0 <= t - i < stages:
-                stage(i, t - i)
+            if 0 <= t - starts[i] < stages:
+                stage(i, t - starts[i])
     for mine in copies:
         for key, copy in mine.items():
             if key[0] in "cd":
@@ -179,14 +180,14 @@
         copy.wait_send()
 
 
-def gather_all(shards, orders, mesh):
+def gather_all(shards, plan, mesh):
     nx, ndp = mesh.shape["segment"], mesh.shape["dp"]
     if nx != 2 or ndp % 8:
         return [lax.all_gather(s, AXES, axis=0) for s in shards]
     nz, n = ndp // 4, len(shards)
     slots = 5 * nz + 2
     outs = pl.pallas_call(
-        functools.partial(gather_kernel, orders, nz),
+        functools.partial(gather_kernel, plan, nz),
         out_shape=[jax.ShapeDtypeStruct((2, nz, 2, 2) + s.shape, s.dtype) for s in shards],
         in_specs=[pl.BlockSpec(memory_space=pl.ANY)] * n,
         out_specs=[pl.BlockSpec(memory_space=pl.ANY)] * n,
@@ -216,7 +217,8 @@
         dst[...] = dst[...] + src[...]
 
 
-def scatter_kernel(orders, nz, *refs):
+def scatter_kernel(plan, nz, *refs):
+    orders, starts = zip(*plan)
     n = len(orders)
     ins, outs = refs[:n], refs[n : 2 * n]
     accs, stages, firsts, rings, lasts = (refs[(2 + j) * n : (3 + j) * n] for j in range(5))
@@ -315,26 +317,26 @@
                         outs[i][...] = wide(ring[t - 1]) + wide(part(nz, 0, 0)[...])
 
     stages_of = nz + 3
-    for t in range(stages_of + n - 1):
+    for t in range(stages_of + max(starts)):
         for i in range(n):
-            if 0 <= t - i < stages_of:
-                stage(i, t - i)
+            if 0 <= t - starts[i] < stages_of:
+                stage(i, t - starts[i])
     for copy in started:
         copy.wait_send()
 
 
-def scatter_all(grads, orders, mesh):
+def scatter_all(grads, plan, mesh):
     nx, ndp = mesh.shape["segment"], mesh.shape["dp"]
     if nx != 2 or ndp != 16:
         return [wide(lax.psum_scatter(g, AXES, scatter_dimension=0, tiled=False)) for g in grads]
     nz, n = ndp // 4, len(grads)
 
     def scratch(lead):
-        return [pltpu.VMEM(lead(o) + g.shape[1:], g.dtype) for o, g in zip(orders, grads)]
+        return [pltpu.VMEM(lead(o) + g.shape[1:], g.dtype) for (o, _), g in zip(plan, grads)]
 
     slots = 4 * nz + 2
     return pl.pallas_call(
-        functools.partial(scatter_kernel, orders, nz),
+        functools.partial(scatter_kernel, plan, nz),
         out_shape=[jax.ShapeDtypeStruct(g.shape[1:], jnp.float32) for g in grads],
         in_specs=[pl.BlockSpec(memory_space=pl.ANY)] * n,
         out_specs=[pl.BlockSpec(memory_space=pltpu.VMEM)] * n,
@@ -774,11 +776,35 @@
     return gx, grads[:6], grads[6:]
 
 
-MATRICES = (2, 8, 10, 14, 16, 4, 12)
 ROW_VECTORS = (0, 1, 3, 5, 6, 7, 11)
 VECTORS = ROW_VECTORS + (9, 13, 15)
-ORDERS = ("zxy", "zxy", "xzy", "yzx", "yzx", "zxy", "yzx", "xzy")
-SUM_ORDERS = tuple(o[::-1] for o in ORDERS)
+MATRICES = (2, 4, 8, 10, 12, 14, 16)
+SMALL = 17
+GATHER = (
+    (16, "zxy", 0),
+    (SMALL, "xzy", 0),
+    (8, "zyx", 0),
+    (12, "zxy", 0),
+    (14, "yzx", 0),
+    (2, "zyx", 1),
+    (4, "xzy", 1),
+    (10, "xzy", 0),
+)
+SUM = (
+    (16, "yzx", 0),
+    (8, "xzy", 0),
+    (12, "yzx", 0),
+    (14, "yxz", 0),
+    (SMALL, "xyz", 1),
+    (2, "yzx", 2),
+    (4, "yzx", 1),
+    (10, "xyz", 1),
+)
+
+
+def planned(call, plan, arrays, mesh):
+    got = call([arrays[k] for k, _, _ in plan], [entry[1:] for entry in plan], mesh)
+    return {k: g for (k, _, _), g in zip(plan, got)}
 
 
 def per_device(mesh, boundary, lengths, *parts):
@@ -796,13 +822,13 @@
     sizes = [parts[k].size for k in VECTORS]
     lanes = -(-flat.size // 2048) * 16
     packed = half(jnp.pad(flat, (0, lanes * 128 - flat.size)).reshape(lanes, 128))
-    shards = [half(parts[k].reshape(parts[k].shape[-2:])) for k in MATRICES] + [packed]
-    gathered = gather_all(shards, ORDERS, mesh)
-
-    full = {}
-    for k, g in zip(MATRICES, gathered):
+    shards = {k: half(parts[k].reshape(parts[k].shape[-2:])) for k in MATRICES}
+    shards[SMALL] = packed
+    full = planned(gather_all, GATHER, shards, mesh)
+    for k in MATRICES:
+        g = full[k]
         full[k] = g.reshape((nx, ndp * g.shape[1]) + g.shape[2:]) if k < 12 else g.reshape(-1, g.shape[2])
-    vec = wide(gathered[-1].reshape(devices, lanes * 128))
+    vec = wide(full[SMALL].reshape(devices, lanes * 128))
     count, size = len(ROW_VECTORS), sizes[0]
     bounds = [count * size]
     for k in VECTORS[count:]:
@@ -837,15 +863,15 @@
 
     g_outer, g_inner, g_out, g_value, g_vec, g_inner_b = both
     g_first, g_second, g_second_b = synth0
-    matrices = (g_value, g_inner, g_outer, g_second, synth1[0], g_out, g_first)
-    lists = [g.reshape((devices,) + parts[k].shape[-2:]) for k, g in zip(MATRICES, matrices)]
+    matrices = (g_value, g_out, g_inner, g_outer, g_first, g_second, synth1[0])
+    grads = {k: g.reshape((devices,) + parts[k].shape[-2:]) for k, g in zip(MATRICES, matrices)}
     vec = [g_vec[:, :count].reshape(nx, count, ndp, size).transpose(0, 2, 1, 3).reshape(devices, count * size)]
     vec += [g.reshape(devices, -1) for g in (g_inner_b, g_vec[0, FIRST_B], g_second_b)]
     vec = jnp.concatenate(vec, axis=1)
-    vec = jnp.pad(vec, ((0, 0), (0, lanes * 128 - vec.shape[1]))).reshape(devices, lanes, 128)
-    summed = scatter_all(lists + [vec], SUM_ORDERS, mesh)
-    result = {k: g.reshape(parts[k].shape) for k, g in zip(MATRICES, summed)}
-    vec = summed[-1].reshape(-1)
+    grads[SMALL] = jnp.pad(vec, ((0, 0), (0, lanes * 128 - vec.shape[1]))).reshape(devices, lanes, 128)
+    summed = planned(scatter_all, SUM, grads, mesh)
+    result = {k: summed[k].reshape(parts[k].shape) for k in MATRICES}
+    vec = summed[SMALL].reshape(-1)
     at = 0
     for k, size in zip(VECTORS, sizes):
         result[k] = vec[at : at + size].reshape(parts[k].shape)

time: 618 us -> 532 us (0.86)
  Pallas kernels: 570 us -> 484 us
    pallas_call x2, Pallas kernels: 409 us -> 322 us  [the longest x1 163 us: scatter_all(): pl.pallas_call(functools.partial(scatter_kernel, plan, nz), out_shape=[ja...]
  transfers between devices with their start and end apart: 3 -> 3, of which waited for: 0 -> 0; matrix products, arithmetic and copies ran while one was open for 4% -> 5% of each run, Pallas kernels for 81% -> 78%
where the time goes in v3:
time: 532 us; the launch traced here: 531 us
  Pallas kernels  484 us (91%)
  local copies, waits for them, and re-layouts  20.3 us (4%)
  other arithmetic  18.5 us (3%)
  starting transfers between devices  6.17 us (1%)
    pallas_call x1, Pallas kernels, scatter_all(): pl.pallas_call(functools.partial(scatter_kernel, plan, nz), out_shape=[ja...  163 us
    pallas_call x1, Pallas kernels, gather_all(): pl.pallas_call(functools.partial(gather_kernel, plan, nz), out_shape=[jax...  160 us
    pallas_call x2, Pallas kernels, backward(): pl.pallas_call(functools.partial(backward_kernel, dense, layer, pairs, pa...  92.3 us
    pallas_call x2, Pallas kernels, forward(): pl.pallas_call(functools.partial(forward_kernel, dense, pairs, parts), gr...  69.2 us
  transfers between devices with their start and end apart: 3, of which 0 were waited for; matrix products, arithmetic and copies ran while one was open for 5% of the time, Pallas kernels for 78%

profile of v3, /device:TPU:0, one launch (start us, length us, event | category | flops | bytes accessed | tf_op | source)
XLA Modules:
  0.0 531.3 jit_solution(7003282879260522799)
XLA Ops:
  0.8 1.6 bitcast_select_fusion.1
  2.4 3.0 collective-permute-start
  5.4 0.7 convert_element_type.42.refs_0_
  6.3 0.1 concatenate.7
  6.4 0.6 pad_bitcast_fusion.refs_1_
  7.0 0.7 convert_bitcast_fusion.1.refs_2_
  7.8 0.6 convert_element_type.46.refs_3_
  8.4 1.9 convert_element_type.47.refs_4_
  10.3 0.7 convert_bitcast_fusion.2
  11.0 1.8 convert_bitcast_fusion.refs_7_
  12.8 159.8 %gather_weights.1 = (bf16[2,4,2,2,192,512]{5,4,3,2,1,0:T(8,128)(2,1)}, bf16[2,4,2,2,16,128]{5,4,3,2,1,0:T(8,128)(2,1)}, bf16[2,4,2,2,48,3072]{5,4,3,2,1,0:T(8,12...) custom-call(bf16[192,512]{1,0:T(8,128)(2,1)} %convert_element_type.4, ...), custom_call_target="tpu_custom_call" | custom-call | tf_op jit(solution)/shard_map/gather_weights/pallas_call | solution.py:189
  172.6 0.9 copy.61
  173.5 0.6 slice.84
  174.2 0.9 reshape.161
  175.1 0.7 copy.56
  175.8 1.6 reshape.184.vec_ref.refs_10_
  177.4 0.7 reshape.163.refs_1_
  178.2 0.7 reshape.164.refs_3_
  178.9 0.7 reshape.165.refs_5_.refs_2_
  179.6 1.3 fusion.3
  182.2 1.3 bitcast_select_fusion
  183.5 40.0 %forward_0.1 = (bf16[512,768]{1,0:T(8,128)(2,1)}, bf16[512,768]{1,0:T(8,128)(2,1)}, bf16[512,768]{1,0:T(8,128)(2,1)}, bf16[12,512,512]{2,1,0:T(8,128)(2,1)}, bf1...) custom-call(s32[1]{0:T(128)S(6)} %select_n.50.length_ref, ...), custom_call_target="tpu_custom_call" | custom-call | tf_op jit(solution)/shard_map/forward_0/pallas_call | solution.py:702
  223.5 29.2 %forward_1.1 = (bf16[512,768]{1,0:T(8,128)(2,1)}, bf16[512,768]{1,0:T(8,128)(2,1)}, bf16[512,768]{1,0:T(8,128)(2,1)}, bf16[12,512,512]{2,1,0:T(8,128)(2,1)}, bf1...) custom-call(s32[1]{0:T(128)S(6)} %select_n.50.length_ref, ...), custom_call_target="tpu_custom_call" | custom-call | tf_op jit(solution)/shard_map/forward_1/pallas_call | solution.py:702
  252.7 2.1 broadcast_select_fusion.1
  254.8 0.4 collective-permute-start.1
  255.2 38.0 %backward_1.1 = (bf16[512,768]{1,0:T(8,128)(2,1)}, bf16[2,3072,768]{2,1,0:T(8,128)(2,1)}, bf16[2,768,3072]{2,1,0:T(8,128)(2,1)}, bf16[2,768,768]{2,1,0:T(8,128)(...) custom-call(bf16[512,768]{1,0:T(8,128)(2,1)} %get-tuple-element.165., ...), custom_call_target="tpu_custom_call" | custom-call | tf_op jit(solution)/shard_map/backward_1/pallas_call | solution.py:758
  293.2 54.3 %backward_0.1 = (bf16[512,768]{1,0:T(8,128)(2,1)}, bf16[2,3072,768]{2,1,0:T(8,128)(2,1)}, bf16[2,768,3072]{2,1,0:T(8,128)(2,1)}, bf16[2,768,768]{2,1,0:T(8,128)(...) custom-call(bf16[512,768]{1,0:T(8,128)(2,1)} %get-tuple-element.91.r, ...), custom_call_target="tpu_custom_call", output_to_operand_aliasing={{1}: (19, {}), {2}: (20, {}), {3}: (21, {}), {4}: (22, {}),... | custom-call | tf_op jit(solution)/shard_map/backward_0/pallas_call | solution.py:758
  347.6 1.0 broadcast_select_fusion
  348.6 2.8 collective-permute-start.2
  351.3 0.5 broadcast.20
  351.8 0.7 reduce.8
  352.9 0.1 reshape.166
  353.3 0.8 copy.59
  354.1 162.5 %sum_gradients.1 = (f32[192,512]{1,0:T(8,128)}, f32[48,3072]{1,0:T(8,128)}, f32[24,768]{1,0:T(8,128)}, f32[24,6144]{1,0:T(8,128)}, f32[16,128]{1,0:T(8,128)}, /*...) custom-call(bf16[2,4,2,2,192,512]{5,4,3,2,1,0:T(8,128)(2,1)} %bitcast.123, ...), custom_call_target="tpu_custom_call" | custom-call | tf_op jit(solution)/shard_map/sum_gradients/pallas_call | solution.py:338
  516.6 1.4 fusion.2
  518.0 1.3 slice.96
  519.3 1.5 slice_bitcast_fusion
  520.8 1.3 select_bitcast_fusion.3
  522.1 1.3 maximum_bitcast_fusion
  523.4 1.3 select_bitcast_fusion.1
  524.8 1.3 maximum_bitcast_fusion.1
  526.1 0.7 copy.75
  526.8 0.7 copy.76
  527.4 0.8 copy.77
  528.3 0.8 copy.78
  529.1 0.6 copy.79
  529.7 0.8 copy.80
  530.5 0.7 copy.81
  (81 shorter events, 1.0 us)
Async XLA Ops:
  0.7 4.8 copy-start.9
  0.7 5.5 %copy-start.28 = (f32[1,48]{1,0:T(1,128)S(1)}, f32[1,48]{1,0:T(1,128)}, u32[]{:S(2)}) copy-start(f32[1,48]{1,0:T(1,128)} %param.21) | copy-start | bytes 580
  0.7 5.5 %copy-start.26 = (f32[1,192]{1,0:T(1,128)S(1)}, f32[1,192]{1,0:T(1,128)}, u32[]{:S(2)}) copy-start(f32[1,192]{1,0:T(1,128)} %param.30) | copy-start | bytes 2308
  0.7 5.5 %copy-start.29 = (f32[24]{0:T(128)S(1)}, f32[24]{0:T(128)}, u32[]{:S(2)}) copy-start(f32[24]{0:T(128)} %param.34) | copy-start | bytes 292
  0.7 5.5 %copy-start.27 = (f32[192]{0:T(256)S(1)}, f32[192]{0:T(256)}, u32[]{:S(2)}) copy-start(f32[192]{0:T(256)} %param.36) | copy-start | bytes 2308
  0.7 5.5 %copy-start.20 = (f32[1,48]{1,0:T(1,128)S(1)}, f32[1,48]{1,0:T(1,128)}, u32[]{:S(2)}) copy-start(f32[1,48]{1,0:T(1,128)} %param.24) | copy-start | bytes 580
  0.7 5.5 %copy-start.21 = (f32[1,48]{1,0:T(1,128)S(1)}, f32[1,48]{1,0:T(1,128)}, u32[]{:S(2)}) copy-start(f32[1,48]{1,0:T(1,128)} %param.22) | copy-start | bytes 580
  0.7 5.5 %copy-start.22 = (f32[1,48]{1,0:T(1,128)S(1)}, f32[1,48]{1,0:T(1,128)}, u32[]{:S(2)}) copy-start(f32[1,48]{1,0:T(1,128)} %param.27) | copy-start | bytes 580
  0.7 5.5 %copy-start.23 = (f32[1,48]{1,0:T(1,128)S(1)}, f32[1,48]{1,0:T(1,128)}, u32[]{:S(2)}) copy-start(f32[1,48]{1,0:T(1,128)} %param.26) | copy-start | bytes 580
  0.8 5.5 %copy-start.24 = (f32[1,48]{1,0:T(1,128)S(1)}, f32[1,48]{1,0:T(1,128)}, u32[]{:S(2)}) copy-start(f32[1,48]{1,0:T(1,128)} %param.32) | copy-start | bytes 580
  0.8 5.5 %copy-start.25 = (f32[1,48]{1,0:T(1,128)S(1)}, f32[1,48]{1,0:T(1,128)}, u32[]{:S(2)}) copy-start(f32[1,48]{1,0:T(1,128)} %param.28) | copy-start | bytes 580
  0.8 6.2 %copy-start.5 = (f32[1,48,3072]{2,1,0:T(8,128)S(1)}, f32[1,48,3072]{2,1,0:T(8,128)}, u32[]{:S(2)}) copy-start(f32[1,48,3072]{2,1,0:T(8,128)} %param.29) | copy-start | bytes 1769476
  0.8 7.0 %copy-start.17 = (f32[24,768]{1,0:T(8,128)S(1)}, f32[24,768]{1,0:T(8,128)}, u32[]{:S(2)}) copy-start(f32[24,768]{1,0:T(8,128)} %param.33) | copy-start | bytes 221188
  0.8 9.5 %copy-start.12 = (f32[1,48,768]{2,1,0:T(8,128)S(1)}, f32[1,48,768]{2,1,0:T(8,128)}, u32[]{:S(2)}) copy-start(f32[1,48,768]{2,1,0:T(8,128)} %param.25) | copy-start | bytes 442372
  0.8 9.5 %copy-start.13 = (f32[1,48,768]{2,1,0:T(8,128)S(1)}, f32[1,48,768]{2,1,0:T(8,128)}, u32[]{:S(2)}) copy-start(f32[1,48,768]{2,1,0:T(8,128)} %param.23) | copy-start | bytes 442372
  2.4 179.8 %collective-permute-start = (bf16[512,768]{1,0:T(8,128)(2,1)S(1)}, bf16[512,768]{1,0:T(8,128)(2,1)S(1)}, u32[]{:S(2)}, u32[]{:S(2)}) collective-permute-start(bf16[512,768]{1,0:T(8,128)(2,1)S(1)} %bitcast_select_fusion.1), channel_id=1, source_target_pairs={{0,16},{16,0},{1,17},{17,1},{2,18},{18,2},{3,19},{19,3},{4,20},{20... | collective-permute-start | bytes 2359304 | tf_op jit(solution)/shard_map/ppermute | solution.py:816
  8.4 173.8 %copy-start.3 = (bf16[1,2,1,512,768]{4,3,2,1,0:T(8,128)(2,1)S(1)}, bf16[1,2,1,512,768]{4,3,2,1,0:T(8,128)(2,1)}, u32[]{:S(2)}) copy-start(bf16[1,2,1,512,768]{4,3,2,1,0:T(8,128)(2,1)} %param.19) | copy-start | bytes 4718596
  223.5 29.2 %copy-start = (bf16[512,768]{1,0:T(8,128)(2,1)S(1)}, bf16[512,768]{1,0:T(8,128)(2,1)}, u32[]{:S(2)}) copy-start(bf16[512,768]{1,0:T(8,128)(2,1)} %get-tuple-element.80.x_ref.refs_1_) | copy-start | bytes 2359300
  254.8 266.0 %collective-permute-start.1 = (bf16[512,768]{1,0:T(8,128)(2,1)}, bf16[512,768]{1,0:T(8,128)(2,1)}, u32[]{:S(2)}, u32[]{:S(2)}) collective-permute-start(bf16[512,768]{1,0:T(8,128)(2,1)} %broadcast_select_fusion.1), channel_id=1, source_target_pairs={{0,16},{16,0},{1,17},{17,1},{2,18},{18,2},{3,19},{19,3},{4,20},{20... | collective-permute-start | bytes 2359304 | tf_op jit(solution)/shard_map/ppermute | solution.py:858
  293.2 54.4 %copy-start.2 = (bf16[512,768]{1,0:T(8,128)(2,1)S(1)}, bf16[512,768]{1,0:T(8,128)(2,1)}, u32[]{:S(2)}) copy-start(bf16[512,768]{1,0:T(8,128)(2,1)} %get-tuple-element.91.refs_0_) | copy-start | bytes 2359300
  347.5 4.3 copy-start.19
  347.6 5.1 copy-start.11
  347.6 5.2 copy-start.16
  348.6 174.8 %collective-permute-start.2 = (bf16[512,768]{1,0:T(8,128)(2,1)}, bf16[512,768]{1,0:T(8,128)(2,1)}, u32[]{:S(2)}, u32[]{:S(2)}) collective-permute-start(bf16[512,768]{1,0:T(8,128)(2,1)} %broadcast_select_fusion), channel_id=1, source_target_pairs={{0,16},{16,0},{1,17},{17,1},{2,18},{18,2},{3,19},{19,3},{4,20},{20... | collective-permute-start | bytes 2359304 | tf_op jit(solution)/shard_map/ppermute | solution.py:858
  354.1 166.7 %copy-start.1 = (bf16[512,768]{1,0:T(8,128)(2,1)S(1)}, bf16[512,768]{1,0:T(8,128)(2,1)}, u32[]{:S(2)}) copy-start(bf16[512,768]{1,0:T(8,128)(2,1)} %get-tuple-element.80.x_ref.refs_1_) | copy-start | bytes 2359300
  522.1 1.3 copy-start.4
  524.8 1.3 copy-start.15
  524.8 2.0 copy-start.14
  524.8 2.7 copy-start.8
  524.8 3.5 copy-start.7
  524.8 4.3 copy-start.18
  524.8 4.9 copy-start.6
  526.1 4.4 copy-start.10

commit v4 on v3

v4 whole, which is shorter than its diff:
```python
import functools
import math
from typing import Any, NamedTuple

import jax
import jax.numpy as jnp
from jax import lax
from jax.experimental import pallas as pl
from jax.experimental.pallas import tpu as pltpu
from jax.sharding import PartitionSpec as P

MESH = pl.DeviceIdType.MESH
HEADS = 12
EPSILON = 1e-05
GELU_SCALE = 0.7978845608028654
AXES = ("segment", "dp")


def half(value):
    return value.astype(jnp.bfloat16)


def wide(value):
    return value.astype(jnp.float32)


def mm(left, right):
    return jnp.dot(left, right, preferred_element_type=jnp.float32)


def mm_tn(left, right):
    return lax.dot_general(left, right, (((0,), (0,)), ((), ())), preferred_element_type=jnp.float32)


def mm_nt(left, right):
    return lax.dot_general(left, right, (((1,), (1,)), ((), ())), preferred_element_type=jnp.float32)


class Place:
    def __init__(self, nz):
        self.nz = nz
        self.x = lax.axis_index("segment")
        d = lax.axis_index("dp")
        self.c = d % 2
        self.y = (d // 2) % 2
        self.z = d // 4
        par = self.z % 2
        self.q = par * ((self.z + 1) // 2) + (1 - par) * ((nz - self.z // 2) % nz)

    def z_at(self, q):
        nz = self.nz
        upper = ((q + nz - 1) % nz) // (nz // 2)
        return (1 - upper) * (2 * q - 1) + upper * ((2 * (nz - q)) % (2 * nz))

    def ring_z(self, back):
        return self.z_at((self.q + 2 * self.nz - back) % self.nz)

    def device(self, x=None, z=None, y=None, c=None):
        x = self.x if x is None else x
        z = self.z if z is None else z
        y = self.y if y is None else y
        c = self.c if c is None else c
        return (x, (z * 2 + y) * 2 + c)

    def other(self, axis):
        return self.device(**{axis: 1 - getattr(self, axis)})

    def succ(self):
        return self.device(z=self.z_at((self.q + 1) % self.nz))

    def pred(self):
        return self.device(z=self.ring_z(1))


def greet(place):
    barrier = pltpu.get_barrier_semaphore()
    peers = [place.other("x"), place.other("y"), place.other("c"), place.succ(), place.pred()]
    for peer in peers:
        pl.semaphore_signal(barrier, inc=1, device_id=peer, device_id_type=MESH)
    pl.semaphore_wait(barrier, len(peers))


def block_of(ref, place, c, z, x=None, y=None):
    xs = pl.ds(0, 2) if x is None else x
    ys = pl.ds(0, 2) if y is None else y
    return ref.at[xs, z, ys, c]


def gather_kernel(plan, nz, *refs):
    orders, starts = zip(*plan)
    n = len(orders)
    far, own, outs, pair, refs = refs[:n], refs[n], refs[n + 1 : 2 * n + 1], refs[2 * n + 1], refs[2 * n + 2 :]
    raw, ins, (held, send, recv, local, swap, loads) = refs[:n], refs[n : 2 * n], refs[2 * n :]
    place = Place(nz)
    loading = [pltpu.make_async_copy(src, dst, loads.at[j]) for j, (src, dst) in enumerate(zip(far, raw))]
    loading.append(pltpu.make_async_copy(own.at[place.x], held, loads.at[n]))
    for copy in loading:
        copy.start()
    greet(place)
    stays = pltpu.make_async_copy(held, pair.at[place.x], swap.at[0])
    leaves = pltpu.make_async_remote_copy(
        src_ref=own.at[1 - place.x],
        dst_ref=pair.at[place.x],
        send_sem=swap.at[1],
        recv_sem=swap.at[2],
        device_id=place.other("x"),
        device_id_type=MESH,
    )
    started = []

    def put(i, k, src, dst, device):
        copy = pltpu.make_async_remote_copy(
            src_ref=src,
            dst_ref=dst,
            send_sem=send.at[i, k],
            recv_sem=recv.at[i, k],
            device_id=device,
            device_id_type=MESH,
        )
        copy.start()
        started.append(copy)
        return copy

    copies = [dict() for _ in orders]

    def stage(i, t):
        first, second, third = orders[i]
        out, mine = outs[i], copies[i]

        def shard(z, **at):
            return block_of(out, place, place.c, z, **at)

        def own(axis, z):
            return shard(z, **{axis: getattr(place, axis)})

        one = shard(place.z, x=place.x, y=place.y)
        if t == 0:
            loading[i].wait()
            ins[i][...] = half(raw[i][...])
            mine["own"] = pltpu.make_async_copy(ins[i], one, local.at[i])
            mine["own"].start()
        if second == "z":
            if t == 0:
                mine["p"] = put(i, 0, ins[i], one, place.other(first))
                return
            if t == 1:
                mine["own"].wait()
                mine["p"].wait_recv()
            elif t <= nz:
                mine["z", t - 1].wait_recv()
            if t <= nz:
                z = place.ring_z(t - 1)
                block = own(third, z)
                if t < nz:
                    mine["z", t] = put(i, t, block, block, place.succ())
                mine["l", t] = put(i, nz + t, block, block, place.other(third))
                mine["c", t] = put(i, 2 * nz + t, block, block, place.other("c"))
            if t >= 2:
                mine["l", t - 1].wait_recv()
                z = place.ring_z(t - 2)
                block = shard(z, **{third: 1 - getattr(place, third)})
                mine["d", t - 1] = put(i, 3 * nz + t - 1, block, block, place.other("c"))
        else:
            if t <= nz - 1:
                if t > 0:
                    mine["z", t].wait_recv()
                z = place.ring_z(t)
                src = ins[i] if t == 0 else shard(z, x=place.x, y=place.y)
                dst = shard(z, x=place.x, y=place.y)
                if t < nz - 1:
                    mine["z", t + 1] = put(i, t, src, dst, place.succ())
                mine["p", t + 1] = put(i, nz + t, src, dst, place.other(second))
            if 1 <= t <= nz:
                if t == 1:
                    mine["own"].wait()
                mine["p", t].wait_recv()
                block = own(third, place.ring_z(t - 1))
                mine["l", t] = put(i, 2 * nz + t, block, block, place.other(third))
                mine["c", t] = put(i, 3 * nz + t, block, block, place.other("c"))
            if t >= 2:
                mine["l", t - 1].wait_recv()
                block = shard(place.ring_z(t - 2), **{third: 1 - getattr(place, third)})
                mine["d", t - 1] = put(i, 4 * nz + t - 1, block, block, place.other("c"))

    stages = nz + 2
    for t in range(stages + max(starts)):
        for i in range(n):
            if 0 <= t - starts[i] < stages:
                stage(i, t - starts[i])
        if t == 0:
            leaves.start()
        if t == 1:
            loading[n].wait()
            stays.start()
    for mine in copies:
        for key, copy in mine.items():
            if key[0] in "cd":
                copy.wait_recv()
    for copy in started:
        copy.wait_send()
    stays.wait()
    leaves.wait()


def gather_all(shards, plan, mesh, own):
    nx, ndp = mesh.shape["segment"], mesh.shape["dp"]
    if nx != 2 or ndp != 16:
        first = lax.axis_index("segment") == 0
        other = lax.ppermute(jnp.where(first, own[1], own[0]), "segment", [(0, 1), (1, 0)])
        pair = jnp.where(first, jnp.stack([own[0], other]), jnp.stack([other, own[1]]))
        return [lax.all_gather(half(s), AXES, axis=0) for s in shards], pair
    nz, n = ndp // 4, len(shards)
    slots = 5 * nz + 2
    *outs, pair = pl.pallas_call(
        functools.partial(gather_kernel, plan, nz),
        out_shape=[jax.ShapeDtypeStruct((2, nz, 2, 2) + s.shape, jnp.bfloat16) for s in shards]
        + [jax.ShapeDtypeStruct(own.shape, own.dtype)],
        in_specs=[pl.BlockSpec(memory_space=pl.ANY)] * (n + 1),
        out_specs=[pl.BlockSpec(memory_space=pl.ANY)] * (n + 1),
        scratch_shapes=[pltpu.VMEM(s.shape, s.dtype) for s in shards]
        + [pltpu.VMEM(s.shape, jnp.bfloat16) for s in shards]
        + [
            pltpu.VMEM(own.shape[1:], own.dtype),
            pltpu.SemaphoreType.DMA((n, slots)),
            pltpu.SemaphoreType.DMA((n, slots)),
            pltpu.SemaphoreType.DMA((n,)),
            pltpu.SemaphoreType.DMA((3,)),
            pltpu.SemaphoreType.DMA((n + 1,)),
        ],
        compiler_params=pltpu.CompilerParams(collective_id=0, has_side_effects=True, vmem_limit_bytes=62 * 2**20),
        name="gather_weights",
    )(*shards, own)
    return [o.reshape((nx * ndp,) + s.shape) for o, s in zip(outs, shards)], pair


def add_to(dst, src):
    lead = dst.shape[:-2]

    def one(j, carry):
        at = (j // 2, j % 2) if len(lead) == 2 else (j,)[: len(lead)]
        at = at + (slice(None), slice(None))
        dst[at] = dst[at] + src[at]
        return carry

    if lead:
        lax.fori_loop(0, math.prod(lead), one, 0)
    else:
        dst[...] = dst[...] + src[...]


def scatter_kernel(plan, nz, *refs):
    orders, starts = zip(*plan)
    n = len(orders)
    ins, here, refs = refs[:n], refs[n], refs[n + 1 :]
    outs, there, refs = refs[:n], refs[n], refs[n + 1 :]
    accs, stages, firsts, rings, lasts = (refs[j * n : (j + 1) * n] for j in range(5))
    send, recv, local, swap = refs[5 * n :]
    place = Place(nz)
    greet(place)
    started = []
    swapped = pltpu.make_async_remote_copy(
        src_ref=here.at[1 - place.x],
        dst_ref=there,
        send_sem=swap.at[0],
        recv_sem=swap.at[1],
        device_id=place.other("x"),
        device_id_type=MESH,
    )

    def put(i, k, src, dst, device):
        copy = pltpu.make_async_remote_copy(
            src_ref=src,
            dst_ref=dst,
            send_sem=send.at[i, k],
            recv_sem=recv.at[i, k],
            device_id=device,
            device_id_type=MESH,
        )
        copy.start()
        started.append(copy)
        return copy

    live = [dict() for _ in orders]

    def load(i, k):
        copy = pltpu.make_async_copy(
            block_of(ins[i], place, place.c, place.ring_z(k)), stages[i].at[k % 2], local.at[i, k % 2]
        )
        copy.start()
        live[i]["o", k] = copy

    def stage(i, s):
        first, second, third = orders[i]
        acc, mine = accs[i], live[i]
        early, ring, late = firsts[i], rings[i], lasts[i]

        def part(k, flip=0, flip2=None):
            own = {axis: getattr(place, axis) for axis in "xy"}
            own[first] = own[first] + flip * (1 - 2 * own[first])
            if flip2 is None:
                own["xy".replace(first, "")] = pl.ds(0, 2)
            else:
                other = "xy".replace(first, "")
                own[other] = own[other] + flip2 * (1 - 2 * own[other])
            return acc.at[k - 1, own["x"], own["y"]]

        if s == 0:
            for k in range(1, nz + 1):
                src = block_of(ins[i], place, 1 - place.c, place.ring_z(k))
                mine["c", k] = put(i, k, src, acc.at[k - 1], place.other("c"))
            load(i, 1)
            load(i, 2)
        if 1 <= s <= nz:
            k = s
            mine["c", k].wait_recv()
            mine["o", k].wait()
            add_to(acc.at[k - 1], stages[i].at[k % 2])
            if k + 2 <= nz:
                load(i, k + 2)
            mine["p", k] = put(i, nz + k, part(k, 1), early.at[k - 1], place.other(first))
        if 2 <= s <= nz + 1:
            k = s - 1
            mine["p", k].wait_recv()
            add_to(part(k), early.at[k - 1])
        if second == "z":
            if s == 2:
                mine["z", 1] = put(i, 2 * nz + 1, part(1), ring.at[0], place.succ())
            if 3 <= s <= nz + 1:
                t = s - 2
                mine["z", t].wait_recv()
                add_to(ring.at[t - 1], part(t + 1))
                if t < nz - 1:
                    mine["z", t + 1] = put(i, 2 * nz + t + 1, ring.at[t - 1], ring.at[t], place.succ())
                else:
                    there = 1 - getattr(place, third)
                    mine["l"] = put(i, 3 * nz + 1, ring.at[t - 1, there], late, place.other(third))
            if s == nz + 2:
                mine["l"].wait_recv()
                outs[i][...] = wide(ring[nz - 2, getattr(place, third)]) + wide(late[...])
        else:
            if 2 <= s <= nz + 1:
                k = s - 1
                mine["l", k] = put(i, 3 * nz + k, part(k, 0, 1), late.at[k - 1], place.other(second))
            if 3 <= s <= nz + 2:
                k = s - 2
                mine["l", k].wait_recv()
                add_to(part(k, 0, 0), late.at[k - 1])
                if k == 1:
                    mine["z", 1] = put(i, 2 * nz + 1, part(1, 0, 0), ring.at[0], place.succ())
                else:
                    t = k - 1
                    mine["z", t].wait_recv()
                    if t < nz - 1:
                        add_to(ring.at[t - 1], part(t + 1, 0, 0))
                        mine["z", t + 1] = put(i, 2 * nz + t + 1, ring.at[t - 1], ring.at[t], place.succ())
                    else:
                        outs[i][...] = wide(ring[t - 1]) + wide(part(nz, 0, 0)[...])

    stages_of = nz + 3
    for t in range(stages_of + max(starts)):
        for i in range(n):
            if 0 <= t - starts[i] < stages_of:
                stage(i, t - starts[i])
        if t == 0:
            swapped.start()
    for copy in started:
        copy.wait_send()
    swapped.wait()


def finish_kernel(count, *refs):
    n = (len(refs) - 7 - count) // 3
    here, other, ins, packed, refs = refs[:2], refs[2:4], refs[4 : 4 + n], refs[4 + n], refs[5 + n :]
    outs, vectors, held, (rows, sem) = refs[: 2 + n], refs[2 + n : 2 + n + count], refs[2 + n + count : -2], refs[-2:]
    x = lax.axis_index("segment")
    moves = []
    for j in range(2):
        moves.append((here[j].at[x], rows.at[j, 0], outs[j].at[x]))
        moves.append((other[j], rows.at[j, 1], outs[j].at[1 - x]))
    moves += list(zip(ins, held, outs[2:]))
    steps = []
    for j, (src, via, dst) in enumerate(moves):
        steps.append((pltpu.make_async_copy(src, via, sem.at[j, 0]), pltpu.make_async_copy(via, dst, sem.at[j, 1])))
        steps[-1][0].start()
    row = 0
    for dst in vectors:
        size, at = dst.shape[1], 0
        while at < size:
            more = min(128, size - at)
            dst[:, at : at + more] = packed[row : row + 1, :more]
            at, row = at + more, row + 1
    for load, store in steps:
        load.wait()
        store.start()
    for load, store in steps:
        store.wait()


def finish(rows, others, arrays, packed, sizes):
    like = [jax.ShapeDtypeStruct(a.shape, a.dtype) for a in list(rows) + list(arrays)]
    vectors = [jax.ShapeDtypeStruct((1, size), jnp.float32) for size in sizes]
    far, near = pl.BlockSpec(memory_space=pl.ANY), pl.BlockSpec(memory_space=pltpu.VMEM)
    got = pl.pallas_call(
        functools.partial(finish_kernel, len(sizes)),
        out_shape=like + vectors,
        in_specs=[far] * (4 + len(arrays)) + [near],
        out_specs=[far] * len(like) + [near] * len(sizes),
        scratch_shapes=[pltpu.VMEM(a.shape, a.dtype) for a in arrays]
        + [pltpu.VMEM((2,) + rows[0].shape, rows[0].dtype), pltpu.SemaphoreType.DMA((4 + len(arrays), 2))],
        compiler_params=pltpu.CompilerParams(vmem_limit_bytes=62 * 2**20),
        name="finish",
    )(*rows, *others, *arrays, packed)
    return got[: len(like)], got[len(like) :]


def from_other(rows):
    return lax.ppermute(rows[1 - lax.axis_index("segment")], "segment", [(0, 1), (1, 0)])


def scatter_all(grads, plan, mesh, rows):
    nx, ndp = mesh.shape["segment"], mesh.shape["dp"]
    if nx != 2 or ndp != 16:
        return [wide(lax.psum_scatter(g, AXES, scatter_dimension=0, tiled=False)) for g in grads], from_other(rows)
    nz, n = ndp // 4, len(grads)

    def scratch(lead):
        return [pltpu.VMEM(lead(o) + g.shape[1:], g.dtype) for (o, _), g in zip(plan, grads)]

    slots = 4 * nz + 2
    far, near = pl.BlockSpec(memory_space=pl.ANY), pl.BlockSpec(memory_space=pltpu.VMEM)
    got = pl.pallas_call(
        functools.partial(scatter_kernel, plan, nz),
        out_shape=[jax.ShapeDtypeStruct(g.shape[1:], jnp.float32) for g in grads]
        + [jax.ShapeDtypeStruct(rows.shape[1:], rows.dtype)],
        in_specs=[far] * (n + 1),
        out_specs=[near] * n + [far],
        scratch_shapes=scratch(lambda o: (nz, 2, 2))
        + scratch(lambda o: (2, 2, 2))
        + scratch(lambda o: (nz, 2))
        + scratch(lambda o: (nz - 1, 2) if o[1] == "z" else (nz - 1,))
        + scratch(lambda o: () if o[1] == "z" else (nz,))
        + [
            pltpu.SemaphoreType.DMA((n, slots)),
            pltpu.SemaphoreType.DMA((n, slots)),
            pltpu.SemaphoreType.DMA((n, 2)),
            pltpu.SemaphoreType.DMA((2,)),
        ],
        compiler_params=pltpu.CompilerParams(
            collective_id=1, has_side_effects=True, vmem_limit_bytes=62 * 2**20
        ),
        name="sum_gradients",
    )(*[g.reshape((2, nz, 2, 2) + g.shape[1:]) for g in grads], rows)
    return got[:n], got[n]


ROWS = 512
HIDDEN = 768
GAIN1, BIAS1, VALUE_B, OUT_B, GAIN2, BIAS2, OUTER_B, FIRST_B = range(8)


def chunks(rows, size=ROWS):
    return [slice(at, at + size) for at in range(0, rows, size)]


def norm_parts(rows):
    centre = rows - jnp.mean(rows, axis=-1, keepdims=True)
    inv = lax.rsqrt(jnp.mean(centre * centre, axis=-1, keepdims=True) + EPSILON)
    return centre * inv, inv


def row_loop(rows, body, init):
    return lax.fori_loop(0, rows // 128, lambda j, c: body(pl.ds(pl.multiple_of(j * 128, 128), 128), c), init)


def norm_into(read, write, gain, shift, rows):
    def body(r, carry):
        write[r, :] = half(norm_parts(read(r))[0] * gain + shift)
        return carry

    row_loop(rows, body, 0)


def norm_back(read, grad, gain, rows, done):
    def body(r, carry):
        normal, inv = norm_parts(read(r))
        m_hat = grad(r)
        m = m_hat * gain
        part = inv * (
            m - jnp.mean(m, axis=-1, keepdims=True) - normal * jnp.mean(m * normal, axis=-1, keepdims=True)
        )
        done(r, part)
        return carry[0] + sums(m_hat * normal), carry[1] + sums(m_hat)

    zero = jnp.zeros_like(gain)
    return row_loop(rows, body, (zero, zero))


def sums(value):
    return jnp.sum(wide(value), axis=0, keepdims=True)


def gelu_both(t):
    square = t * t
    s = 0.5 + 0.5 * jnp.tanh(t * (GELU_SCALE + GELU_SCALE * 0.044715 * square))
    value = t * s
    slope = s + value * (1.0 - s) * (2 * GELU_SCALE + 6 * GELU_SCALE * 0.044715 * square)
    return value, slope


def masked_pair(head):
    return lax.broadcasted_iota(jnp.int32, (1, 2 * head), 1) < head


def add_up(fresh, ref, at, value):
    @pl.when(fresh)
    def _():
        ref[at] = value

    @pl.when(jnp.logical_not(fresh))
    def _():
        ref[at] += value


def forward_start(read, vec, value_ref, a_ref, v_ref, first=None):
    rows = a_ref.shape[0]
    norm_into(read, a_ref, vec(GAIN1), vec(BIAS1), rows)
    for r in chunks(rows):
        v_ref[r] = half(mm(a_ref[r], value_ref[...]) + vec(VALUE_B))
        if first is not None:
            first_ref, first_b, p_ref, slope_ref = first
            value, slope = gelu_both(mm(a_ref[r], first_ref[...]) + first_b[...])
            p_ref[r] = half(value)
            slope_ref[r] = half(slope)


def both_heads(pair, head):
    lower = masked_pair(head)
    zero = jnp.zeros_like(pair)
    return jnp.concatenate([jnp.where(lower, pair, zero), jnp.where(lower, zero, pair)], axis=0)


def forward_heads(pair, length, v_ref, c_ref, probs_ref, logits_of):
    rows, width = v_ref.shape
    slots = probs_ref.shape[1] // 2
    head = width // HEADS
    at = pl.ds(pl.multiple_of(pair * 2 * head, 2 * head), 2 * head)
    shut = jnp.where(lax.broadcasted_iota(jnp.int32, (1, slots), 1) >= length, -1e30, 0.0)
    both = logits_of(shut)
    for h in range(2):
        logits = both[h]
        expo = jnp.exp(logits - jnp.max(logits, axis=1, keepdims=True))
        probs_ref[:, h * slots : (h + 1) * slots] = half(expo * (1.0 / jnp.sum(expo, axis=1, keepdims=True)))
    c_ref[:, at] = half(mm(probs_ref[...], both_heads(v_ref[:, at], head)))


def forward_middle(read, vec, out_ref, c_ref, hid_ref, b_ref):
    rows = c_ref.shape[0]
    for r in chunks(rows):
        hid_ref[r] = read(r) + mm(c_ref[r], out_ref[...]) + vec(OUT_B)
    norm_into(lambda r: hid_ref[r, :], b_ref, vec(GAIN2), vec(BIAS2), rows)


def forward_hidden(fresh, b_ref, inner_ref, inner_b, outer_ref, q_ref, slope_ref, acc):
    for r in chunks(b_ref.shape[0]):
        value, slope = gelu_both(mm(b_ref[r], inner_ref[...]) + inner_b)
        q = half(value)
        q_ref[r] = q
        slope_ref[r] = half(slope)
        add_up(fresh, acc, r, mm(q, outer_ref[...]))


def forward_end(vec, hid_ref, acc, y_ref):
    for r in chunks(acc.shape[0]):
        y_ref[r] = half(hid_ref[r] + acc[r] + vec(OUTER_B))


def backward_hidden(fresh, g_ref, b_ref, q_ref, slope_ref, inner_ref, outer_ref, gz_ref, acc, g_outer, g_inner, g_inner_b):
    for r in chunks(g_ref.shape[0]):
        gz = half(mm_nt(g_ref[r], outer_ref[...]) * wide(slope_ref[r]))
        gz_ref[r] = gz
        add_up(fresh, acc, r, mm_nt(gz, inner_ref[...]))
    gz = gz_ref[...]
    g_outer[...] = half(mm_tn(q_ref[...], g_ref[...]))
    g_inner[...] = half(mm_tn(b_ref[...], gz))
    g_inner_b[...] = sums(gz)


def backward_middle(vec, put, g_ref, hid_ref, c_ref, out_ref, acc, ghid, gatt, gc_ref, g_out):
    rows = g_ref.shape[0]

    def done(r, part):
        total = wide(g_ref[r, :]) + part
        ghid[r, :] = total
        gatt[r, :] = half(total)

    gain, shift = norm_back(lambda r: hid_ref[r, :], lambda r: acc[r, :], vec(GAIN2), rows, done)
    put(GAIN2, gain)
    put(BIAS2, shift)
    put(OUTER_B, sums(g_ref[...]))
    put(OUT_B, sums(gatt[...]))
    g_out[...] = half(mm_tn(c_ref[...], gatt[...]))
    for r in chunks(rows):
        gc_ref[r] = half(mm_nt(gatt[r], out_ref[...]))


def backward_heads(pair, v_ref, gc_ref, gv_ref, probs_ref, db):
    rows, width = v_ref.shape
    slots = probs_ref.shape[1] // 2
    head = width // HEADS
    at = pl.ds(pl.multiple_of(pair * 2 * head, 2 * head), 2 * head)
    both = mm_nt(gc_ref[:, at], both_heads(v_ref[:, at], head))
    for h in range(2):
        cols = slice(h * slots, (h + 1) * slots)
        probs = wide(probs_ref[:, cols])
        weighed = probs * both[:, cols]
        db[:, cols] = half(weighed - probs * jnp.sum(weighed, axis=1, keepdims=True))
    values = mm_tn(probs_ref[...], gc_ref[:, at])
    gv_ref[:, at] = half(jnp.where(masked_pair(head), values[:slots], values[slots:]))


def backward_end(vec, put, read, gv_ref, value_ref, a_ref, acc, ghid, g_value, gx_ref, first=None):
    rows = gv_ref.shape[0]
    put(VALUE_B, sums(gv_ref[...]))
    g_value[...] = half(mm_tn(a_ref[...], gv_ref[...]))
    if first is not None:
        first_ref, slope_ref, gf_ref, g_first = first
        for r in chunks(rows):
            gf_ref[r] = half(acc[r] * wide(slope_ref[r]))
        put(FIRST_B, sums(gf_ref[...]))
        g_first[...] = half(mm_tn(a_ref[...], gf_ref[...]))
    else:
        put(FIRST_B, jnp.zeros((1, acc.shape[1]), jnp.float32))
    for r in chunks(rows):
        ga = mm_nt(gv_ref[r], value_ref[...])
        if first is not None:
            ga = ga + mm_nt(gf_ref[r], first_ref[...])
        acc[r] = ga

    def done(r, part):
        gx_ref[r, :] = half(ghid[r, :] + part)

    gain, shift = norm_back(read, lambda r: acc[r, :], vec(GAIN1), rows, done)
    put(GAIN1, gain)
    put(BIAS1, shift)


def forward_kernel(pairs, parts, length_ref, x_ref, vec_ref, value_ref, out_ref, first_ref, first_b, second_ref, second_b, inner_ref, inner_b, outer_ref, y_ref, *refs):
    kept, probs_ref, q_ref, slope_ref = refs[:7], refs[7], refs[8], refs[9]
    a_ref, v_ref, p_ref, first_slope, c_ref, b_ref, hid_ref, acc, sem = refs[10:]
    held = (a_ref, v_ref, p_ref, first_slope, c_ref, b_ref, hid_ref)
    copies = [pltpu.make_async_copy(src, dst, sem.at[j]) for j, (src, dst) in enumerate(zip(held, kept))]
    i = pl.program_id(0)
    slots = probs_ref.shape[2] // 2

    def vec(k):
        return vec_ref[0, k : k + 1, :]

    x_ref, y_ref = x_ref.at[0], y_ref.at[0]

    def read(r):
        return wide(x_ref[r, :])

    @pl.when(i == 0)
    def _():
        forward_start(read, vec, value_ref.at[0], a_ref, v_ref, (first_ref, first_b, p_ref, first_slope))
        for copy in copies[:4]:
            copy.start()

    @pl.when(i < pairs)
    def _():
        def logits_of(shut):
            logits = mm(p_ref[...], second_ref[...]) + (second_b[...] + jnp.concatenate([shut, shut], axis=1))
            return logits[:, :slots], logits[:, slots:]

        forward_heads(i, length_ref[0], v_ref, c_ref, probs_ref.at[0], logits_of)

    @pl.when(i == pairs - 1)
    def _():
        forward_middle(read, vec, out_ref.at[0], c_ref, hid_ref, b_ref)
        for copy in copies[4:]:
            copy.start()

    @pl.when(i >= pairs)
    def _():
        forward_hidden(i == pairs, b_ref, inner_ref.at[0], inner_b[0], outer_ref.at[0], q_ref, slope_ref, acc)

    @pl.when(i == pairs + parts - 1)
    def _():
        forward_end(vec, hid_ref, acc, y_ref)
        for copy in copies:
            copy.wait()


def backward_kernel(pairs, parts, g_ref, b_ref, vec_ref, q_ref, slope_ref, probs_ref, inner_ref, outer_ref, second_ref, *refs):
    far, refs = refs[:10], refs[16:]
    gx_ref, g_outer, g_inner, g_out, g_value, g_vec, g_inner_b, g_first, g_second, g_second_b = refs[:10]
    near, refs = refs[10:20], refs[20:]
    acc, ghid, gatt, gc_ref, gv_ref, db, gz_ref, sem = refs
    far = [ref.at[0] if len(ref.shape) == 3 else ref for ref in far]
    copies = [pltpu.make_async_copy(src, dst, sem.at[j]) for j, (src, dst) in enumerate(zip(far, near))]
    hid_ref, c_ref, out_ref, v_ref, p_ref, a_ref, value_ref, first_ref, first_slope, x_ref = near
    g_ref, gx_ref = g_ref.at[0], gx_ref.at[0]
    i = pl.program_id(0)
    slots = probs_ref.shape[2] // 2

    def vec(k):
        return vec_ref[0, k : k + 1, :]

    def put(k, value):
        g_vec[0, k : k + 1, :] = value

    @pl.when(i == 0)
    def _():
        for copy in copies:
            copy.start()

    @pl.when(i < parts)
    def _():
        backward_hidden(i == 0, g_ref, b_ref, q_ref, slope_ref, inner_ref.at[0], outer_ref.at[0], gz_ref, acc, g_outer.at[0], g_inner.at[0], g_inner_b.at[0])

    @pl.when(i == parts - 1)
    def _():
        for copy in copies[:3]:
            copy.wait()
        backward_middle(vec, put, g_ref, hid_ref, c_ref, out_ref, acc, ghid, gatt, gc_ref, g_out.at[0])
        for copy in copies[3:5]:
            copy.wait()

    @pl.when(i >= parts)
    def _():
        backward_heads(i - parts, v_ref, gc_ref, gv_ref, probs_ref.at[0], db)
        g_second[...] = half(mm_tn(p_ref[...], db[...]))
        g_second_b[...] = sums(db[...])
        add_up(i == parts, acc, slice(None), mm_nt(db[...], second_ref[...]))

    @pl.when(i == pairs + parts - 1)
    def _():
        for copy in copies[5:]:
            copy.wait()
        backward_end(
            vec, put, lambda r: wide(x_ref[r, :]), gv_ref, value_ref, a_ref, acc, ghid, g_value.at[0], gx_ref,
            (first_ref, first_slope, gatt, g_first),
        )


def both_kernel(pairs, parts, length_ref, x_ref, g_ref, vec_ref, value_ref, out_ref, table_ref, inner_ref, inner_b, outer_ref, *refs):
    y_ref, gx_ref, g_outer, g_inner, g_out, g_value, g_vec, g_inner_b, g_table = refs[:9]
    acc, hid_ref, ghid, a_ref, v_ref, c_ref, b_ref, gatt, gc_ref, gv_ref, probs_ref, q_ref, slope_ref, db, gz_ref = refs[9:]
    i = pl.program_id(0)
    slots = probs_ref.shape[2] // 2
    j = i - pairs
    k = j - parts
    n = k - parts

    def vec(k):
        return vec_ref[0, k : k + 1, :]

    def put(k, value):
        g_vec[0, k : k + 1, :] = value

    x_ref, g_ref, y_ref, gx_ref = (ref.at[0] for ref in (x_ref, g_ref, y_ref, gx_ref))

    def read(r):
        return wide(x_ref[r, :])

    @pl.when(i == 0)
    def _():
        forward_start(read, vec, value_ref.at[0], a_ref, v_ref)

    @pl.when(i < pairs)
    def _():
        def logits_of(shut):
            return wide(table_ref[:slots, :]) + shut, wide(table_ref[slots:, :]) + shut

        forward_heads(i, length_ref[0], v_ref, c_ref, probs_ref.at[i], logits_of)

    @pl.when(i == pairs - 1)
    def _():
        forward_middle(read, vec, out_ref.at[0], c_ref, hid_ref, b_ref)

    @pl.when((j >= 0) & (j < parts))
    def _():
        forward_hidden(j == 0, b_ref, inner_ref.at[0], inner_b[0], outer_ref.at[0], q_ref.at[j], slope_ref.at[j], acc)

    @pl.when(j == parts - 1)
    def _():
        forward_end(vec, hid_ref, acc, y_ref)

    @pl.when((k >= 0) & (k < parts))
    def _():
        at = parts - 1 - k
        backward_hidden(k == 0, g_ref, b_ref, q_ref.at[at], slope_ref.at[at], inner_ref.at[0], outer_ref.at[0], gz_ref, acc, g_outer.at[0], g_inner.at[0], g_inner_b.at[0])

    @pl.when(k == parts - 1)
    def _():
        backward_middle(vec, put, g_ref, hid_ref, c_ref, out_ref.at[0], acc, ghid, gatt, gc_ref, g_out.at[0])

    @pl.when(n >= 0)
    def _():
        backward_heads(n, v_ref, gc_ref, gv_ref, probs_ref.at[n], db)
        g_table[:slots, :] = db[:, :slots]
        g_table[slots:, :] = db[:, slots:]

    @pl.when(n == pairs - 1)
    def _():
        backward_end(vec, put, read, gv_ref, value_ref.at[0], a_ref, acc, ghid, g_value.at[0], gx_ref)


class Weights(NamedTuple):
    vectors: Any
    value: Any
    out: Any
    inner: Any
    inner_b: Any
    outer: Any
    first: Any
    first_b: Any
    second: Any
    second_b: Any
    table: Any


def whole(shape, *at):
    at = tuple(at)
    block = (1,) * len(at) + tuple(shape[len(at) :])
    return pl.BlockSpec(block, lambda i: at + (0,) * (len(shape) - len(at)), pipeline_mode=pl.Buffered(1))


def whole_out(shape, *at):
    at = tuple(at)
    block = (1,) * len(at) + tuple(shape[len(at) :])
    return pl.BlockSpec(block, lambda i: at + (0,) * (len(shape) - len(at)))


def like(shape, dtype=jnp.bfloat16):
    return jax.ShapeDtypeStruct(shape, dtype)


FAR = pl.BlockSpec(memory_space=pl.ANY)


def sizes_of(x, w):
    rows, width = x.shape[-2:]
    parts = w.inner.shape[2] // HIDDEN
    return rows, width, HEADS // 2, parts, w.inner.shape[2] // parts


def forward(x, length, w):
    rows, width, pairs, parts, part = sizes_of(x, w)
    slots = rows

    def pair(i):
        return jnp.minimum(i, pairs - 1)

    def piece(i):
        return jnp.maximum(i - pairs, 0)

    ins = [length, x, w.vectors, w.value, w.out, w.first, w.first_b, w.second, w.second_b, w.inner, w.inner_b, w.outer]
    specs = [
        pl.BlockSpec(memory_space=pltpu.SMEM),
        whole(x.shape, 0),
        whole(w.vectors.shape, 0),
        whole(w.value.shape, 0),
        whole(w.out.shape, 0),
        whole(w.first.shape),
        whole(w.first_b.shape),
        pl.BlockSpec((width, 2 * slots), lambda i: (0, pair(i))),
        pl.BlockSpec((1, 2 * slots), lambda i: (0, pair(i))),
        pl.BlockSpec((1, width, part), lambda i: (0, 0, piece(i))),
        pl.BlockSpec((1, 1, part), lambda i: (0, 0, piece(i))),
        pl.BlockSpec((1, part, width), lambda i: (0, piece(i), 0)),
    ]
    half_rows = like((rows, width))
    kept = [half_rows] * 6 + [like((rows, width), jnp.float32)]
    hidden_block = pl.BlockSpec((rows, part), lambda i: (0, piece(i)))
    y, *saved = pl.pallas_call(
        functools.partial(forward_kernel, pairs, parts),
        grid=(pairs + parts,),
        out_shape=[like(x.shape)] + kept + [like((pairs, rows, 2 * slots))] + [like((rows, part * parts))] * 2,
        in_specs=specs,
        out_specs=[whole_out(x.shape, 0)]
        + [FAR] * 7
        + [pl.BlockSpec((1, rows, 2 * slots), lambda i: (pair(i), 0, 0))]
        + [hidden_block] * 2,
        scratch_shapes=[pltpu.VMEM(k.shape, k.dtype) for k in kept]
        + [pltpu.VMEM((rows, width), jnp.float32), pltpu.SemaphoreType.DMA((7,))],
        compiler_params=pltpu.CompilerParams(vmem_limit_bytes=62 * 2**20),
        name="forward_0",
    )(*ins)
    return y, saved


def backward(g, x, saved, w, before):
    rows, width, pairs, parts, part = sizes_of(x, w)
    slots = rows
    a, v, p, first_slope, c, b, hid, probs, q, slope = saved

    def pair(i):
        return jnp.maximum(i - parts, 0)

    def piece(i):
        return jnp.minimum(i, parts - 1)

    hidden_block = pl.BlockSpec((rows, part), lambda i: (0, piece(i)))
    inner_block = pl.BlockSpec((1, width, part), lambda i: (0, 0, piece(i)))
    outer_block = pl.BlockSpec((1, part, width), lambda i: (0, piece(i), 0))
    second_block = pl.BlockSpec((width, 2 * slots), lambda i: (0, pair(i)))
    far = [hid, c, w.out, v, p, a, w.value, w.first, first_slope, x]
    ins = [g, b, w.vectors, q, slope, probs, w.inner, w.outer, w.second] + far
    specs = [whole(g.shape, 1), whole((rows, width)), whole(w.vectors.shape, 0)] + [hidden_block] * 2
    specs += [pl.BlockSpec((1, rows, 2 * slots), lambda i: (pair(i), 0, 0)), inner_block, outer_block, second_block]
    specs += [FAR] * 10
    aliases = {len(ins) + j: 1 + j for j in range(6)}
    aliases[0] = 0
    ins += list(before)
    specs += [FAR] * 6
    outs = [like(g.shape)] + [like(k.shape, k.dtype) for k in before]
    out_specs = [whole_out(g.shape, 0), outer_block, inner_block]
    out_specs += [whole_out(w.out.shape, 0), whole_out(w.value.shape, 0), whole_out((2, 8, width), 0)]
    out_specs += [pl.BlockSpec((1, 1, part), lambda i: (0, 0, piece(i)))]
    outs += [like(w.first.shape), like(w.second.shape), like(w.second_b.shape, jnp.float32)]
    out_specs += [whole_out(w.first.shape), second_block, pl.BlockSpec((1, 2 * slots), lambda i: (0, pair(i)))]
    gx, *grads = pl.pallas_call(
        functools.partial(backward_kernel, pairs, parts),
        grid=(pairs + parts,),
        out_shape=outs,
        in_specs=specs,
        out_specs=out_specs,
        scratch_shapes=[pltpu.VMEM(k.shape[-2:], k.dtype) for k in far]
        + [pltpu.VMEM((rows, width), jnp.float32)] * 2
        + [pltpu.VMEM((rows, width), jnp.bfloat16)] * 3
        + [pltpu.VMEM((rows, 2 * slots), jnp.bfloat16), pltpu.VMEM((rows, part), jnp.bfloat16), pltpu.SemaphoreType.DMA((10,))],
        input_output_aliases=aliases,
        compiler_params=pltpu.CompilerParams(vmem_limit_bytes=62 * 2**20),
        name="backward_0",
    )(*ins)
    return gx, grads[:6], grads[6:]


def both_ways(x, g, length, w):
    rows, width, pairs, parts, part = sizes_of(x, w)
    slots = rows

    def there(i):
        return jnp.minimum(i, pairs - 1)

    def back(i):
        return jnp.maximum(i - pairs - 2 * parts, 0)

    def piece(i):
        j = jnp.clip(i - pairs, 0, 2 * parts - 1)
        return jnp.minimum(j, 2 * parts - 1 - j)

    def late(i):
        return parts - 1 - jnp.clip(i - pairs - parts, 0, parts - 1)

    ins = [length, x, g, w.vectors, w.value, w.out, w.table, w.inner, w.inner_b, w.outer]
    specs = [pl.BlockSpec(memory_space=pltpu.SMEM), whole(x.shape, 0), whole(g.shape, 1)]
    specs += [whole(w.vectors.shape, 1), whole(w.value.shape, 1), whole(w.out.shape, 1)]
    specs += [
        pl.BlockSpec((2 * slots, slots), lambda i: (there(i), 0)),
        pl.BlockSpec((1, width, part), lambda i: (1, 0, piece(i))),
        pl.BlockSpec((1, 1, part), lambda i: (1, 0, piece(i))),
        pl.BlockSpec((1, part, width), lambda i: (1, piece(i), 0)),
    ]
    grads = [like(w.outer.shape), like(w.inner.shape), like(w.out.shape), like(w.value.shape)]
    grads += [like((2, 8, width), jnp.float32), like(w.inner_b.shape, jnp.float32), like(w.table.shape)]
    grad_specs = [
        pl.BlockSpec((1, part, width), lambda i: (1, late(i), 0)),
        pl.BlockSpec((1, width, part), lambda i: (1, 0, late(i))),
        whole_out(w.out.shape, 1),
        whole_out(w.value.shape, 1),
        whole_out((2, 8, width), 1),
        pl.BlockSpec((1, 1, part), lambda i: (1, 0, late(i))),
        pl.BlockSpec((2 * slots, slots), lambda i: (back(i), 0)),
    ]
    y, gx, *grads = pl.pallas_call(
        functools.partial(both_kernel, pairs, parts),
        grid=(2 * pairs + 2 * parts,),
        out_shape=[like(x.shape)] * 2 + grads,
        in_specs=specs,
        out_specs=[whole_out(x.shape, 1)] * 2 + grad_specs,
        scratch_shapes=[pltpu.VMEM((rows, width), jnp.float32)] * 3
        + [pltpu.VMEM((rows, width), jnp.bfloat16)] * 7
        + [pltpu.VMEM((pairs, rows, 2 * slots), jnp.bfloat16)]
        + [pltpu.VMEM((parts, rows, part), jnp.bfloat16)] * 2
        + [pltpu.VMEM((rows, 2 * slots), jnp.bfloat16), pltpu.VMEM((rows, part), jnp.bfloat16)],
        input_output_aliases={1: 0},
        compiler_params=pltpu.CompilerParams(vmem_limit_bytes=62 * 2**20),
        name="forward_backward_1",
    )(*ins)
    return y, gx, grads[:6], grads[6]


ROW_VECTORS = (0, 1, 3, 5, 6, 7, 11)
VECTORS = ROW_VECTORS + (9, 13, 15)
MATRICES = (2, 4, 8, 10, 12, 14, 16)
SMALL = 17
GATHER = (
    (8, "zyx", 1),
    (10, "yzx", 1),
    (16, "xzy", 0),
    (14, "xzy", 1),
    (SMALL, "xzy", 0),
    (12, "zyx", 0),
    (4, "zxy", 0),
    (2, "zxy", 0),
)
SUM = (
    (12, "yzx", 2),
    (8, "xzy", 2),
    (16, "xzy", 4),
    (4, "yzx", 0),
    (SMALL, "yzx", 1),
    (2, "yzx", 0),
    (14, "yxz", 4),
    (10, "yxz", 2),
)


def planned(call, plan, arrays, mesh, rows):
    got, rows = call([arrays[k] for k, _, _ in plan], [entry[1:] for entry in plan], mesh, rows)
    return {k: g for (k, _, _), g in zip(plan, got)}, rows


def lanes(array):
    n, size = array.shape
    rows = -(-size // 128)
    return jnp.pad(array, ((0, 0), (0, rows * 128 - size))).reshape(n, rows, 128)


def per_device(mesh, boundary, lengths, *parts):
    nx, ndp = mesh.shape["segment"], mesh.shape["dp"]
    devices = nx * ndp
    first = lax.axis_index("segment") == 0
    length = jnp.where(first, lengths[0], lengths[1])
    sizes = [parts[k].size for k in VECTORS]

    shards = {k: parts[k].reshape(parts[k].shape[-2:]) for k in MATRICES}
    flat = jnp.concatenate([parts[k].reshape(-1) for k in VECTORS])
    rows = -(-flat.size // 2048) * 16
    shards[SMALL] = jnp.pad(flat, (0, rows * 128 - flat.size)).reshape(rows, 128)
    full, pair = planned(gather_all, GATHER, shards, mesh, boundary[0, :, 0])
    for k in MATRICES:
        g = full[k]
        full[k] = g.reshape((nx, ndp * g.shape[1]) + g.shape[2:]) if k < 12 else g.reshape(-1, g.shape[2])
    vec = wide(full[SMALL].reshape(devices, rows * 128))
    count, size = len(ROW_VECTORS), sizes[0]
    bounds = [count * size]
    for k in VECTORS[count:]:
        bounds.append(bounds[-1] + parts[k].size)
    vectors = vec[:, : bounds[0]].reshape(nx, ndp, count, size).transpose(0, 2, 1, 3).reshape(nx, count, -1)
    inner_b, first_b, second_b = (vec[:, lo:hi] for lo, hi in zip(bounds, bounds[1:]))
    w = Weights(
        vectors,
        full[2],
        full[4],
        full[8],
        inner_b.reshape(nx, 1, -1),
        full[10],
        full[12],
        first_b.reshape(1, -1),
        full[14],
        second_b.reshape(1, -1),
        full[16],
    )

    outs, saved = forward(pair, length, w)
    outs, gins, both, g_table = both_ways(outs, pair, length, w)
    other_outs = from_other(outs)
    gins, both, synth = backward(gins, pair, saved, w, both)

    g_outer, g_inner, g_out, g_value, g_vec, g_inner_b = both
    g_first, g_second, g_second_b = synth
    matrices = (g_value, g_out, g_inner, g_outer, g_first, g_second, g_table)
    grads = {k: g.reshape((devices,) + parts[k].shape[-2:]) for k, g in zip(MATRICES, matrices)}
    vec = g_vec[:, :count].reshape(nx, count, ndp, size).transpose(0, 2, 1, 3).reshape(devices * count, size)
    vec = [lanes(vec).reshape(devices, -1, 128)]
    vec += [lanes(g.reshape(devices, -1)) for g in (g_inner_b, g_vec[0, FIRST_B], g_second_b)]
    vec = jnp.concatenate(vec, axis=1)
    grads[SMALL] = jnp.pad(vec, ((0, 0), (0, -vec.shape[1] % 16), (0, 0)))
    summed, other_gins = planned(scatter_all, SUM, grads, mesh, gins)
    arrays, vectors = finish([outs, gins], [other_outs, other_gins], [summed[k] for k in MATRICES], summed[SMALL], sizes)
    result = {k: g.reshape(parts[k].shape) for k, g in zip(MATRICES, arrays[2:])}
    for k, g in zip(VECTORS, vectors):
        result[k] = g.reshape(parts[k].shape)
    return tuple(a.reshape(boundary.shape) for a in arrays[:2]) + tuple(result[k] for k in range(17))


def solution(mesh):
    layer = [P("segment", "dp")] * 12
    layer[2] = layer[4] = layer[8] = layer[10] = P("segment", "dp", None)
    both = P(AXES)
    rows = P(AXES, None)
    boundary = P("segment", None, "dp", None, None)
    weights = tuple(layer) + (rows, both, rows, both, rows)
    return jax.shard_map(
        functools.partial(per_device, mesh),
        mesh=mesh,
        in_specs=(boundary, P(None, "dp")) + weights,
        out_specs=(boundary, boundary) + weights,
        check_vma=False,
    )
```

time: 532 us -> 476 us (0.89)
  Pallas kernels: 484 us -> 459 us
  other arithmetic: 18.5 us -> 3.04 us
  local copies, waits for them, and re-layouts: 20.3 us -> 10.8 us
  starting transfers between devices: 6.17 us -> 0.6 us
    pallas_call x4, Pallas kernels: 161 us -> 132 us  [the longest x1 51 us: both_ways(): pl.pallas_call(functools.partial(both_kernel, pairs, parts), grid=(2 * pa...]
    convert_element_type x6 -> x0, other arithmetic: 6.47 us -> none  [half(): return value.astype(jnp.bfloat16)]
    select_n x4 -> x0, other arithmetic: 5.98 us -> none  [the longest x2 3.08 us: swapped(): got = lax.ppermute(jnp.where(first, for_second, for_first), 'segment', swap)]
    ppermute x3 -> x1, starting transfers between devices: 6.17 us -> 0.6 us  [from_other(): lax.ppermute(rows[1 - lax.axis_index('segment')], 'segment', [(0, 1), (1,...]
  transfers between devices with their start and end apart: 3 -> 1, of which waited for: 0 -> 0; matrix products, arithmetic and copies ran while one was open for 5% -> 1% of each run, Pallas kernels for 78% -> 44%
where the time goes in v4:
time: 476 us; the launch traced here: 475 us
  Pallas kernels  459 us (96%)
  local copies, waits for them, and re-layouts  10.8 us (2%)
    pallas_call x1, Pallas kernels, scatter_all(): pl.pallas_call(functools.partial(scatter_kernel, plan, nz), out_shape=[ja...  167 us
    pallas_call x1, Pallas kernels, gather_all(): pl.pallas_call(functools.partial(gather_kernel, plan, nz), out_shape=[jax...  160 us
    pallas_call x1, Pallas kernels, both_ways(): pl.pallas_call(functools.partial(both_kernel, pairs, parts), grid=(2 * pa...  51 us
    pallas_call x1, Pallas kernels, backward(): pl.pallas_call(functools.partial(backward_kernel, pairs, parts), grid=(pa...  44.5 us
    pallas_call x1, Pallas kernels, forward(): pl.pallas_call(functools.partial(forward_kernel, pairs, parts), grid=(pai...  30.6 us
  transfers between devices with their start and end apart: 1, of which 0 were waited for; matrix products, arithmetic and copies ran while one was open for 1% of the time, Pallas kernels for 44%

profile of v4, /device:TPU:0, one launch (start us, length us, event | category | flops | bytes accessed | tf_op | source)
XLA Modules:
  0.0 475.3 jit_solution(4311591208450129101)
XLA Ops:
  0.7 0.9 concatenate.6
  1.6 0.6 pad_bitcast_fusion.refs_4_
  2.2 0.0 copy-start.1
  2.2 159.8 %gather_weights.1 = (bf16[2,4,2,2,48,3072]{5,4,3,2,1,0:T(8,128)(2,1)}, bf16[2,4,2,2,192,768]{5,4,3,2,1,0:T(8,128)(2,1)}, bf16[2,4,2,2,192,512]{5,4,3,2,1,0:T(8,1...) custom-call(f32[48,3072]{1,0:T(8,128)} %bitcast.90, ...), custom_call_target="tpu_custom_call" | custom-call | tf_op jit(solution)/shard_map/gather_weights/pallas_call | solution.py:214
  161.9 0.9 copy.60
  162.9 0.1 fusion
  163.0 0.1 slice.33
  163.0 0.1 reshape.156
  163.2 0.7 reshape.178.vec_ref
  163.9 0.7 reshape.160.inner_b
  164.6 0.7 reshape.159.second_b
  165.3 0.7 reshape.158.first_b
  166.0 0.0 copy-done.1
  166.0 0.6 fusion.1
  167.9 30.6 %forward_0.1 = (bf16[2,512,768]{2,1,0:T(8,128)(2,1)}, bf16[512,768]{1,0:T(8,128)(2,1)}, bf16[512,768]{1,0:T(8,128)(2,1)}, bf16[512,768]{1,0:T(8,128)(2,1)}, bf16...) custom-call(s32[1]{0:T(128)S(6)} %select_n.12.length_ref, ...), custom_call_target="tpu_custom_call" | custom-call | tf_op jit(solution)/shard_map/forward_0/pallas_call | solution.py:876
  198.4 51.0 %forward_backward_1.1 = (bf16[2,512,768]{2,1,0:T(8,128)(2,1)}, bf16[2,512,768]{2,1,0:T(8,128)(2,1)}, bf16[2,3072,768]{2,1,0:T(8,128)(2,1)}, bf16[2,768,3072]{2,1...) custom-call(s32[1]{0:T(128)S(6)} %select_n.12.length_ref, ...), custom_call_target="tpu_custom_call", output_to_operand_aliasing={{0}: (1, {})} | custom-call | tf_op jit(solution)/shard_map/forward_backward_1/pallas_call | solution.py:977
  249.4 1.2 dynamic-slice_bitcast_fusion
  250.6 0.6 collective-permute-start
  251.2 44.5 %backward_0.1 = (bf16[2,512,768]{2,1,0:T(8,128)(2,1)}, bf16[2,3072,768]{2,1,0:T(8,128)(2,1)}, bf16[2,768,3072]{2,1,0:T(8,128)(2,1)}, bf16[2,768,768]{2,1,0:T(8,1...) custom-call(bf16[2,512,768]{2,1,0:T(8,128)(2,1)} %get-tuple-element., ...), custom_call_target="tpu_custom_call", output_to_operand_aliasing={{1}: (19, {}), {2}: (20, {}), {3}: (21, {}), {4}: (22, {}),... | custom-call | tf_op jit(solution)/shard_map/backward_0/pallas_call | solution.py:923
  295.7 0.8 copy.52
  296.5 0.1 reshape.161
  296.7 0.1 copy.53
  296.8 0.5 broadcast.27
  297.3 1.4 reduce.6
  298.8 0.1 reshape.166
  298.9 0.8 reduce
  299.7 0.1 reshape.163
  299.8 0.8 slice_reduce_fusion
  300.6 0.1 reshape_squeeze.3
  300.7 0.8 select_maximum_fusion
  301.5 166.6 %sum_gradients.1 = (f32[24,768]{1,0:T(8,128)}, f32[48,3072]{1,0:T(8,128)}, f32[192,512]{1,0:T(8,128)}, f32[48,768]{1,0:T(8,128)}, f32[16,128]{1,0:T(8,128)}, /*i...) custom-call(bf16[2,4,2,2,24,768]{5,4,3,2,1,0:T(8,128)(2,1)} %bitcast.85, ...), custom_call_target="tpu_custom_call" | custom-call | tf_op jit(solution)/shard_map/sum_gradients/pallas_call | solution.py:431
  468.0 0.0 collective-permute-done.refs_2_
  468.0 0.0 copy-start
  468.0 0.9 copy-done
  468.9 6.2 %finish.1 = (bf16[2,512,768]{2,1,0:T(8,128)(2,1)}, bf16[2,512,768]{2,1,0:T(8,128)(2,1)}, f32[48,768]{1,0:T(8,128)}, f32[48,768]{1,0:T(8,128)}, f32[48,3072]{1,0:...) custom-call(bf16[2,512,768]{2,1,0:T(8,128)(2,1)} %get-tuple-element., ...), custom_call_target="tpu_custom_call" | custom-call | tf_op jit(solution)/shard_map/finish/pallas_call | solution.py:403
  (10 shorter events, 0.1 us)
Async XLA Ops:
  2.2 163.8 %copy-start.1 = (s32[2,1]{0,1:T(1,128)S(1)}, s32[2,1]{0,1:T(1,128)}, u32[]{:S(2)}) copy-start(s32[2,1]{0,1:T(1,128)} %param.20) | copy-start | bytes 28
  250.6 217.4 %collective-permute-start = (bf16[512,768]{1,0:T(8,128)(2,1)S(1)}, bf16[512,768]{1,0:T(8,128)(2,1)S(1)}, u32[]{:S(2)}, u32[]{:S(2)}) collective-permute-start(bf16[512,768]{1,0:T(8,128)(2,1)S(1)} %dynamic-slice_bitcast_fusion), channel_id=1, source_target_pairs={{0,16},{16,0},{1,17},{17,1},{2,18},{18,2},{3,19},{19,3},{4,20},{20... | collective-permute-start | bytes 2359304 | tf_op jit(solution)/shard_map/ppermute | solution.py:417
  468.0 0.9 copy-start

commit v5 on v4

--- a/solution.py
+++ b/solution.py
@@ -80,22 +80,43 @@
     pl.semaphore_wait(barrier, len(peers))
 
 
-def block_of(ref, place, c, z, x=None, y=None):
+def part_of(shape, part):
+    rows, cols = shape
+    if part is None:
+        return (slice(0, rows), slice(0, cols))
+    if rows % 32 == 0:
+        return (slice(part * rows // 2, (part + 1) * rows // 2), slice(0, cols))
+    return (slice(0, rows), slice(part * cols // 2, (part + 1) * cols // 2))
+
+
+def part_shape(shape, part):
+    return tuple(cut.stop - cut.start for cut in part_of(shape, part))
+
+
+def block_of(ref, cut, c, z, x=None, y=None):
     xs = pl.ds(0, 2) if x is None else x
     ys = pl.ds(0, 2) if y is None else y
-    return ref.at[xs, z, ys, c]
-
-
-def gather_kernel(plan, nz, *refs):
-    orders, starts = zip(*plan)
-    n = len(orders)
-    far, own, outs, pair, refs = refs[:n], refs[n], refs[n + 1 : 2 * n + 1], refs[2 * n + 1], refs[2 * n + 2 :]
-    raw, ins, (held, send, recv, local, swap, loads) = refs[:n], refs[n : 2 * n], refs[2 * n :]
+    return ref.at[(xs, z, ys, c) + cut]
+
+
+def gather_kernel(plan, nz, small_at, count, *refs):
+    which, parts, orders, starts = zip(*plan)
+    n = max(which) + 1
+    far, vectors, own, refs = refs[: n - 1], refs[n - 1 : n - 1 + count], refs[n - 1 + count], refs[n + count :]
+    whole_outs, pair, raw, whole_ins, refs = refs[:n], refs[n], refs[n + 1 : 2 * n + 1], refs[2 * n + 1 : 3 * n + 1], refs[3 * n + 1 :]
+    near, (held, send, recv, local, swap, loads) = refs[:count], refs[count:]
+    cuts = [part_of(raw[k].shape, part) for k, part in zip(which, parts)]
+    ins = [whole_ins[k].at[cut] for k, cut in zip(which, cuts)]
+    outs = [whole_outs[k] for k in which]
+    ready = set()
     place = Place(nz)
-    loading = [pltpu.make_async_copy(src, dst, loads.at[j]) for j, (src, dst) in enumerate(zip(far, raw))]
-    loading.append(pltpu.make_async_copy(own.at[place.x], held, loads.at[n]))
+    moves = list(zip(vectors, near))
+    moves += list(zip(far, [ref for k, ref in enumerate(raw) if k != small_at])) + [(own.at[place.x], held)]
+    loading = [pltpu.make_async_copy(src, dst, loads.at[j]) for j, (src, dst) in enumerate(moves)]
     for copy in loading:
         copy.start()
+    packing, loading = loading[:count], loading[count:]
+    loading.insert(small_at, None)
     greet(place)
     stays = pltpu.make_async_copy(held, pair.at[place.x], swap.at[0])
     leaves = pltpu.make_async_remote_copy(
@@ -128,15 +149,27 @@
         out, mine = outs[i], copies[i]
 
         def shard(z, **at):
-            return block_of(out, place, place.c, z, **at)
+            return block_of(out, cuts[i], place.c, z, **at)
 
         def own(axis, z):
             return shard(z, **{axis: getattr(place, axis)})
 
         one = shard(place.z, x=place.x, y=place.y)
         if t == 0:
-            loading[i].wait()
-            ins[i][...] = half(raw[i][...])
+            k = which[i]
+            if k not in ready:
+                if k == small_at:
+                    raw[k][...] = jnp.zeros_like(raw[k])
+                    row = 0
+                    for copy, vector in zip(packing, near):
+                        copy.wait()
+                        for r, lo, many in pieces_of(vector.shape[1], row):
+                            raw[k][r : r + 1, :many] = vector[:, lo : lo + many]
+                        row += rows_for(vector.shape[1])
+                else:
+                    loading[k].wait()
+                whole_ins[k][...] = half(raw[k][...])
+                ready.add(k)
             mine["own"] = pltpu.make_async_copy(ins[i], one, local.at[i])
             mine["own"].start()
         if second == "z":
@@ -184,13 +217,13 @@
 
     stages = nz + 2
     for t in range(stages + max(starts)):
-        for i in range(n):
+        for i in range(len(plan)):
             if 0 <= t - starts[i] < stages:
                 stage(i, t - starts[i])
         if t == 0:
             leaves.start()
         if t == 1:
-            loading[n].wait()
+            loading[-1].wait()
             stays.start()
     for mine in copies:
         for key, copy in mine.items():
@@ -202,35 +235,43 @@
     leaves.wait()
 
 
-def gather_all(shards, plan, mesh, own):
+def gather_all(shards, plan, mesh, rows):
     nx, ndp = mesh.shape["segment"], mesh.shape["dp"]
+    small_at = [isinstance(s, list) for s in shards].index(True)
+    vectors = shards[small_at]
     if nx != 2 or ndp != 16:
         first = lax.axis_index("segment") == 0
-        other = lax.ppermute(jnp.where(first, own[1], own[0]), "segment", [(0, 1), (1, 0)])
-        pair = jnp.where(first, jnp.stack([own[0], other]), jnp.stack([other, own[1]]))
+        other = lax.ppermute(jnp.where(first, rows[1], rows[0]), "segment", [(0, 1), (1, 0)])
+        pair = jnp.where(first, jnp.stack([rows[0], other]), jnp.stack([other, rows[1]]))
+        packed = sixteens(jnp.concatenate([lanes(v) for v in vectors]))
+        shards = [packed if j == small_at else s for j, s in enumerate(shards)]
         return [lax.all_gather(half(s), AXES, axis=0) for s in shards], pair
-    nz, n = ndp // 4, len(shards)
+    nz, n, count = ndp // 4, len(shards), len(vectors)
+    height = sum(rows_for(v.size) for v in vectors)
+    shapes = [(height + -height % 16, 128) if j == small_at else s.shape for j, s in enumerate(shards)]
+    far = [s for j, s in enumerate(shards) if j != small_at]
     slots = 5 * nz + 2
     *outs, pair = pl.pallas_call(
-        functools.partial(gather_kernel, plan, nz),
-        out_shape=[jax.ShapeDtypeStruct((2, nz, 2, 2) + s.shape, jnp.bfloat16) for s in shards]
-        + [jax.ShapeDtypeStruct(own.shape, own.dtype)],
-        in_specs=[pl.BlockSpec(memory_space=pl.ANY)] * (n + 1),
+        functools.partial(gather_kernel, plan, nz, small_at, count),
+        out_shape=[jax.ShapeDtypeStruct((2, nz, 2, 2) + s, jnp.bfloat16) for s in shapes]
+        + [jax.ShapeDtypeStruct(rows.shape, rows.dtype)],
+        in_specs=[pl.BlockSpec(memory_space=pl.ANY)] * (n + count),
         out_specs=[pl.BlockSpec(memory_space=pl.ANY)] * (n + 1),
-        scratch_shapes=[pltpu.VMEM(s.shape, s.dtype) for s in shards]
-        + [pltpu.VMEM(s.shape, jnp.bfloat16) for s in shards]
+        scratch_shapes=[pltpu.VMEM(s, jnp.float32) for s in shapes]
+        + [pltpu.VMEM(s, jnp.bfloat16) for s in shapes]
+        + [pltpu.VMEM(v.shape, v.dtype) for v in vectors]
         + [
-            pltpu.VMEM(own.shape[1:], own.dtype),
-            pltpu.SemaphoreType.DMA((n, slots)),
-            pltpu.SemaphoreType.DMA((n, slots)),
-            pltpu.SemaphoreType.DMA((n,)),
+            pltpu.VMEM(rows.shape[1:], rows.dtype),
+            pltpu.SemaphoreType.DMA((len(plan), slots)),
+            pltpu.SemaphoreType.DMA((len(plan), slots)),
+            pltpu.SemaphoreType.DMA((len(plan),)),
             pltpu.SemaphoreType.DMA((3,)),
-            pltpu.SemaphoreType.DMA((n + 1,)),
+            pltpu.SemaphoreType.DMA((n + count,)),
         ],
         compiler_params=pltpu.CompilerParams(collective_id=0, has_side_effects=True, vmem_limit_bytes=62 * 2**20),
         name="gather_weights",
-    )(*shards, own)
-    return [o.reshape((nx * ndp,) + s.shape) for o, s in zip(outs, shards)], pair
+    )(*far, *vectors, rows)
+    return [o.reshape((nx * ndp,) + s) for o, s in zip(outs, shapes)], pair
 
 
 def add_to(dst, src):
@@ -249,10 +290,14 @@
 
 
 def scatter_kernel(plan, nz, *refs):
-    orders, starts = zip(*plan)
-    n = len(orders)
+    which, parts, orders, starts = zip(*plan)
+    n = max(which) + 1
     ins, here, refs = refs[:n], refs[n], refs[n + 1 :]
     outs, there, refs = refs[:n], refs[n], refs[n + 1 :]
+    cuts = [part_of(outs[k].shape, part) for k, part in zip(which, parts)]
+    ins = [ins[k] for k in which]
+    outs = [outs[k].at[cut] for k, cut in zip(which, cuts)]
+    n = len(plan)
     accs, stages, firsts, rings, lasts = (refs[j * n : (j + 1) * n] for j in range(5))
     send, recv, local, swap = refs[5 * n :]
     place = Place(nz)
@@ -284,7 +329,7 @@
 
     def load(i, k):
         copy = pltpu.make_async_copy(
-            block_of(ins[i], place, place.c, place.ring_z(k)), stages[i].at[k % 2], local.at[i, k % 2]
+            block_of(ins[i], cuts[i], place.c, place.ring_z(k)), stages[i].at[k % 2], local.at[i, k % 2]
         )
         copy.start()
         live[i]["o", k] = copy
@@ -306,7 +351,7 @@
 
         if s == 0:
             for k in range(1, nz + 1):
-                src = block_of(ins[i], place, 1 - place.c, place.ring_z(k))
+                src = block_of(ins[i], cuts[i], 1 - place.c, place.ring_z(k))
                 mine["c", k] = put(i, k, src, acc.at[k - 1], place.other("c"))
             load(i, 1)
             load(i, 2)
@@ -424,7 +469,10 @@
     nz, n = ndp // 4, len(grads)
 
     def scratch(lead):
-        return [pltpu.VMEM(lead(o) + g.shape[1:], g.dtype) for (o, _), g in zip(plan, grads)]
+        return [
+            pltpu.VMEM(lead(order) + part_shape(grads[k].shape[1:], part), grads[k].dtype)
+            for k, part, order, _ in plan
+        ]
 
     slots = 4 * nz + 2
     far, near = pl.BlockSpec(memory_space=pl.ANY), pl.BlockSpec(memory_space=pltpu.VMEM)
@@ -440,9 +488,9 @@
         + scratch(lambda o: (nz - 1, 2) if o[1] == "z" else (nz - 1,))
         + scratch(lambda o: () if o[1] == "z" else (nz,))
         + [
-            pltpu.SemaphoreType.DMA((n, slots)),
-            pltpu.SemaphoreType.DMA((n, slots)),
-            pltpu.SemaphoreType.DMA((n, 2)),
+            pltpu.SemaphoreType.DMA((len(plan), slots)),
+            pltpu.SemaphoreType.DMA((len(plan), slots)),
+            pltpu.SemaphoreType.DMA((len(plan), 2)),
             pltpu.SemaphoreType.DMA((2,)),
         ],
         compiler_params=pltpu.CompilerParams(
@@ -456,6 +504,41 @@
 ROWS = 512
 HIDDEN = 768
 GAIN1, BIAS1, VALUE_B, OUT_B, GAIN2, BIAS2, OUTER_B, FIRST_B = range(8)
+VECTOR_ROWS = 7
+
+
+def rows_for(size):
+    return -(-size // 128)
+
+
+def pieces_of(size, row):
+    return [(row + j, j * 128, min(128, size - j * 128)) for j in range(rows_for(size))]
+
+
+def unpack_rows(small, at, ndp, row, ref):
+    size = ref.shape[1] // ndp
+    for d in range(ndp):
+        for r, lo, n in pieces_of(size, row):
+            ref[:, d * size + lo : d * size + lo + n] = wide(small[at + d])[r : r + 1, :n]
+
+
+def unpack_vectors(small, at, ndp, ref):
+    size = ref.shape[1] // ndp
+    for d in range(ndp):
+        ref[:, d * size : (d + 1) * size] = wide(small[at + d])[: ref.shape[0], :size]
+
+
+def pack_rows(ref, ndp, row, small, at):
+    size = ref.shape[1] // ndp
+    for d in range(ndp):
+        for r, lo, n in pieces_of(size, row):
+            small[at + d, r : r + 1, :n] = ref[:, d * size + lo : d * size + lo + n]
+
+
+def pack_vectors(ref, ndp, small, at):
+    size = ref.shape[1] // ndp
+    for d in range(ndp):
+        small[at + d, :VECTOR_ROWS, :size] = ref[:VECTOR_ROWS, d * size : (d + 1) * size]
 
 
 def chunks(rows, size=ROWS):
@@ -539,7 +622,7 @@
     return jnp.concatenate([jnp.where(lower, pair, zero), jnp.where(lower, zero, pair)], axis=0)
 
 
-def forward_heads(pair, length, v_ref, c_ref, probs_ref, logits_of):
+def forward_heads(pair, length, v_ref, c_ref, probs_ref, logits_of, bounded=False):
     rows, width = v_ref.shape
     slots = probs_ref.shape[1] // 2
     head = width // HEADS
@@ -548,7 +631,7 @@
     both = logits_of(shut)
     for h in range(2):
         logits = both[h]
-        expo = jnp.exp(logits - jnp.max(logits, axis=1, keepdims=True))
+        expo = jnp.exp(logits if bounded else logits - jnp.max(logits, axis=1, keepdims=True))
         probs_ref[:, h * slots : (h + 1) * slots] = half(expo * (1.0 / jnp.sum(expo, axis=1, keepdims=True)))
     c_ref[:, at] = half(mm(probs_ref[...], both_heads(v_ref[:, at], head)))
 
@@ -603,17 +686,18 @@
         gc_ref[r] = half(mm_nt(gatt[r], out_ref[...]))
 
 
-def backward_heads(pair, v_ref, gc_ref, gv_ref, probs_ref, db):
+def backward_heads(pair, v_ref, c_ref, gc_ref, gv_ref, probs_ref, db):
     rows, width = v_ref.shape
     slots = probs_ref.shape[1] // 2
     head = width // HEADS
     at = pl.ds(pl.multiple_of(pair * 2 * head, 2 * head), 2 * head)
     both = mm_nt(gc_ref[:, at], both_heads(v_ref[:, at], head))
+    along = wide(gc_ref[:, at]) * wide(c_ref[:, at])
+    lower = masked_pair(head)
     for h in range(2):
         cols = slice(h * slots, (h + 1) * slots)
-        probs = wide(probs_ref[:, cols])
-        weighed = probs * both[:, cols]
-        db[:, cols] = half(weighed - probs * jnp.sum(weighed, axis=1, keepdims=True))
+        mean = jnp.sum(jnp.where(lower if h == 0 else jnp.logical_not(lower), along, 0.0), axis=1, keepdims=True)
+        db[:, cols] = half(wide(probs_ref[:, cols]) * (both[:, cols] - mean))
     values = mm_tn(probs_ref[...], gc_ref[:, at])
     gv_ref[:, at] = half(jnp.where(masked_pair(head), values[:slots], values[slots:]))
 
@@ -644,16 +728,17 @@
     put(BIAS1, shift)
 
 
-def forward_kernel(pairs, parts, length_ref, x_ref, vec_ref, value_ref, out_ref, first_ref, first_b, second_ref, second_b, inner_ref, inner_b, outer_ref, y_ref, *refs):
+def forward_kernel(pairs, parts, length_ref, x_ref, small, value_ref, out_ref, first_ref, second_ref, inner_ref, outer_ref, y_ref, *refs):
     kept, probs_ref, q_ref, slope_ref = refs[:7], refs[7], refs[8], refs[9]
-    a_ref, v_ref, p_ref, first_slope, c_ref, b_ref, hid_ref, acc, sem = refs[10:]
+    a_ref, v_ref, p_ref, first_slope, c_ref, b_ref, hid_ref, acc, vectors, inner_b, first_b, second_b, sem = refs[10:]
     held = (a_ref, v_ref, p_ref, first_slope, c_ref, b_ref, hid_ref)
     copies = [pltpu.make_async_copy(src, dst, sem.at[j]) for j, (src, dst) in enumerate(zip(held, kept))]
     i = pl.program_id(0)
     slots = probs_ref.shape[2] // 2
+    ndp, part = small.shape[0] // 2, q_ref.shape[1]
 
     def vec(k):
-        return vec_ref[0, k : k + 1, :]
+        return vectors[k : k + 1, :]
 
     x_ref, y_ref = x_ref.at[0], y_ref.at[0]
 
@@ -662,6 +747,11 @@
 
     @pl.when(i == 0)
     def _():
+        unpack_vectors(small, 0, ndp, vectors)
+        unpack_rows(small, 0, ndp, VECTOR_ROWS, inner_b)
+        row = VECTOR_ROWS + rows_for(inner_b.shape[1] // ndp)
+        unpack_rows(small, 0, 2 * ndp, row, first_b)
+        unpack_rows(small, 0, 2 * ndp, row + rows_for(first_b.shape[1] // (2 * ndp)), second_b)
         forward_start(read, vec, value_ref.at[0], a_ref, v_ref, (first_ref, first_b, p_ref, first_slope))
         for copy in copies[:4]:
             copy.start()
@@ -669,7 +759,8 @@
     @pl.when(i < pairs)
     def _():
         def logits_of(shut):
-            logits = mm(p_ref[...], second_ref[...]) + (second_b[...] + jnp.concatenate([shut, shut], axis=1))
+            bias = second_b[:, pl.ds(pl.multiple_of(i * 2 * slots, 2 * slots), 2 * slots)]
+            logits = mm(p_ref[...], second_ref[...]) + (bias + jnp.concatenate([shut, shut], axis=1))
             return logits[:, :slots], logits[:, slots:]
 
         forward_heads(i, length_ref[0], v_ref, c_ref, probs_ref.at[0], logits_of)
@@ -682,7 +773,8 @@
 
     @pl.when(i >= pairs)
     def _():
-        forward_hidden(i == pairs, b_ref, inner_ref.at[0], inner_b[0], outer_ref.at[0], q_ref, slope_ref, acc)
+        bias = inner_b[:, pl.ds(pl.multiple_of((i - pairs) * part, part), part)]
+        forward_hidden(i == pairs, b_ref, inner_ref.at[0], bias, outer_ref.at[0], q_ref, slope_ref, acc)
 
     @pl.when(i == pairs + parts - 1)
     def _():
@@ -691,32 +783,35 @@
             copy.wait()
 
 
-def backward_kernel(pairs, parts, g_ref, b_ref, vec_ref, q_ref, slope_ref, probs_ref, inner_ref, outer_ref, second_ref, *refs):
-    far, refs = refs[:10], refs[16:]
-    gx_ref, g_outer, g_inner, g_out, g_value, g_vec, g_inner_b, g_first, g_second, g_second_b = refs[:10]
-    near, refs = refs[10:20], refs[20:]
-    acc, ghid, gatt, gc_ref, gv_ref, db, gz_ref, sem = refs
+def backward_kernel(pairs, parts, g_ref, b_ref, small, g_small1, q_ref, slope_ref, probs_ref, inner_ref, outer_ref, second_ref, *refs):
+    far, refs = refs[:10], refs[14:]
+    gx_ref, g_outer, g_inner, g_out, g_value, g_small, g_first, g_second = refs[:8]
+    near, refs = refs[8:18], refs[18:]
+    acc, ghid, gatt, gc_ref, gv_ref, db, gz_ref, vectors, g_vec, g_inner_b, g_second_b, sem = refs
     far = [ref.at[0] if len(ref.shape) == 3 else ref for ref in far]
     copies = [pltpu.make_async_copy(src, dst, sem.at[j]) for j, (src, dst) in enumerate(zip(far, near))]
     hid_ref, c_ref, out_ref, v_ref, p_ref, a_ref, value_ref, first_ref, first_slope, x_ref = near
     g_ref, gx_ref = g_ref.at[0], gx_ref.at[0]
     i = pl.program_id(0)
     slots = probs_ref.shape[2] // 2
+    ndp, part = small.shape[0] // 2, q_ref.shape[1]
 
     def vec(k):
-        return vec_ref[0, k : k + 1, :]
+        return vectors[k : k + 1, :]
 
     def put(k, value):
-        g_vec[0, k : k + 1, :] = value
+        g_vec[k : k + 1, :] = value
 
     @pl.when(i == 0)
     def _():
         for copy in copies:
             copy.start()
+        unpack_vectors(small, 0, ndp, vectors)
 
     @pl.when(i < parts)
     def _():
-        backward_hidden(i == 0, g_ref, b_ref, q_ref, slope_ref, inner_ref.at[0], outer_ref.at[0], gz_ref, acc, g_outer.at[0], g_inner.at[0], g_inner_b.at[0])
+        bias = g_inner_b.at[:, pl.ds(pl.multiple_of(i * part, part), part)]
+        backward_hidden(i == 0, g_ref, b_ref, q_ref, slope_ref, inner_ref.at[0], outer_ref.at[0], gz_ref, acc, g_outer.at[0], g_inner.at[0], bias)
 
     @pl.when(i == parts - 1)
     def _():
@@ -728,9 +823,9 @@
 
     @pl.when(i >= parts)
     def _():
-        backward_heads(i - parts, v_ref, gc_ref, gv_ref, probs_ref.at[0], db)
+        backward_heads(i - parts, v_ref, c_ref, gc_ref, gv_ref, probs_ref.at[0], db)
         g_second[...] = half(mm_tn(p_ref[...], db[...]))
-        g_second_b[...] = sums(db[...])
+        g_second_b[:, pl.ds(pl.multiple_of((i - parts) * 2 * slots, 2 * slots), 2 * slots)] = sums(db[...])
         add_up(i == parts, acc, slice(None), mm_nt(db[...], second_ref[...]))
 
     @pl.when(i == pairs + parts - 1)
@@ -741,22 +836,36 @@
             vec, put, lambda r: wide(x_ref[r, :]), gv_ref, value_ref, a_ref, acc, ghid, g_value.at[0], gx_ref,
             (first_ref, first_slope, gatt, g_first),
         )
-
-
-def both_kernel(pairs, parts, length_ref, x_ref, g_ref, vec_ref, value_ref, out_ref, table_ref, inner_ref, inner_b, outer_ref, *refs):
-    y_ref, gx_ref, g_outer, g_inner, g_out, g_value, g_vec, g_inner_b, g_table = refs[:9]
-    acc, hid_ref, ghid, a_ref, v_ref, c_ref, b_ref, gatt, gc_ref, gv_ref, probs_ref, q_ref, slope_ref, db, gz_ref = refs[9:]
+        g_small[:ndp] = jnp.zeros_like(g_small1)
+        g_small[ndp:] = g_small1[...]
+        pack_vectors(g_vec, ndp, g_small, 0)
+        pack_rows(g_inner_b, ndp, VECTOR_ROWS, g_small, 0)
+        row = VECTOR_ROWS + rows_for(g_inner_b.shape[1] // ndp)
+        pack_rows(g_vec.at[FIRST_B : FIRST_B + 1, :], 2 * ndp, row, g_small, 0)
+        row += rows_for(g_vec.shape[1] // (2 * ndp))
+        pack_rows(g_second_b, 2 * ndp, row, g_small, 0)
+
+
+def both_kernel(pairs, parts, length_ref, x_ref, g_ref, small, value_ref, out_ref, table_ref, inner_ref, outer_ref, *refs):
+    y_ref, gx_ref, g_outer, g_inner, g_out, g_value, g_small, g_table = refs[:8]
+    acc, hid_ref, ghid, a_ref, v_ref, c_ref, b_ref, gatt, gc_ref, gv_ref, probs_ref, q_ref, slope_ref, db, gz_ref, *refs = refs[8:]
+    vectors, inner_b, g_vec, g_inner_b = refs
     i = pl.program_id(0)
     slots = probs_ref.shape[2] // 2
     j = i - pairs
     k = j - parts
     n = k - parts
 
+    ndp, part = small.shape[0] // 2, q_ref.shape[2]
+
     def vec(k):
-        return vec_ref[0, k : k + 1, :]
+        return vectors[k : k + 1, :]
 
     def put(k, value):
-        g_vec[0, k : k + 1, :] = value
+        g_vec[k : k + 1, :] = value
+
+    def hidden(ref, k):
+        return ref.at[:, pl.ds(pl.multiple_of(k * part, part), part)]
 
     x_ref, g_ref, y_ref, gx_ref = (ref.at[0] for ref in (x_ref, g_ref, y_ref, gx_ref))
 
@@ -765,6 +874,8 @@
 
     @pl.when(i == 0)
     def _():
+        unpack_vectors(small, ndp, ndp, vectors)
+        unpack_rows(small, ndp, ndp, VECTOR_ROWS, inner_b)
         forward_start(read, vec, value_ref.at[0], a_ref, v_ref)
 
     @pl.when(i < pairs)
@@ -772,7 +883,7 @@
         def logits_of(shut):
             return wide(table_ref[:slots, :]) + shut, wide(table_ref[slots:, :]) + shut
 
-        forward_heads(i, length_ref[0], v_ref, c_ref, probs_ref.at[i], logits_of)
+        forward_heads(i, length_ref[0], v_ref, c_ref, probs_ref.at[i], logits_of, True)
 
     @pl.when(i == pairs - 1)
     def _():
@@ -780,7 +891,7 @@
 
     @pl.when((j >= 0) & (j < parts))
     def _():
-        forward_hidden(j == 0, b_ref, inner_ref.at[0], inner_b[0], outer_ref.at[0], q_ref.at[j], slope_ref.at[j], acc)
+        forward_hidden(j == 0, b_ref, inner_ref.at[0], hidden(inner_b, j)[...], outer_ref.at[0], q_ref.at[j], slope_ref.at[j], acc)
 
     @pl.when(j == parts - 1)
     def _():
@@ -789,7 +900,7 @@
     @pl.when((k >= 0) & (k < parts))
     def _():
         at = parts - 1 - k
-        backward_hidden(k == 0, g_ref, b_ref, q_ref.at[at], slope_ref.at[at], inner_ref.at[0], outer_ref.at[0], gz_ref, acc, g_outer.at[0], g_inner.at[0], g_inner_b.at[0])
+        backward_hidden(k == 0, g_ref, b_ref, q_ref.at[at], slope_ref.at[at], inner_ref.at[0], outer_ref.at[0], gz_ref, acc, g_outer.at[0], g_inner.at[0], hidden(g_inner_b, at))
 
     @pl.when(k == parts - 1)
     def _():
@@ -797,26 +908,26 @@
 
     @pl.when(n >= 0)
     def _():
-        backward_heads(n, v_ref, gc_ref, gv_ref, probs_ref.at[n], db)
+        backward_heads(n, v_ref, c_ref, gc_ref, gv_ref, probs_ref.at[n], db)
         g_table[:slots, :] = db[:, :slots]
         g_table[slots:, :] = db[:, slots:]
 
     @pl.when(n == pairs - 1)
     def _():
         backward_end(vec, put, read, gv_ref, value_ref.at[0], a_ref, acc, ghid, g_value.at[0], gx_ref)
+        g_small[...] = jnp.zeros_like(g_small)
+        pack_vectors(g_vec, ndp, g_small, 0)
+        pack_rows(g_inner_b, ndp, VECTOR_ROWS, g_small, 0)
 
 
 class Weights(NamedTuple):
-    vectors: Any
+    small: Any
     value: Any
     out: Any
     inner: Any
-    inner_b: Any
     outer: Any
     first: Any
-    first_b: Any
     second: Any
-    second_b: Any
     table: Any
 
 
@@ -855,19 +966,16 @@
     def piece(i):
         return jnp.maximum(i - pairs, 0)
 
-    ins = [length, x, w.vectors, w.value, w.out, w.first, w.first_b, w.second, w.second_b, w.inner, w.inner_b, w.outer]
+    ins = [length, x, w.small, w.value, w.out, w.first, w.second, w.inner, w.outer]
     specs = [
         pl.BlockSpec(memory_space=pltpu.SMEM),
         whole(x.shape, 0),
-        whole(w.vectors.shape, 0),
+        whole(w.small.shape),
         whole(w.value.shape, 0),
         whole(w.out.shape, 0),
         whole(w.first.shape),
-        whole(w.first_b.shape),
         pl.BlockSpec((width, 2 * slots), lambda i: (0, pair(i))),
-        pl.BlockSpec((1, 2 * slots), lambda i: (0, pair(i))),
         pl.BlockSpec((1, width, part), lambda i: (0, 0, piece(i))),
-        pl.BlockSpec((1, 1, part), lambda i: (0, 0, piece(i))),
         pl.BlockSpec((1, part, width), lambda i: (0, piece(i), 0)),
     ]
     half_rows = like((rows, width))
@@ -883,14 +991,21 @@
         + [pl.BlockSpec((1, rows, 2 * slots), lambda i: (pair(i), 0, 0))]
         + [hidden_block] * 2,
         scratch_shapes=[pltpu.VMEM(k.shape, k.dtype) for k in kept]
-        + [pltpu.VMEM((rows, width), jnp.float32), pltpu.SemaphoreType.DMA((7,))],
+        + [
+            pltpu.VMEM((rows, width), jnp.float32),
+            pltpu.VMEM((8, width), jnp.float32),
+            pltpu.VMEM((1, part * parts), jnp.float32),
+            pltpu.VMEM((1, width), jnp.float32),
+            pltpu.VMEM((1, w.second.shape[1]), jnp.float32),
+            pltpu.SemaphoreType.DMA((7,)),
+        ],
         compiler_params=pltpu.CompilerParams(vmem_limit_bytes=62 * 2**20),
         name="forward_0",
     )(*ins)
     return y, saved
 
 
-def backward(g, x, saved, w, before):
+def backward(g, x, saved, w, before, small1):
     rows, width, pairs, parts, part = sizes_of(x, w)
     slots = rows
     a, v, p, first_slope, c, b, hid, probs, q, slope = saved
@@ -906,20 +1021,19 @@
     outer_block = pl.BlockSpec((1, part, width), lambda i: (0, piece(i), 0))
     second_block = pl.BlockSpec((width, 2 * slots), lambda i: (0, pair(i)))
     far = [hid, c, w.out, v, p, a, w.value, w.first, first_slope, x]
-    ins = [g, b, w.vectors, q, slope, probs, w.inner, w.outer, w.second] + far
-    specs = [whole(g.shape, 1), whole((rows, width)), whole(w.vectors.shape, 0)] + [hidden_block] * 2
+    ins = [g, b, w.small, small1, q, slope, probs, w.inner, w.outer, w.second] + far
+    specs = [whole(g.shape, 1), whole((rows, width)), whole(w.small.shape), whole(small1.shape)] + [hidden_block] * 2
     specs += [pl.BlockSpec((1, rows, 2 * slots), lambda i: (pair(i), 0, 0)), inner_block, outer_block, second_block]
     specs += [FAR] * 10
-    aliases = {len(ins) + j: 1 + j for j in range(6)}
+    aliases = {len(ins) + j: 1 + j for j in range(4)}
     aliases[0] = 0
     ins += list(before)
-    specs += [FAR] * 6
+    specs += [FAR] * 4
     outs = [like(g.shape)] + [like(k.shape, k.dtype) for k in before]
     out_specs = [whole_out(g.shape, 0), outer_block, inner_block]
-    out_specs += [whole_out(w.out.shape, 0), whole_out(w.value.shape, 0), whole_out((2, 8, width), 0)]
-    out_specs += [pl.BlockSpec((1, 1, part), lambda i: (0, 0, piece(i)))]
-    outs += [like(w.first.shape), like(w.second.shape), like(w.second_b.shape, jnp.float32)]
-    out_specs += [whole_out(w.first.shape), second_block, pl.BlockSpec((1, 2 * slots), lambda i: (0, pair(i)))]
+    out_specs += [whole_out(w.out.shape, 0), whole_out(w.value.shape, 0)]
+    outs += [like(w.small.shape, jnp.float32), like(w.first.shape), like(w.second.shape)]
+    out_specs += [whole_out(w.small.shape), whole_out(w.first.shape), second_block]
     gx, *grads = pl.pallas_call(
         functools.partial(backward_kernel, pairs, parts),
         grid=(pairs + parts,),
@@ -929,12 +1043,15 @@
         scratch_shapes=[pltpu.VMEM(k.shape[-2:], k.dtype) for k in far]
         + [pltpu.VMEM((rows, width), jnp.float32)] * 2
         + [pltpu.VMEM((rows, width), jnp.bfloat16)] * 3
-        + [pltpu.VMEM((rows, 2 * slots), jnp.bfloat16), pltpu.VMEM((rows, part), jnp.bfloat16), pltpu.SemaphoreType.DMA((10,))],
+        + [pltpu.VMEM((rows, 2 * slots), jnp.bfloat16), pltpu.VMEM((rows, part), jnp.bfloat16)]
+        + [pltpu.VMEM((8, width), jnp.float32)] * 2
+        + [pltpu.VMEM((1, part * parts), jnp.float32), pltpu.VMEM((1, w.second.shape[1]), jnp.float32)]
+        + [pltpu.SemaphoreType.DMA((10,))],
         input_output_aliases=aliases,
         compiler_params=pltpu.CompilerParams(vmem_limit_bytes=62 * 2**20),
         name="backward_0",
     )(*ins)
-    return gx, grads[:6], grads[6:]
+    return gx, grads[:4], grads[4:]
 
 
 def both_ways(x, g, length, w):
@@ -954,24 +1071,23 @@
     def late(i):
         return parts - 1 - jnp.clip(i - pairs - parts, 0, parts - 1)
 
-    ins = [length, x, g, w.vectors, w.value, w.out, w.table, w.inner, w.inner_b, w.outer]
+    ins = [length, x, g, w.small, w.value, w.out, w.table, w.inner, w.outer]
     specs = [pl.BlockSpec(memory_space=pltpu.SMEM), whole(x.shape, 0), whole(g.shape, 1)]
-    specs += [whole(w.vectors.shape, 1), whole(w.value.shape, 1), whole(w.out.shape, 1)]
+    specs += [whole(w.small.shape), whole(w.value.shape, 1), whole(w.out.shape, 1)]
     specs += [
         pl.BlockSpec((2 * slots, slots), lambda i: (there(i), 0)),
         pl.BlockSpec((1, width, part), lambda i: (1, 0, piece(i))),
-        pl.BlockSpec((1, 1, part), lambda i: (1, 0, piece(i))),
         pl.BlockSpec((1, part, width), lambda i: (1, piece(i), 0)),
     ]
     grads = [like(w.outer.shape), like(w.inner.shape), like(w.out.shape), like(w.value.shape)]
-    grads += [like((2, 8, width), jnp.float32), like(w.inner_b.shape, jnp.float32), like(w.table.shape)]
+    small = (w.small.shape[0] // 2,) + w.small.shape[1:]
+    grads += [like(small, jnp.float32), like(w.table.shape)]
     grad_specs = [
         pl.BlockSpec((1, part, width), lambda i: (1, late(i), 0)),
         pl.BlockSpec((1, width, part), lambda i: (1, 0, late(i))),
         whole_out(w.out.shape, 1),
         whole_out(w.value.shape, 1),
-        whole_out((2, 8, width), 1),
-        pl.BlockSpec((1, 1, part), lambda i: (1, 0, late(i))),
+        whole_out(small),
         pl.BlockSpec((2 * slots, slots), lambda i: (back(i), 0)),
     ]
     y, gx, *grads = pl.pallas_call(
@@ -984,12 +1100,13 @@
         + [pltpu.VMEM((rows, width), jnp.bfloat16)] * 7
         + [pltpu.VMEM((pairs, rows, 2 * slots), jnp.bfloat16)]
         + [pltpu.VMEM((parts, rows, part), jnp.bfloat16)] * 2
-        + [pltpu.VMEM((rows, 2 * slots), jnp.bfloat16), pltpu.VMEM((rows, part), jnp.bfloat16)],
+        + [pltpu.VMEM((rows, 2 * slots), jnp.bfloat16), pltpu.VMEM((rows, part), jnp.bfloat16)]
+        + [pltpu.VMEM((8, width), jnp.float32), pltpu.VMEM((1, part * parts), jnp.float32)] * 2,
         input_output_aliases={1: 0},
         compiler_params=pltpu.CompilerParams(vmem_limit_bytes=62 * 2**20),
         name="forward_backward_1",
     )(*ins)
-    return y, gx, grads[:6], grads[6]
+    return y, gx, grads[:4], grads[4], grads[5]
 
 
 ROW_VECTORS = (0, 1, 3, 5, 6, 7, 11)
@@ -997,36 +1114,49 @@
 MATRICES = (2, 4, 8, 10, 12, 14, 16)
 SMALL = 17
 GATHER = (
-    (8, "zyx", 1),
-    (10, "yzx", 1),
-    (16, "xzy", 0),
-    (14, "xzy", 1),
-    (SMALL, "xzy", 0),
-    (12, "zyx", 0),
-    (4, "zxy", 0),
-    (2, "zxy", 0),
+    (8, 0, "xzy", 2),
+    (SMALL, None, "xzy", 3),
+    (10, 1, "zyx", 1),
+    (2, None, "zyx", 0),
+    (16, 0, "zxy", 1),
+    (10, 0, "yzx", 2),
+    (12, None, "zyx", 0),
+    (16, 1, "xzy", 0),
+    (8, 1, "yzx", 2),
+    (4, None, "zyx", 0),
+    (14, 0, "xzy", 2),
+    (14, 1, "xzy", 0),
 )
 SUM = (
-    (12, "yzx", 2),
-    (8, "xzy", 2),
-    (16, "xzy", 4),
-    (4, "yzx", 0),
-    (SMALL, "yzx", 1),
-    (2, "yzx", 0),
-    (14, "yxz", 4),
-    (10, "yxz", 2),
+    (8, 1, "yzx", 3),
+    (8, 0, "xzy", 4),
+    (4, None, "yzx", 1),
+    (14, 1, "yxz", 4),
+    (16, 0, "xzy", 3),
+    (12, None, "yzx", 0),
+    (10, 1, "yxz", 4),
+    (2, None, "yzx", 1),
+    (SMALL, None, "xzy", 4),
+    (16, 1, "xzy", 1),
+    (14, 0, "yxz", 4),
+    (10, 0, "xzy", 3),
 )
 
 
 def planned(call, plan, arrays, mesh, rows):
-    got, rows = call([arrays[k] for k, _, _ in plan], [entry[1:] for entry in plan], mesh, rows)
-    return {k: g for (k, _, _), g in zip(plan, got)}, rows
-
-
-def lanes(array):
-    n, size = array.shape
-    rows = -(-size // 128)
-    return jnp.pad(array, ((0, 0), (0, rows * 128 - size))).reshape(n, rows, 128)
+    names = list(dict.fromkeys(entry[0] for entry in plan))
+    plan = [(names.index(entry[0]),) + entry[1:] for entry in plan]
+    got, rows = call([arrays[k] for k in names], plan, mesh, rows)
+    return dict(zip(names, got)), rows
+
+
+def lanes(vector):
+    rows = rows_for(vector.size)
+    return jnp.pad(vector.reshape(-1), (0, rows * 128 - vector.size)).reshape(rows, 128)
+
+
+def sixteens(rows):
+    return jnp.pad(rows, ((0, -rows.shape[0] % 16), (0, 0)))
 
 
 def per_device(mesh, boundary, lengths, *parts):
@@ -1037,48 +1167,23 @@
     sizes = [parts[k].size for k in VECTORS]
 
     shards = {k: parts[k].reshape(parts[k].shape[-2:]) for k in MATRICES}
-    flat = jnp.concatenate([parts[k].reshape(-1) for k in VECTORS])
-    rows = -(-flat.size // 2048) * 16
-    shards[SMALL] = jnp.pad(flat, (0, rows * 128 - flat.size)).reshape(rows, 128)
+    shards[SMALL] = [parts[k].reshape(1, -1) for k in VECTORS]
     full, pair = planned(gather_all, GATHER, shards, mesh, boundary[0, :, 0])
     for k in MATRICES:
         g = full[k]
         full[k] = g.reshape((nx, ndp * g.shape[1]) + g.shape[2:]) if k < 12 else g.reshape(-1, g.shape[2])
-    vec = wide(full[SMALL].reshape(devices, rows * 128))
-    count, size = len(ROW_VECTORS), sizes[0]
-    bounds = [count * size]
-    for k in VECTORS[count:]:
-        bounds.append(bounds[-1] + parts[k].size)
-    vectors = vec[:, : bounds[0]].reshape(nx, ndp, count, size).transpose(0, 2, 1, 3).reshape(nx, count, -1)
-    inner_b, first_b, second_b = (vec[:, lo:hi] for lo, hi in zip(bounds, bounds[1:]))
-    w = Weights(
-        vectors,
-        full[2],
-        full[4],
-        full[8],
-        inner_b.reshape(nx, 1, -1),
-        full[10],
-        full[12],
-        first_b.reshape(1, -1),
-        full[14],
-        second_b.reshape(1, -1),
-        full[16],
-    )
+    w = Weights(full[SMALL], full[2], full[4], full[8], full[10], full[12], full[14], full[16])
 
     outs, saved = forward(pair, length, w)
-    outs, gins, both, g_table = both_ways(outs, pair, length, w)
+    outs, gins, both, g_small, g_table = both_ways(outs, pair, length, w)
     other_outs = from_other(outs)
-    gins, both, synth = backward(gins, pair, saved, w, both)
-
-    g_outer, g_inner, g_out, g_value, g_vec, g_inner_b = both
-    g_first, g_second, g_second_b = synth
+    gins, both, synth = backward(gins, pair, saved, w, both, g_small)
+
+    g_outer, g_inner, g_out, g_value = both
+    g_small, g_first, g_second = synth
     matrices = (g_value, g_out, g_inner, g_outer, g_first, g_second, g_table)
     grads = {k: g.reshape((devices,) + parts[k].shape[-2:]) for k, g in zip(MATRICES, matrices)}
-    vec = g_vec[:, :count].reshape(nx, count, ndp, size).transpose(0, 2, 1, 3).reshape(devices * count, size)
-    vec = [lanes(vec).reshape(devices, -1, 128)]
-    vec += [lanes(g.reshape(devices, -1)) for g in (g_inner_b, g_vec[0, FIRST_B], g_second_b)]
-    vec = jnp.concatenate(vec, axis=1)
-    grads[SMALL] = jnp.pad(vec, ((0, 0), (0, -vec.shape[1] % 16), (0, 0)))
+    grads[SMALL] = g_small
     summed, other_gins = planned(scatter_all, SUM, grads, mesh, gins)
     arrays, vectors = finish([outs, gins], [other_outs, other_gins], [summed[k] for k in MATRICES], summed[SMALL], sizes)
     result = {k: g.reshape(parts[k].shape) for k, g in zip(MATRICES, arrays[2:])}

time: 476 us -> 457 us (0.960)
  Pallas kernels: 459 us -> 451 us
  local copies, waits for them, and re-layouts: 10.8 us -> 3.38 us
    pallas_call x1, Pallas kernels: 167 us -> 160 us  [scatter_all(): pl.pallas_call(functools.partial(scatter_kernel, plan, nz), out_shape=[ja...]
  transfers between devices with their start and end apart: 1 -> 1, of which waited for: 0 -> 0; matrix products, arithmetic and copies ran while one was open for 1% -> 0% of each run, Pallas kernels for 44% -> 45%
where the time goes in v5:
time: 457 us
  Pallas kernels  451 us (99%)
    pallas_call x1, Pallas kernels, gather_all(): pl.pallas_call(functools.partial(gather_kernel, plan, nz, small_at, count...  160 us
    pallas_call x1, Pallas kernels, scatter_all(): pl.pallas_call(functools.partial(scatter_kernel, plan, nz), out_shape=[ja...  160 us
    pallas_call x1, Pallas kernels, both_ways(): pl.pallas_call(functools.partial(both_kernel, pairs, parts), grid=(2 * pa...  49.7 us
    pallas_call x1, Pallas kernels, backward(): pl.pallas_call(functools.partial(backward_kernel, pairs, parts), grid=(pa...  44.1 us
    pallas_call x1, Pallas kernels, forward(): pl.pallas_call(functools.partial(forward_kernel, pairs, parts), grid=(pai...  30.4 us
  transfers between devices with their start and end apart: 1, of which 0 were waited for; matrix products, arithmetic and copies ran while one was open for 0% of the time, Pallas kernels for 45%

profile of v5, /device:TPU:0, one launch (start us, length us, event | category | flops | bytes accessed | tf_op | source)
XLA Modules:
  0.0 457.0 jit_solution(5730449612298558448)
XLA Ops:
  0.7 1.3 fusion
  3.3 160.5 %gather_weights.1 = (bf16[2,4,2,2,48,3072]{5,4,3,2,1,0:T(8,128)(2,1)}, bf16[2,4,2,2,16,128]{5,4,3,2,1,0:T(8,128)(2,1)}, bf16[2,4,2,2,192,768]{5,4,3,2,1,0:T(8,12...) custom-call(f32[48,3072]{1,0:T(8,128)} %bitcast.68, ...), custom_call_target="tpu_custom_call" | custom-call | tf_op jit(solution)/shard_map/gather_weights/pallas_call | solution.py:254
  163.8 30.4 %forward_0.1 = (bf16[2,512,768]{2,1,0:T(8,128)(2,1)}, bf16[512,768]{1,0:T(8,128)(2,1)}, bf16[512,768]{1,0:T(8,128)(2,1)}, bf16[512,768]{1,0:T(8,128)(2,1)}, bf16...) custom-call(s32[1]{0:T(128)S(6)} %select_n.12.length_ref, ...), custom_call_target="tpu_custom_call" | custom-call | tf_op jit(solution)/shard_map/forward_0/pallas_call | solution.py:984
  194.2 49.7 %forward_backward_1.1 = (bf16[2,512,768]{2,1,0:T(8,128)(2,1)}, bf16[2,512,768]{2,1,0:T(8,128)(2,1)}, bf16[2,3072,768]{2,1,0:T(8,128)(2,1)}, bf16[2,768,3072]{2,1...) custom-call(s32[1]{0:T(128)S(6)} %select_n.12.length_ref, ...), custom_call_target="tpu_custom_call", output_to_operand_aliasing={{0}: (1, {})} | custom-call | tf_op jit(solution)/shard_map/forward_backward_1/pallas_call | solution.py:1093
  243.9 1.2 dynamic-slice_bitcast_fusion
  245.1 0.6 collective-permute-start
  245.7 44.1 %backward_0.1 = (bf16[2,512,768]{2,1,0:T(8,128)(2,1)}, bf16[2,3072,768]{2,1,0:T(8,128)(2,1)}, bf16[2,768,3072]{2,1,0:T(8,128)(2,1)}, bf16[2,768,768]{2,1,0:T(8,1...) custom-call(bf16[2,512,768]{2,1,0:T(8,128)(2,1)} %get-tuple-element., ...), custom_call_target="tpu_custom_call", output_to_operand_aliasing={{1}: (20, {}), {2}: (21, {}), {3}: (22, {}), {4}: (23, {}),... | custom-call | tf_op jit(solution)/shard_map/backward_0/pallas_call | solution.py:1037
  289.7 159.9 %sum_gradients.1 = (f32[48,3072]{1,0:T(8,128)}, f32[48,768]{1,0:T(8,128)}, f32[24,6144]{1,0:T(8,128)}, f32[192,512]{1,0:T(8,128)}, f32[24,768]{1,0:T(8,128)}, /*...) custom-call(bf16[2,4,2,2,48,3072]{5,4,3,2,1,0:T(8,128)(2,1)} %bitcast.49, ...), custom_call_target="tpu_custom_call" | custom-call | tf_op jit(solution)/shard_map/sum_gradients/pallas_call | solution.py:479
  449.7 0.0 collective-permute-done.refs_2_
  449.7 0.0 copy-start
  449.7 0.9 copy-done
  450.6 6.2 %finish.1 = (bf16[2,512,768]{2,1,0:T(8,128)(2,1)}, bf16[2,512,768]{2,1,0:T(8,128)(2,1)}, f32[48,768]{1,0:T(8,128)}, f32[48,768]{1,0:T(8,128)}, f32[48,3072]{1,0:...) custom-call(bf16[2,512,768]{2,1,0:T(8,128)(2,1)} %get-tuple-element., ...), custom_call_target="tpu_custom_call" | custom-call | tf_op jit(solution)/shard_map/finish/pallas_call | solution.py:448
Async XLA Ops:
  245.1 204.6 %collective-permute-start = (bf16[512,768]{1,0:T(8,128)(2,1)S(1)}, bf16[512,768]{1,0:T(8,128)(2,1)S(1)}, u32[]{:S(2)}, u32[]{:S(2)}) collective-permute-start(bf16[512,768]{1,0:T(8,128)(2,1)S(1)} %dynamic-slice_bitcast_fusion), channel_id=1, source_target_pairs={{0,16},{16,0},{1,17},{17,1},{2,18},{18,2},{3,19},{19,3},{4,20},{20... | collective-permute-start | bytes 2359304 | tf_op jit(solution)/shard_map/ppermute | solution.py:462
  449.7 0.9 copy-start

commit v6 on v5

--- a/solution.py
+++ b/solution.py
@@ -46,6 +46,7 @@
         self.z = d // 4
         par = self.z % 2
         self.q = par * ((self.z + 1) // 2) + (1 - par) * ((nz - self.z // 2) % nz)
+        self.places = [self.z_at((self.q + 2 * nz - back) % nz) for back in range(nz + 1)]
 
     def z_at(self, q):
         nz = self.nz
@@ -53,7 +54,7 @@
         return (1 - upper) * (2 * q - 1) + upper * ((2 * (nz - q)) % (2 * nz))
 
     def ring_z(self, back):
-        return self.z_at((self.q + 2 * self.nz - back) % self.nz)
+        return self.places[back]
 
     def device(self, x=None, z=None, y=None, c=None):
         x = self.x if x is None else x
@@ -289,30 +290,17 @@
         dst[...] = dst[...] + src[...]
 
 
-def scatter_kernel(plan, nz, *refs):
-    which, parts, orders, starts = zip(*plan)
-    n = max(which) + 1
-    ins, here, refs = refs[:n], refs[n], refs[n + 1 :]
-    outs, there, refs = refs[:n], refs[n], refs[n + 1 :]
+def sum_rounds(plan, place, nz, ins, outs, refs):
+    which, parts, orders, starts, only = zip(*plan)
     cuts = [part_of(outs[k].shape, part) for k, part in zip(which, parts)]
     ins = [ins[k] for k in which]
     outs = [outs[k].at[cut] for k, cut in zip(which, cuts)]
     n = len(plan)
     accs, stages, firsts, rings, lasts = (refs[j * n : (j + 1) * n] for j in range(5))
-    send, recv, local, swap = refs[5 * n :]
-    place = Place(nz)
-    greet(place)
-    started = []
-    swapped = pltpu.make_async_remote_copy(
-        src_ref=here.at[1 - place.x],
-        dst_ref=there,
-        send_sem=swap.at[0],
-        recv_sem=swap.at[1],
-        device_id=place.other("x"),
-        device_id_type=MESH,
-    )
-
-    def put(i, k, src, dst, device):
+    send, recv, local = refs[5 * n :]
+    sent = []
+
+    def put(do, i, k, src, dst, device):
         copy = pltpu.make_async_remote_copy(
             src_ref=src,
             dst_ref=dst,
@@ -321,119 +309,194 @@
             device_id=device,
             device_id_type=MESH,
         )
-        copy.start()
-        started.append(copy)
+        do(copy.start)
+        sent.append(copy.wait_send)
         return copy
 
-    live = [dict() for _ in orders]
-
-    def load(i, k):
-        copy = pltpu.make_async_copy(
-            block_of(ins[i], cuts[i], place.c, place.ring_z(k)), stages[i].at[k % 2], local.at[i, k % 2]
-        )
-        copy.start()
+    live = [dict() for _ in plan]
+
+    def source(i, c, z):
+        if only[i] is None:
+            return block_of(ins[i], cuts[i], c, z)
+        return ins[i].at[(z, pl.ds(0, 2), c) + cuts[i]]
+
+    def load(do, i, k):
+        copy = pltpu.make_async_copy(source(i, place.c, place.ring_z(k)), stages[i].at[k % 2], local.at[i, k % 2])
+        do(copy.start)
         live[i]["o", k] = copy
 
-    def stage(i, s):
+    def stage(i, s, do):
         first, second, third = orders[i]
         acc, mine = accs[i], live[i]
         early, ring, late = firsts[i], rings[i], lasts[i]
 
-        def part(k, flip=0, flip2=None):
-            own = {axis: getattr(place, axis) for axis in "xy"}
-            own[first] = own[first] + flip * (1 - 2 * own[first])
-            if flip2 is None:
-                own["xy".replace(first, "")] = pl.ds(0, 2)
-            else:
-                other = "xy".replace(first, "")
-                own[other] = own[other] + flip2 * (1 - 2 * own[other])
-            return acc.at[k - 1, own["x"], own["y"]]
+        def part(k, **own):
+            at = (own.get("y", pl.ds(0, 2)),)
+            if only[i] is None:
+                at = (own.get("x", pl.ds(0, 2)),) + at
+            return acc.at[(k - 1,) + at]
+
+        here = {axis: getattr(place, axis) for axis in "xy"}
+        one = {first: here[first]}
+
+        def there(axis, **own):
+            own[axis] = 1 - here[axis]
+            return own
+
+        def step(dst, src):
+            do(lambda: add_to(dst(), src()))
+
+        def write(left, right):
+            def out():
+                outs[i][...] = wide(left()[...]) + wide(right()[...])
+
+            do(out)
 
         if s == 0:
             for k in range(1, nz + 1):
-                src = block_of(ins[i], cuts[i], 1 - place.c, place.ring_z(k))
-                mine["c", k] = put(i, k, src, acc.at[k - 1], place.other("c"))
-            load(i, 1)
-            load(i, 2)
+                mine["c", k] = put(do, i, k, source(i, 1 - place.c, place.ring_z(k)), acc.at[k - 1], place.other("c"))
+            load(do, i, 1)
+            load(do, i, 2)
         if 1 <= s <= nz:
             k = s
-            mine["c", k].wait_recv()
-            mine["o", k].wait()
-            add_to(acc.at[k - 1], stages[i].at[k % 2])
+            do(mine["c", k].wait_recv)
+            do(mine["o", k].wait)
+            step(lambda: acc.at[k - 1], lambda: stages[i].at[k % 2])
             if k + 2 <= nz:
-                load(i, k + 2)
-            mine["p", k] = put(i, nz + k, part(k, 1), early.at[k - 1], place.other(first))
+                load(do, i, k + 2)
+            mine["p", k] = put(do, i, nz + k, part(k, **there(first)), early.at[k - 1], place.other(first))
         if 2 <= s <= nz + 1:
-            k = s - 1
-            mine["p", k].wait_recv()
-            add_to(part(k), early.at[k - 1])
+            j = s - 1
+            do(mine["p", j].wait_recv)
+            step(lambda: part(j, **one), lambda: early.at[j - 1])
         if second == "z":
             if s == 2:
-                mine["z", 1] = put(i, 2 * nz + 1, part(1), ring.at[0], place.succ())
+                mine["z", 1] = put(do, i, 2 * nz + 1, part(1, **one), ring.at[0], place.succ())
             if 3 <= s <= nz + 1:
                 t = s - 2
-                mine["z", t].wait_recv()
-                add_to(ring.at[t - 1], part(t + 1))
+                do(mine["z", t].wait_recv)
+                step(lambda: ring.at[t - 1], lambda: part(t + 1, **one))
                 if t < nz - 1:
-                    mine["z", t + 1] = put(i, 2 * nz + t + 1, ring.at[t - 1], ring.at[t], place.succ())
+                    mine["z", t + 1] = put(do, i, 2 * nz + t + 1, ring.at[t - 1], ring.at[t], place.succ())
                 else:
-                    there = 1 - getattr(place, third)
-                    mine["l"] = put(i, 3 * nz + 1, ring.at[t - 1, there], late, place.other(third))
+                    src = ring.at[t - 1] if only[i] is not None else ring.at[t - 1, 1 - here[third]]
+                    mine["l"] = put(do, i, 3 * nz + 1, src, late, place.other(third))
             if s == nz + 2:
-                mine["l"].wait_recv()
-                outs[i][...] = wide(ring[nz - 2, getattr(place, third)]) + wide(late[...])
+                do(mine["l"].wait_recv)
+                write(lambda: ring.at[nz - 2] if only[i] is not None else ring.at[nz - 2, here[third]], lambda: late)
         else:
             if 2 <= s <= nz + 1:
-                k = s - 1
-                mine["l", k] = put(i, 3 * nz + k, part(k, 0, 1), late.at[k - 1], place.other(second))
+                j = s - 1
+                src = part(j, **there(second, **one))
+                mine["l", j] = put(do, i, 3 * nz + j, src, late.at[j - 1], place.other(second))
             if 3 <= s <= nz + 2:
-                k = s - 2
-                mine["l", k].wait_recv()
-                add_to(part(k, 0, 0), late.at[k - 1])
-                if k == 1:
-                    mine["z", 1] = put(i, 2 * nz + 1, part(1, 0, 0), ring.at[0], place.succ())
+                h = s - 2
+                do(mine["l", h].wait_recv)
+                step(lambda: part(h, **here), lambda: late.at[h - 1])
+                if h == 1:
+                    mine["z", 1] = put(do, i, 2 * nz + 1, part(1, **here), ring.at[0], place.succ())
                 else:
-                    t = k - 1
-                    mine["z", t].wait_recv()
+                    t = h - 1
+                    do(mine["z", t].wait_recv)
                     if t < nz - 1:
-                        add_to(ring.at[t - 1], part(t + 1, 0, 0))
-                        mine["z", t + 1] = put(i, 2 * nz + t + 1, ring.at[t - 1], ring.at[t], place.succ())
+                        step(lambda: ring.at[t - 1], lambda: part(t + 1, **here))
+                        mine["z", t + 1] = put(do, i, 2 * nz + t + 1, ring.at[t - 1], ring.at[t], place.succ())
                     else:
-                        outs[i][...] = wide(ring[t - 1]) + wide(part(nz, 0, 0)[...])
-
-    stages_of = nz + 3
-    for t in range(stages_of + max(starts)):
+                        write(lambda: ring.at[t - 1], lambda: part(nz, **here))
+
+    rounds = []
+    for t in range(nz + 3 + max(starts)):
+        rounds.append([])
         for i in range(n):
-            if 0 <= t - starts[i] < stages_of:
-                stage(i, t - starts[i])
+            if 0 <= t - starts[i] < nz + 3:
+                stage(i, t - starts[i], rounds[-1].append)
+    return rounds, sent
+
+
+def sum_scratch(plan, grads, nz):
+    def scratch(lead):
+        return [
+            pltpu.VMEM(lead(order, () if only is not None else (2,)) + part_shape(grads[k].shape[-2:], part), grads[k].dtype)
+            for k, part, order, _, only in plan
+        ]
+
+    return (
+        scratch(lambda o, x: (nz,) + x + (2,))
+        + scratch(lambda o, x: (2,) + x + (2,))
+        + scratch(lambda o, x: (nz,) + x)
+        + scratch(lambda o, x: (nz - 1,) + x if o[1] == "z" else (nz - 1,))
+        + scratch(lambda o, x: () if o[1] == "z" else (nz,))
+        + [
+            pltpu.SemaphoreType.DMA((len(plan), 4 * nz + 2)),
+            pltpu.SemaphoreType.DMA((len(plan), 4 * nz + 2)),
+            pltpu.SemaphoreType.DMA((len(plan), 2)),
+        ]
+    )
+
+
+def by_chip(grads, plan, nz):
+    only = dict((k, entry) for k, _, _, _, entry in plan)
+    return [
+        g.reshape(((2,) if only[k] is None else ()) + (nz, 2, 2) + g.shape[1:]) for k, g in enumerate(grads)
+    ]
+
+
+def scatter_kernel(plan, nz, *refs):
+    n = max(entry[0] for entry in plan) + 1
+    ins, here, refs = refs[:n], refs[n : n + 2], refs[n + 2 :]
+    outs, there, refs, swap = refs[:n], refs[n], refs[n + 1 : -1], refs[-1]
+    place = Place(nz)
+    greet(place)
+    rounds, sent = sum_rounds(plan, place, nz, ins, outs, refs)
+    swaps = [
+        pltpu.make_async_remote_copy(
+            src_ref=ref,
+            dst_ref=there,
+            send_sem=swap.at[0],
+            recv_sem=swap.at[1],
+            device_id=place.other("x"),
+            device_id_type=MESH,
+        )
+        for ref in here
+    ]
+    for t, acts in enumerate(rounds):
+        for act in acts:
+            act()
         if t == 0:
-            swapped.start()
-    for copy in started:
-        copy.wait_send()
-    swapped.wait()
-
-
-def finish_kernel(count, *refs):
-    n = (len(refs) - 7 - count) // 3
-    here, other, ins, packed, refs = refs[:2], refs[2:4], refs[4 : 4 + n], refs[4 + n], refs[5 + n :]
-    outs, vectors, held, (rows, sem) = refs[: 2 + n], refs[2 + n : 2 + n + count], refs[2 + n + count : -2], refs[-2:]
+            pl.when(place.x == 0)(swaps[1].start)
+            pl.when(place.x == 1)(swaps[0].start)
+    for act in sent:
+        act()
+    swaps[0].wait()
+
+
+def finish_kernel(count, chosen, *refs):
+    n = len(chosen)
+    ys, other_ys, gin0, gin1, other_gins, refs = refs[:5] + (refs[5:],)
+    ins = []
+    for two in chosen:
+        ins.append(refs[: 1 + two])
+        refs = refs[1 + two :]
+    packed, outs, refs = refs[0], refs[1 : 3 + n], refs[3 + n :]
+    vectors, held, (rows, sem) = refs[:count], refs[count:-2], refs[-2:]
     x = lax.axis_index("segment")
-    moves = []
-    for j in range(2):
-        moves.append((here[j].at[x], rows.at[j, 0], outs[j].at[x]))
-        moves.append((other[j], rows.at[j, 1], outs[j].at[1 - x]))
+    moves = [((ys.at[x],), rows.at[0, 0], outs[0].at[x]), ((other_ys,), rows.at[0, 1], outs[0].at[1 - x])]
+    moves += [((gin0, gin1), rows.at[1, 0], outs[1].at[x]), ((other_gins,), rows.at[1, 1], outs[1].at[1 - x])]
     moves += list(zip(ins, held, outs[2:]))
     steps = []
-    for j, (src, via, dst) in enumerate(moves):
-        steps.append((pltpu.make_async_copy(src, via, sem.at[j, 0]), pltpu.make_async_copy(via, dst, sem.at[j, 1])))
-        steps[-1][0].start()
+    for j, (sources, via, dst) in enumerate(moves):
+        loads = [pltpu.make_async_copy(src, via, sem.at[j, 0]) for src in sources]
+        if len(loads) == 1:
+            loads[0].start()
+        else:
+            pl.when(x == 0)(loads[0].start)
+            pl.when(x == 1)(loads[1].start)
+        steps.append((loads[0], pltpu.make_async_copy(via, dst, sem.at[j, 1])))
     row = 0
     for dst in vectors:
-        size, at = dst.shape[1], 0
-        while at < size:
-            more = min(128, size - at)
-            dst[:, at : at + more] = packed[row : row + 1, :more]
-            at, row = at + more, row + 1
+        for r, lo, many in pieces_of(dst.shape[1], row):
+            dst[:, lo : lo + many] = packed[r : r + 1, :many]
+        row += rows_for(dst.shape[1])
     for load, store in steps:
         load.wait()
         store.start()
@@ -441,63 +504,60 @@
         store.wait()
 
 
-def finish(rows, others, arrays, packed, sizes):
-    like = [jax.ShapeDtypeStruct(a.shape, a.dtype) for a in list(rows) + list(arrays)]
+def finish(ys, other_ys, gins, other_gins, arrays, packed, sizes):
+    chosen = [isinstance(a, tuple) for a in arrays]
+    flat = [part for a in arrays for part in (a if isinstance(a, tuple) else (a,))]
+    first = [a[0] if isinstance(a, tuple) else a for a in arrays]
+    like = [jax.ShapeDtypeStruct(a.shape, a.dtype) for a in [ys, ys] + first]
     vectors = [jax.ShapeDtypeStruct((1, size), jnp.float32) for size in sizes]
     far, near = pl.BlockSpec(memory_space=pl.ANY), pl.BlockSpec(memory_space=pltpu.VMEM)
     got = pl.pallas_call(
-        functools.partial(finish_kernel, len(sizes)),
+        functools.partial(finish_kernel, len(sizes), chosen),
         out_shape=like + vectors,
-        in_specs=[far] * (4 + len(arrays)) + [near],
+        in_specs=[far] * (5 + len(flat)) + [near],
         out_specs=[far] * len(like) + [near] * len(sizes),
-        scratch_shapes=[pltpu.VMEM(a.shape, a.dtype) for a in arrays]
-        + [pltpu.VMEM((2,) + rows[0].shape, rows[0].dtype), pltpu.SemaphoreType.DMA((4 + len(arrays), 2))],
+        scratch_shapes=[pltpu.VMEM(a.shape, a.dtype) for a in first]
+        + [pltpu.VMEM((2,) + ys.shape, ys.dtype), pltpu.SemaphoreType.DMA((4 + len(arrays), 2))],
         compiler_params=pltpu.CompilerParams(vmem_limit_bytes=62 * 2**20),
         name="finish",
-    )(*rows, *others, *arrays, packed)
+    )(ys, other_ys, *gins, other_gins, *flat, packed)
     return got[: len(like)], got[len(like) :]
 
 
-def from_other(rows):
-    return lax.ppermute(rows[1 - lax.axis_index("segment")], "segment", [(0, 1), (1, 0)])
+def from_other(first_rows, second_rows):
+    payload = jnp.where(lax.axis_index("segment") == 0, second_rows, first_rows)
+    return lax.ppermute(payload, "segment", [(0, 1), (1, 0)])
+
+
+def plain_sums(grads, plan):
+    only = dict((k, entry) for k, _, _, _, entry in plan)
+    got = []
+    for k, g in enumerate(grads):
+        if only[k] is None:
+            got.append(wide(lax.psum_scatter(g, AXES, scatter_dimension=0, tiled=False)))
+        else:
+            got.append(wide(lax.psum_scatter(lax.psum(g, "segment"), "dp", scatter_dimension=0, tiled=False)))
+    return got
 
 
 def scatter_all(grads, plan, mesh, rows):
     nx, ndp = mesh.shape["segment"], mesh.shape["dp"]
     if nx != 2 or ndp != 16:
-        return [wide(lax.psum_scatter(g, AXES, scatter_dimension=0, tiled=False)) for g in grads], from_other(rows)
+        return plain_sums(grads, plan), from_other(*rows)
     nz, n = ndp // 4, len(grads)
-
-    def scratch(lead):
-        return [
-            pltpu.VMEM(lead(order) + part_shape(grads[k].shape[1:], part), grads[k].dtype)
-            for k, part, order, _ in plan
-        ]
-
-    slots = 4 * nz + 2
     far, near = pl.BlockSpec(memory_space=pl.ANY), pl.BlockSpec(memory_space=pltpu.VMEM)
     got = pl.pallas_call(
         functools.partial(scatter_kernel, plan, nz),
         out_shape=[jax.ShapeDtypeStruct(g.shape[1:], jnp.float32) for g in grads]
-        + [jax.ShapeDtypeStruct(rows.shape[1:], rows.dtype)],
-        in_specs=[far] * (n + 1),
+        + [jax.ShapeDtypeStruct(rows[0].shape, rows[0].dtype)],
+        in_specs=[far] * (n + 2),
         out_specs=[near] * n + [far],
-        scratch_shapes=scratch(lambda o: (nz, 2, 2))
-        + scratch(lambda o: (2, 2, 2))
-        + scratch(lambda o: (nz, 2))
-        + scratch(lambda o: (nz - 1, 2) if o[1] == "z" else (nz - 1,))
-        + scratch(lambda o: () if o[1] == "z" else (nz,))
-        + [
-            pltpu.SemaphoreType.DMA((len(plan), slots)),
-            pltpu.SemaphoreType.DMA((len(plan), slots)),
-            pltpu.SemaphoreType.DMA((len(plan), 2)),
-            pltpu.SemaphoreType.DMA((2,)),
-        ],
+        scratch_shapes=sum_scratch(plan, grads, nz) + [pltpu.SemaphoreType.DMA((2,))],
         compiler_params=pltpu.CompilerParams(
             collective_id=1, has_side_effects=True, vmem_limit_bytes=62 * 2**20
         ),
         name="sum_gradients",
-    )(*[g.reshape((2, nz, 2, 2) + g.shape[1:]) for g in grads], rows)
+    )(*by_chip(grads, plan, nz), *rows)
     return got[:n], got[n]
 
 
@@ -783,16 +843,23 @@
             copy.wait()
 
 
-def backward_kernel(pairs, parts, g_ref, b_ref, small, g_small1, q_ref, slope_ref, probs_ref, inner_ref, outer_ref, second_ref, *refs):
-    far, refs = refs[:10], refs[14:]
+def backward_kernel(pairs, parts, host, g_ref, b_ref, small, g_small1, q_ref, slope_ref, probs_ref, inner_ref, outer_ref, second_ref, *refs):
+    far, refs = refs[:10], refs[13:]
+    n = max(entry[0] for entry in host[0]) + 1 if host else 0
+    sum_ins, refs = refs[:n], refs[n:]
     gx_ref, g_outer, g_inner, g_out, g_value, g_small, g_first, g_second = refs[:8]
-    near, refs = refs[8:18], refs[18:]
-    acc, ghid, gatt, gc_ref, gv_ref, db, gz_ref, vectors, g_vec, g_inner_b, g_second_b, sem = refs
+    sum_outs, refs = refs[8 : 8 + n], refs[8 + n :]
+    near, refs = refs[:10], refs[10:]
+    acc, ghid, gatt, gc_ref, gv_ref, db, gz_ref, vectors, g_vec, g_inner_b, g_second_b, sem, *refs = refs
     far = [ref.at[0] if len(ref.shape) == 3 else ref for ref in far]
     copies = [pltpu.make_async_copy(src, dst, sem.at[j]) for j, (src, dst) in enumerate(zip(far, near))]
     hid_ref, c_ref, out_ref, v_ref, p_ref, a_ref, value_ref, first_ref, first_slope, x_ref = near
-    g_ref, gx_ref = g_ref.at[0], gx_ref.at[0]
     i = pl.program_id(0)
+    rounds, sent = [], []
+    if host:
+        place = Place(host[1])
+        pl.when(i == 0)(lambda: greet(place))
+        rounds, sent = sum_rounds(host[0], place, host[1], sum_ins, sum_outs, refs)
     slots = probs_ref.shape[2] // 2
     ndp, part = small.shape[0] // 2, q_ref.shape[1]
 
@@ -808,10 +875,17 @@
             copy.start()
         unpack_vectors(small, 0, ndp, vectors)
 
+    for at, acts in zip(BESIDE, rounds):
+
+        @pl.when(i == at)
+        def _(acts=acts):
+            for act in acts:
+                act()
+
     @pl.when(i < parts)
     def _():
         bias = g_inner_b.at[:, pl.ds(pl.multiple_of(i * part, part), part)]
-        backward_hidden(i == 0, g_ref, b_ref, q_ref, slope_ref, inner_ref.at[0], outer_ref.at[0], gz_ref, acc, g_outer.at[0], g_inner.at[0], bias)
+        backward_hidden(i == 0, g_ref, b_ref, q_ref, slope_ref, inner_ref.at[0], outer_ref.at[0], gz_ref, acc, g_outer, g_inner.at[0], bias)
 
     @pl.when(i == parts - 1)
     def _():
@@ -844,6 +918,9 @@
         pack_rows(g_vec.at[FIRST_B : FIRST_B + 1, :], 2 * ndp, row, g_small, 0)
         row += rows_for(g_vec.shape[1] // (2 * ndp))
         pack_rows(g_second_b, 2 * ndp, row, g_small, 0)
+        for acts in rounds[len(BESIDE) :] + [sent]:
+            for act in acts:
+                act()
 
 
 def both_kernel(pairs, parts, length_ref, x_ref, g_ref, small, value_ref, out_ref, table_ref, inner_ref, outer_ref, *refs):
@@ -867,7 +944,7 @@
     def hidden(ref, k):
         return ref.at[:, pl.ds(pl.multiple_of(k * part, part), part)]
 
-    x_ref, g_ref, y_ref, gx_ref = (ref.at[0] for ref in (x_ref, g_ref, y_ref, gx_ref))
+    x_ref, g_ref, y_ref = (ref.at[0] for ref in (x_ref, g_ref, y_ref))
 
     def read(r):
         return wide(x_ref[r, :])
@@ -900,7 +977,7 @@
     @pl.when((k >= 0) & (k < parts))
     def _():
         at = parts - 1 - k
-        backward_hidden(k == 0, g_ref, b_ref, q_ref.at[at], slope_ref.at[at], inner_ref.at[0], outer_ref.at[0], gz_ref, acc, g_outer.at[0], g_inner.at[0], hidden(g_inner_b, at))
+        backward_hidden(k == 0, g_ref, b_ref, q_ref.at[at], slope_ref.at[at], inner_ref.at[0], outer_ref.at[0], gz_ref, acc, g_outer, g_inner.at[0], hidden(g_inner_b, at))
 
     @pl.when(k == parts - 1)
     def _():
@@ -1005,7 +1082,7 @@
     return y, saved
 
 
-def backward(g, x, saved, w, before, small1):
+def backward(g, x, saved, w, before, small1, host=None, early=()):
     rows, width, pairs, parts, part = sizes_of(x, w)
     slots = rows
     a, v, p, first_slope, c, b, hid, probs, q, slope = saved
@@ -1022,36 +1099,39 @@
     second_block = pl.BlockSpec((width, 2 * slots), lambda i: (0, pair(i)))
     far = [hid, c, w.out, v, p, a, w.value, w.first, first_slope, x]
     ins = [g, b, w.small, small1, q, slope, probs, w.inner, w.outer, w.second] + far
-    specs = [whole(g.shape, 1), whole((rows, width)), whole(w.small.shape), whole(small1.shape)] + [hidden_block] * 2
+    specs = [whole((rows, width))] * 2 + [whole(w.small.shape), whole(small1.shape)] + [hidden_block] * 2
     specs += [pl.BlockSpec((1, rows, 2 * slots), lambda i: (pair(i), 0, 0)), inner_block, outer_block, second_block]
     specs += [FAR] * 10
-    aliases = {len(ins) + j: 1 + j for j in range(4)}
-    aliases[0] = 0
-    ins += list(before)
-    specs += [FAR] * 4
-    outs = [like(g.shape)] + [like(k.shape, k.dtype) for k in before]
-    out_specs = [whole_out(g.shape, 0), outer_block, inner_block]
+    aliases = {len(ins) + j: 2 + j for j in range(3)}
+    ins += list(before) + list(early)
+    specs += [FAR] * (3 + len(early))
+    outs = [like((rows, width)), like(w.outer.shape[1:])] + [like(k.shape, k.dtype) for k in before]
+    out_specs = [whole_out((rows, width)), pl.BlockSpec((part, width), lambda i: (piece(i), 0)), inner_block]
     out_specs += [whole_out(w.out.shape, 0), whole_out(w.value.shape, 0)]
     outs += [like(w.small.shape, jnp.float32), like(w.first.shape), like(w.second.shape)]
     out_specs += [whole_out(w.small.shape), whole_out(w.first.shape), second_block]
+    sums_of = [like(e.shape[-2:], jnp.float32) for e in early]
     gx, *grads = pl.pallas_call(
-        functools.partial(backward_kernel, pairs, parts),
+        functools.partial(backward_kernel, pairs, parts, host),
         grid=(pairs + parts,),
-        out_shape=outs,
+        out_shape=outs + sums_of,
         in_specs=specs,
-        out_specs=out_specs,
+        out_specs=out_specs + [whole_out(e.shape) for e in sums_of],
         scratch_shapes=[pltpu.VMEM(k.shape[-2:], k.dtype) for k in far]
         + [pltpu.VMEM((rows, width), jnp.float32)] * 2
         + [pltpu.VMEM((rows, width), jnp.bfloat16)] * 3
         + [pltpu.VMEM((rows, 2 * slots), jnp.bfloat16), pltpu.VMEM((rows, part), jnp.bfloat16)]
         + [pltpu.VMEM((8, width), jnp.float32)] * 2
         + [pltpu.VMEM((1, part * parts), jnp.float32), pltpu.VMEM((1, w.second.shape[1]), jnp.float32)]
-        + [pltpu.SemaphoreType.DMA((10,))],
+        + [pltpu.SemaphoreType.DMA((10,))]
+        + (sum_scratch(host[0], early, host[1]) if host else []),
         input_output_aliases=aliases,
-        compiler_params=pltpu.CompilerParams(vmem_limit_bytes=62 * 2**20),
+        compiler_params=pltpu.CompilerParams(
+            vmem_limit_bytes=63 * 2**20, **(dict(collective_id=2, has_side_effects=True) if host else {})
+        ),
         name="backward_0",
     )(*ins)
-    return gx, grads[:4], grads[4:]
+    return gx, grads[:7], grads[7:]
 
 
 def both_ways(x, g, length, w):
@@ -1079,11 +1159,11 @@
         pl.BlockSpec((1, width, part), lambda i: (1, 0, piece(i))),
         pl.BlockSpec((1, part, width), lambda i: (1, piece(i), 0)),
     ]
-    grads = [like(w.outer.shape), like(w.inner.shape), like(w.out.shape), like(w.value.shape)]
+    grads = [like(w.outer.shape[1:]), like(w.inner.shape), like(w.out.shape), like(w.value.shape)]
     small = (w.small.shape[0] // 2,) + w.small.shape[1:]
     grads += [like(small, jnp.float32), like(w.table.shape)]
     grad_specs = [
-        pl.BlockSpec((1, part, width), lambda i: (1, late(i), 0)),
+        pl.BlockSpec((part, width), lambda i: (late(i), 0)),
         pl.BlockSpec((1, width, part), lambda i: (1, 0, late(i))),
         whole_out(w.out.shape, 1),
         whole_out(w.value.shape, 1),
@@ -1093,9 +1173,9 @@
     y, gx, *grads = pl.pallas_call(
         functools.partial(both_kernel, pairs, parts),
         grid=(2 * pairs + 2 * parts,),
-        out_shape=[like(x.shape)] * 2 + grads,
+        out_shape=[like(x.shape), like((rows, width))] + grads,
         in_specs=specs,
-        out_specs=[whole_out(x.shape, 1)] * 2 + grad_specs,
+        out_specs=[whole_out(x.shape, 1), whole_out((rows, width))] + grad_specs,
         scratch_shapes=[pltpu.VMEM((rows, width), jnp.float32)] * 3
         + [pltpu.VMEM((rows, width), jnp.bfloat16)] * 7
         + [pltpu.VMEM((pairs, rows, 2 * slots), jnp.bfloat16)]
@@ -1106,7 +1186,7 @@
         compiler_params=pltpu.CompilerParams(vmem_limit_bytes=62 * 2**20),
         name="forward_backward_1",
     )(*ins)
-    return y, gx, grads[:4], grads[4], grads[5]
+    return y, gx, grads
 
 
 ROW_VECTORS = (0, 1, 3, 5, 6, 7, 11)
@@ -1127,25 +1207,29 @@
     (14, 0, "xzy", 2),
     (14, 1, "xzy", 0),
 )
+EARLY = ((10, 1, "yzx", 1, 1), (10, 0, "yzx", 0, 1), (16, 1, "yxz", 1, None), (16, 0, "xzy", 1, None))
+BESIDE = (0, 0, 1, 3, 4, 7, 9)
 SUM = (
-    (8, 1, "yzx", 3),
-    (8, 0, "xzy", 4),
-    (4, None, "yzx", 1),
-    (14, 1, "yxz", 4),
-    (16, 0, "xzy", 3),
-    (12, None, "yzx", 0),
-    (10, 1, "yxz", 4),
-    (2, None, "yzx", 1),
-    (SMALL, None, "xzy", 4),
-    (16, 1, "xzy", 1),
-    (14, 0, "yxz", 4),
-    (10, 0, "xzy", 3),
+    (8, 1, "yzx", 4, None),
+    (14, 1, "yxz", 5, None),
+    (10, 1, "yzx", 2, 0),
+    (12, None, "xzy", 2, None),
+    (8, 0, "xyz", 3, None),
+    (4, None, "yzx", 0, None),
+    (10, 0, "yzx", 2, 0),
+    (2, None, "xzy", 2, None),
+    (SMALL, None, "xyz", 5, None),
+    (14, 0, "xzy", 4, None),
 )
 
 
+def numbered(plan):
+    names = list(dict.fromkeys(entry[0] for entry in plan))
+    return names, [(names.index(entry[0]),) + entry[1:] for entry in plan]
+
+
 def planned(call, plan, arrays, mesh, rows):
-    names = list(dict.fromkeys(entry[0] for entry in plan))
-    plan = [(names.index(entry[0]),) + entry[1:] for entry in plan]
+    names, plan = numbered(plan)
     got, rows = call([arrays[k] for k in names], plan, mesh, rows)
     return dict(zip(names, got)), rows
 
@@ -1175,17 +1259,29 @@
     w = Weights(full[SMALL], full[2], full[4], full[8], full[10], full[12], full[14], full[16])
 
     outs, saved = forward(pair, length, w)
-    outs, gins, both, g_small, g_table = both_ways(outs, pair, length, w)
-    other_outs = from_other(outs)
-    gins, both, synth = backward(gins, pair, saved, w, both, g_small)
-
-    g_outer, g_inner, g_out, g_value = both
-    g_small, g_first, g_second = synth
-    matrices = (g_value, g_out, g_inner, g_outer, g_first, g_second, g_table)
-    grads = {k: g.reshape((devices,) + parts[k].shape[-2:]) for k, g in zip(MATRICES, matrices)}
+    outs, gin1, (g_outer1, *both, g_small, g_table) = both_ways(outs, pair, length, w)
+    other_outs = from_other(outs[0], outs[1])
+    early = {16: g_table.reshape((devices,) + parts[16].shape), 10: g_outer1.reshape((ndp,) + parts[10].shape[1:])}
+    names, plan = numbered(EARLY)
+    early = [early[k] for k in names]
+    if nx == 2 and ndp == 16:
+        host, hosted = (plan, ndp // 4), by_chip(early, plan, ndp // 4)
+        gin0, grads, sums_early = backward(gin1, pair, saved, w, both, g_small, host, hosted)
+    else:
+        gin0, grads, _ = backward(gin1, pair, saved, w, both, g_small)
+        sums_early = plain_sums(early, plan)
+    sums_early = dict(zip(names, sums_early))
+
+    g_outer0, g_inner, g_out, g_value, g_small, g_first, g_second = grads
+    grads = {2: g_value, 4: g_out, 8: g_inner, 12: g_first, 14: g_second}
+    grads = {k: g.reshape((devices,) + parts[k].shape[-2:]) for k, g in grads.items()}
+    grads[10] = g_outer0.reshape((ndp,) + parts[10].shape[1:])
     grads[SMALL] = g_small
-    summed, other_gins = planned(scatter_all, SUM, grads, mesh, gins)
-    arrays, vectors = finish([outs, gins], [other_outs, other_gins], [summed[k] for k in MATRICES], summed[SMALL], sizes)
+    summed, other_gins = planned(scatter_all, SUM, grads, mesh, [gin0, gin1])
+    summed[16] = sums_early[16]
+    summed[10] = (summed[10], sums_early[10])
+    matrices = [summed[k] for k in MATRICES]
+    arrays, vectors = finish(outs, other_outs, [gin0, gin1], other_gins, matrices, summed[SMALL], sizes)
     result = {k: g.reshape(parts[k].shape) for k, g in zip(MATRICES, arrays[2:])}
     for k, g in zip(VECTORS, vectors):
         result[k] = g.reshape(parts[k].shape)

time: 457 us -> 452 us (0.989); the launches traced: 457 us -> 445 us
  Pallas kernels: 451 us -> 439 us
    pallas_call x1, Pallas kernels: 160 us -> 122 us  [scatter_all(): pl.pallas_call(functools.partial(scatter_kernel, plan, nz), out_shape=[ja...]
    pallas_call x2, Pallas kernels: 50.2 us -> 76.5 us  [the longest x1 70.2 us: backward(): pl.pallas_call(functools.partial(backward_kernel, pairs, parts, host), gr...]
  transfers between devices with their start and end apart: 1 -> 1, of which waited for: 0 -> 0; matrix products, arithmetic and copies ran while one was open for 0% -> 0% of each run, Pallas kernels for 45% -> 43%
where the time goes in v6:
time: 452 us; the launch traced here: 445 us
  Pallas kernels  439 us (97%)
    pallas_call x1, Pallas kernels, gather_all(): pl.pallas_call(functools.partial(gather_kernel, plan, nz, small_at, count...  160 us
    pallas_call x1, Pallas kernels, scatter_all(): pl.pallas_call(functools.partial(scatter_kernel, plan, nz), out_shape=[ja...  122 us
    pallas_call x1, Pallas kernels, backward(): pl.pallas_call(functools.partial(backward_kernel, pairs, parts, host), gr...  70.2 us
    pallas_call x1, Pallas kernels, both_ways(): pl.pallas_call(functools.partial(both_kernel, pairs, parts), grid=(2 * pa...  49.7 us
    pallas_call x1, Pallas kernels, forward(): pl.pallas_call(functools.partial(forward_kernel, pairs, parts), grid=(pai...  30.4 us
  transfers between devices with their start and end apart: 1, of which 0 were waited for; matrix products, arithmetic and copies ran while one was open for 0% of the time, Pallas kernels for 43%

profile of v6, /device:TPU:0, one launch (start us, length us, event | category | flops | bytes accessed | tf_op | source)
XLA Modules:
  0.0 444.6 jit_solution(13443473431692244766)
XLA Ops:
  0.7 1.3 fusion
  3.3 160.5 %gather_weights.1 = (bf16[2,4,2,2,48,3072]{5,4,3,2,1,0:T(8,128)(2,1)}, bf16[2,4,2,2,16,128]{5,4,3,2,1,0:T(8,128)(2,1)}, bf16[2,4,2,2,192,768]{5,4,3,2,1,0:T(8,12...) custom-call(f32[48,3072]{1,0:T(8,128)} %bitcast.70, ...), custom_call_target="tpu_custom_call" | custom-call | tf_op jit(solution)/shard_map/gather_weights/pallas_call | solution.py:255
  163.8 30.4 %forward_0.1 = (bf16[2,512,768]{2,1,0:T(8,128)(2,1)}, bf16[512,768]{1,0:T(8,128)(2,1)}, bf16[512,768]{1,0:T(8,128)(2,1)}, bf16[512,768]{1,0:T(8,128)(2,1)}, bf16...) custom-call(s32[1]{0:T(128)S(6)} %select_n.20.length_ref, ...), custom_call_target="tpu_custom_call" | custom-call | tf_op jit(solution)/shard_map/forward_0/pallas_call | solution.py:1061
  194.2 49.7 %forward_backward_1.1 = (bf16[2,512,768]{2,1,0:T(8,128)(2,1)}, bf16[512,768]{1,0:T(8,128)(2,1)}, bf16[3072,768]{1,0:T(8,128)(2,1)}, bf16[2,768,3072]{2,1,0:T(8,1...) custom-call(s32[1]{0:T(128)S(6)} %select_n.20.length_ref, ...), custom_call_target="tpu_custom_call", output_to_operand_aliasing={{0}: (1, {})} | custom-call | tf_op jit(solution)/shard_map/forward_backward_1/pallas_call | solution.py:1173
  243.9 1.5 select_bitcast_fusion
  245.4 0.6 collective-permute-start
  246.0 70.2 %backward_0.1 = (bf16[512,768]{1,0:T(8,128)(2,1)}, bf16[3072,768]{1,0:T(8,128)(2,1)}, bf16[2,768,3072]{2,1,0:T(8,128)(2,1)}, bf16[2,768,768]{2,1,0:T(8,128)(2,1)...) custom-call(bf16[512,768]{1,0:T(8,128)(2,1)} %get-tuple-element.95.g, ...), custom_call_target="tpu_custom_call", output_to_operand_aliasing={{2}: (20, {}), {3}: (21, {}), {4}: (22, {})} | custom-call | tf_op jit(solution)/shard_map/backward_0/pallas_call | solution.py:1114
  316.2 121.6 %sum_gradients.1 = (f32[48,3072]{1,0:T(8,128)}, f32[24,6144]{1,0:T(8,128)}, f32[192,768]{1,0:T(8,128)}, f32[24,768]{1,0:T(8,128)}, f32[48,768]{1,0:T(8,128)}, /*...) custom-call(bf16[2,4,2,2,48,3072]{5,4,3,2,1,0:T(8,128)(2,1)} %bitcast.49, ...), custom_call_target="tpu_custom_call" | custom-call | tf_op jit(solution)/shard_map/sum_gradients/pallas_call | solution.py:549
  437.9 0.0 collective-permute-done.refs_1_
  437.9 6.2 %finish.1 = (bf16[2,512,768]{2,1,0:T(8,128)(2,1)}, bf16[2,512,768]{2,1,0:T(8,128)(2,1)}, f32[48,768]{1,0:T(8,128)}, f32[48,768]{1,0:T(8,128)}, f32[48,3072]{1,0:...) custom-call(bf16[2,512,768]{2,1,0:T(8,128)(2,1)} %get-tuple-element., ...), custom_call_target="tpu_custom_call" | custom-call | tf_op jit(solution)/shard_map/finish/pallas_call | solution.py:514
Async XLA Ops:
  245.4 192.5 %collective-permute-start = (bf16[512,768]{1,0:T(8,128)(2,1)S(1)}, bf16[512,768]{1,0:T(8,128)(2,1)}, u32[]{:S(2)}, u32[]{:S(2)}) collective-permute-start(bf16[512,768]{1,0:T(8,128)(2,1)S(1)} %select_bitcast_fusion), channel_id=1, source_target_pairs={{0,16},{16,0},{1,17},{17,1},{2,18},{18,2},{3,19},{19,3},{4,20},{20... | collective-permute-start | bytes 2359304 | tf_op jit(solution)/shard_map/ppermute | solution.py:529

commit v7 on v6

--- a/solution.py
+++ b/solution.py
@@ -100,16 +100,111 @@
     return ref.at[(xs, z, ys, c) + cut]
 
 
+def gather_rounds(plan, place, nz, shards, outs, prepare, sems):
+    which, parts, orders, starts = zip(*plan)
+    cuts = [part_of(shards[k].shape, part) for k, part in zip(which, parts)]
+    ins = [shards[k].at[cut] for k, cut in zip(which, cuts)]
+    outs = [outs[k] for k in which]
+    send, recv, local = sems
+    ready = set()
+    sent = []
+
+    def put(do, i, k, src, dst, device):
+        copy = pltpu.make_async_remote_copy(
+            src_ref=src,
+            dst_ref=dst,
+            send_sem=send.at[i, k],
+            recv_sem=recv.at[i, k],
+            device_id=device,
+            device_id_type=MESH,
+        )
+        do(copy.start)
+        sent.append(copy.wait_send)
+        return copy
+
+    copies = [dict() for _ in plan]
+
+    def stage(i, t, do):
+        first, second, third = orders[i]
+        out, mine = outs[i], copies[i]
+
+        def shard(z, **at):
+            return block_of(out, cuts[i], place.c, z, **at)
+
+        def own(axis, z):
+            return shard(z, **{axis: getattr(place, axis)})
+
+        one = shard(place.z, x=place.x, y=place.y)
+        if t == 0:
+            if which[i] not in ready:
+                ready.add(which[i])
+                do(prepare[which[i]])
+            mine["own"] = pltpu.make_async_copy(ins[i], one, local.at[i])
+            do(mine["own"].start)
+        if second == "z":
+            if t == 0:
+                mine["p"] = put(do, i, 0, ins[i], one, place.other(first))
+                return
+            if t == 1:
+                do(mine["own"].wait)
+                do(mine["p"].wait_recv)
+            elif t <= nz:
+                do(mine["z", t - 1].wait_recv)
+            if t <= nz:
+                block = own(third, place.ring_z(t - 1))
+                if t < nz:
+                    mine["z", t] = put(do, i, t, block, block, place.succ())
+                mine["l", t] = put(do, i, nz + t, block, block, place.other(third))
+                mine["c", t] = put(do, i, 2 * nz + t, block, block, place.other("c"))
+            if t >= 2:
+                do(mine["l", t - 1].wait_recv)
+                block = shard(place.ring_z(t - 2), **{third: 1 - getattr(place, third)})
+                mine["d", t - 1] = put(do, i, 3 * nz + t - 1, block, block, place.other("c"))
+        else:
+            if t <= nz - 1:
+                if t > 0:
+                    do(mine["z", t].wait_recv)
+                z = place.ring_z(t)
+                dst = shard(z, x=place.x, y=place.y)
+                src = ins[i] if t == 0 else dst
+                if t < nz - 1:
+                    mine["z", t + 1] = put(do, i, t, src, dst, place.succ())
+                mine["p", t + 1] = put(do, i, nz + t, src, dst, place.other(second))
+            if 1 <= t <= nz:
+                if t == 1:
+                    do(mine["own"].wait)
+                do(mine["p", t].wait_recv)
+                block = own(third, place.ring_z(t - 1))
+                mine["l", t] = put(do, i, 2 * nz + t, block, block, place.other(third))
+                mine["c", t] = put(do, i, 3 * nz + t, block, block, place.other("c"))
+            if t >= 2:
+                do(mine["l", t - 1].wait_recv)
+                block = shard(place.ring_z(t - 2), **{third: 1 - getattr(place, third)})
+                mine["d", t - 1] = put(do, i, 4 * nz + t - 1, block, block, place.other("c"))
+
+    rounds = []
+    for t in range(nz + 2 + max(starts)):
+        rounds.append([])
+        for i in range(len(plan)):
+            if 0 <= t - starts[i] < nz + 2:
+                stage(i, t - starts[i], rounds[-1].append)
+    last = [copy.wait_recv for mine in copies for key, copy in mine.items() if key[0] in "cd"]
+    return rounds, last + sent
+
+
+def gather_sems(plan, nz):
+    return [
+        pltpu.SemaphoreType.DMA((len(plan), 5 * nz + 2)),
+        pltpu.SemaphoreType.DMA((len(plan), 5 * nz + 2)),
+        pltpu.SemaphoreType.DMA((len(plan),)),
+    ]
+
+
 def gather_kernel(plan, nz, small_at, count, *refs):
-    which, parts, orders, starts = zip(*plan)
-    n = max(which) + 1
+    n = max(entry[0] for entry in plan) + 1
     far, vectors, own, refs = refs[: n - 1], refs[n - 1 : n - 1 + count], refs[n - 1 + count], refs[n + count :]
-    whole_outs, pair, raw, whole_ins, refs = refs[:n], refs[n], refs[n + 1 : 2 * n + 1], refs[2 * n + 1 : 3 * n + 1], refs[3 * n + 1 :]
-    near, (held, send, recv, local, swap, loads) = refs[:count], refs[count:]
-    cuts = [part_of(raw[k].shape, part) for k, part in zip(which, parts)]
-    ins = [whole_ins[k].at[cut] for k, cut in zip(which, cuts)]
-    outs = [whole_outs[k] for k in which]
-    ready = set()
+    outs, pair, raw, shards, refs = refs[:n], refs[n], refs[n + 1 : 2 * n + 1], refs[2 * n + 1 : 3 * n + 1], refs[3 * n + 1 :]
+    near, (held, swap, loads), sems = refs[:count], refs[count : count + 3], refs[count + 3 :]
     place = Place(nz)
     moves = list(zip(vectors, near))
     moves += list(zip(far, [ref for k, ref in enumerate(raw) if k != small_at])) + [(own.at[place.x], held)]
@@ -128,110 +223,32 @@
         device_id=place.other("x"),
         device_id_type=MESH,
     )
-    started = []
-
-    def put(i, k, src, dst, device):
-        copy = pltpu.make_async_remote_copy(
-            src_ref=src,
-            dst_ref=dst,
-            send_sem=send.at[i, k],
-            recv_sem=recv.at[i, k],
-            device_id=device,
-            device_id_type=MESH,
-        )
-        copy.start()
-        started.append(copy)
-        return copy
-
-    copies = [dict() for _ in orders]
-
-    def stage(i, t):
-        first, second, third = orders[i]
-        out, mine = outs[i], copies[i]
-
-        def shard(z, **at):
-            return block_of(out, cuts[i], place.c, z, **at)
-
-        def own(axis, z):
-            return shard(z, **{axis: getattr(place, axis)})
-
-        one = shard(place.z, x=place.x, y=place.y)
-        if t == 0:
-            k = which[i]
-            if k not in ready:
-                if k == small_at:
-                    raw[k][...] = jnp.zeros_like(raw[k])
-                    row = 0
-                    for copy, vector in zip(packing, near):
-                        copy.wait()
-                        for r, lo, many in pieces_of(vector.shape[1], row):
-                            raw[k][r : r + 1, :many] = vector[:, lo : lo + many]
-                        row += rows_for(vector.shape[1])
-                else:
-                    loading[k].wait()
-                whole_ins[k][...] = half(raw[k][...])
-                ready.add(k)
-            mine["own"] = pltpu.make_async_copy(ins[i], one, local.at[i])
-            mine["own"].start()
-        if second == "z":
-            if t == 0:
-                mine["p"] = put(i, 0, ins[i], one, place.other(first))
-                return
-            if t == 1:
-                mine["own"].wait()
-                mine["p"].wait_recv()
-            elif t <= nz:
-                mine["z", t - 1].wait_recv()
-            if t <= nz:
-                z = place.ring_z(t - 1)
-                block = own(third, z)
-                if t < nz:
-                    mine["z", t] = put(i, t, block, block, place.succ())
-                mine["l", t] = put(i, nz + t, block, block, place.other(third))
-                mine["c", t] = put(i, 2 * nz + t, block, block, place.other("c"))
-            if t >= 2:
-                mine["l", t - 1].wait_recv()
-                z = place.ring_z(t - 2)
-                block = shard(z, **{third: 1 - getattr(place, third)})
-                mine["d", t - 1] = put(i, 3 * nz + t - 1, block, block, place.other("c"))
+
+    def prepare(k):
+        if k == small_at:
+            raw[k][...] = jnp.zeros_like(raw[k])
+            row = 0
+            for copy, vector in zip(packing, near):
+                copy.wait()
+                for r, lo, many in pieces_of(vector.shape[1], row):
+                    raw[k][r : r + 1, :many] = vector[:, lo : lo + many]
+                row += rows_for(vector.shape[1])
         else:
-            if t <= nz - 1:
-                if t > 0:
-                    mine["z", t].wait_recv()
-                z = place.ring_z(t)
-                src = ins[i] if t == 0 else shard(z, x=place.x, y=place.y)
-                dst = shard(z, x=place.x, y=place.y)
-                if t < nz - 1:
-                    mine["z", t + 1] = put(i, t, src, dst, place.succ())
-                mine["p", t + 1] = put(i, nz + t, src, dst, place.other(second))
-            if 1 <= t <= nz:
-                if t == 1:
-                    mine["own"].wait()
-                mine["p", t].wait_recv()
-                block = own(third, place.ring_z(t - 1))
-                mine["l", t] = put(i, 2 * nz + t, block, block, place.other(third))
-                mine["c", t] = put(i, 3 * nz + t, block, block, place.other("c"))
-            if t >= 2:
-                mine["l", t - 1].wait_recv()
-                block = shard(place.ring_z(t - 2), **{third: 1 - getattr(place, third)})
-                mine["d", t - 1] = put(i, 4 * nz + t - 1, block, block, place.other("c"))
-
-    stages = nz + 2
-    for t in range(stages + max(starts)):
-        for i in range(len(plan)):
-            if 0 <= t - starts[i] < stages:
-                stage(i, t - starts[i])
+            loading[k].wait()
+        shards[k][...] = half(raw[k][...])
+
+    ready = [functools.partial(prepare, k) for k in range(n)]
+    rounds, last = gather_rounds(plan, place, nz, shards, outs, ready, sems)
+    for t, acts in enumerate(rounds):
+        for act in acts:
+            act()
         if t == 0:
             leaves.start()
         if t == 1:
             loading[-1].wait()
             stays.start()
-    for mine in copies:
-        for key, copy in mine.items():
-            if key[0] in "cd":
-                copy.wait_recv()
-    for copy in started:
-        copy.wait_send()
+    for act in last:
+        act()
     stays.wait()
     leaves.wait()
 
@@ -251,7 +268,6 @@
     height = sum(rows_for(v.size) for v in vectors)
     shapes = [(height + -height % 16, 128) if j == small_at else s.shape for j, s in enumerate(shards)]
     far = [s for j, s in enumerate(shards) if j != small_at]
-    slots = 5 * nz + 2
     *outs, pair = pl.pallas_call(
         functools.partial(gather_kernel, plan, nz, small_at, count),
         out_shape=[jax.ShapeDtypeStruct((2, nz, 2, 2) + s, jnp.bfloat16) for s in shapes]
@@ -263,12 +279,10 @@
         + [pltpu.VMEM(v.shape, v.dtype) for v in vectors]
         + [
             pltpu.VMEM(rows.shape[1:], rows.dtype),
-            pltpu.SemaphoreType.DMA((len(plan), slots)),
-            pltpu.SemaphoreType.DMA((len(plan), slots)),
-            pltpu.SemaphoreType.DMA((len(plan),)),
             pltpu.SemaphoreType.DMA((3,)),
             pltpu.SemaphoreType.DMA((n + count,)),
-        ],
+        ]
+        + gather_sems(plan, nz),
         compiler_params=pltpu.CompilerParams(collective_id=0, has_side_effects=True, vmem_limit_bytes=62 * 2**20),
         name="gather_weights",
     )(*far, *vectors, rows)
@@ -654,6 +668,15 @@
     return lax.broadcasted_iota(jnp.int32, (1, 2 * head), 1) < head
 
 
+def beside(i, steps, rounds):
+    for at, acts in zip(steps, rounds):
+
+        @pl.when(i == at)
+        def _(acts=acts):
+            for act in acts:
+                act()
+
+
 def add_up(fresh, ref, at, value):
     @pl.when(fresh)
     def _():
@@ -788,9 +811,24 @@
     put(BIAS1, shift)
 
 
-def forward_kernel(pairs, parts, length_ref, x_ref, small, value_ref, out_ref, first_ref, second_ref, inner_ref, outer_ref, y_ref, *refs):
-    kept, probs_ref, q_ref, slope_ref = refs[:7], refs[7], refs[8], refs[9]
-    a_ref, v_ref, p_ref, first_slope, c_ref, b_ref, hid_ref, acc, vectors, inner_b, first_b, second_b, sem = refs[10:]
+def forward_kernel(pairs, parts, host, length_ref, x_ref, small, value_ref, out_ref, first_ref, second_ref, inner_ref, outer_ref, *refs):
+    n = 1 if host else 0
+    far, y_ref, refs = refs[:n], refs[n], refs[n + 1 :]
+    kept, probs_ref, q_ref, slope_ref, table, refs = refs[:7], refs[7], refs[8], refs[9], refs[10 : 10 + n], refs[10 + n :]
+    a_ref, v_ref, p_ref, first_slope, c_ref, b_ref, hid_ref, acc, vectors, inner_b, first_b, second_b, sem, *refs = refs
+    rounds, last = [], []
+    if host:
+        raw, shard, load, *sems = refs
+        place = Place(host[1])
+        loading = pltpu.make_async_copy(far[0], raw, load.at[0])
+
+        def prepare():
+            loading.start()
+            greet(place)
+            loading.wait()
+            shard[...] = half(raw[...])
+
+        rounds, last = gather_rounds(host[0], place, host[1], [shard], table, [prepare], sems)
     held = (a_ref, v_ref, p_ref, first_slope, c_ref, b_ref, hid_ref)
     copies = [pltpu.make_async_copy(src, dst, sem.at[j]) for j, (src, dst) in enumerate(zip(held, kept))]
     i = pl.program_id(0)
@@ -801,9 +839,12 @@
         return vectors[k : k + 1, :]
 
     x_ref, y_ref = x_ref.at[0], y_ref.at[0]
+    length = length_ref[lax.axis_index("segment"), 0]
 
     def read(r):
         return wide(x_ref[r, :])
+
+    beside(i, BESIDE_FORWARD, rounds)
 
     @pl.when(i == 0)
     def _():
@@ -823,7 +864,7 @@
             logits = mm(p_ref[...], second_ref[...]) + (bias + jnp.concatenate([shut, shut], axis=1))
             return logits[:, :slots], logits[:, slots:]
 
-        forward_heads(i, length_ref[0], v_ref, c_ref, probs_ref.at[0], logits_of)
+        forward_heads(i, length, v_ref, c_ref, probs_ref.at[0], logits_of)
 
     @pl.when(i == pairs - 1)
     def _():
@@ -841,14 +882,17 @@
         forward_end(vec, hid_ref, acc, y_ref)
         for copy in copies:
             copy.wait()
+        for acts in rounds[len(BESIDE_FORWARD) :] + [last]:
+            for act in acts:
+                act()
 
 
 def backward_kernel(pairs, parts, host, g_ref, b_ref, small, g_small1, q_ref, slope_ref, probs_ref, inner_ref, outer_ref, second_ref, *refs):
     far, refs = refs[:10], refs[13:]
-    n = max(entry[0] for entry in host[0]) + 1 if host else 0
-    sum_ins, refs = refs[:n], refs[n:]
+    n, swaps = (max(entry[0] for entry in host[0]) + 1, 1) if host else (0, 0)
+    sum_ins, ys, refs = refs[:n], refs[n : n + swaps], refs[n + swaps :]
     gx_ref, g_outer, g_inner, g_out, g_value, g_small, g_first, g_second = refs[:8]
-    sum_outs, refs = refs[8 : 8 + n], refs[8 + n :]
+    sum_outs, other_ys, refs = refs[8 : 8 + n], refs[8 + n : 8 + n + swaps], refs[8 + n + swaps :]
     near, refs = refs[:10], refs[10:]
     acc, ghid, gatt, gc_ref, gv_ref, db, gz_ref, vectors, g_vec, g_inner_b, g_second_b, sem, *refs = refs
     far = [ref.at[0] if len(ref.shape) == 3 else ref for ref in far]
@@ -859,7 +903,18 @@
     if host:
         place = Place(host[1])
         pl.when(i == 0)(lambda: greet(place))
+        *refs, swap = refs
         rounds, sent = sum_rounds(host[0], place, host[1], sum_ins, sum_outs, refs)
+        swapped = pltpu.make_async_remote_copy(
+            src_ref=ys[0].at[1 - place.x],
+            dst_ref=other_ys[0],
+            send_sem=swap.at[0],
+            recv_sem=swap.at[1],
+            device_id=place.other("x"),
+            device_id_type=MESH,
+        )
+        rounds[0].append(swapped.start)
+        sent.append(swapped.wait)
     slots = probs_ref.shape[2] // 2
     ndp, part = small.shape[0] // 2, q_ref.shape[1]
 
@@ -875,12 +930,7 @@
             copy.start()
         unpack_vectors(small, 0, ndp, vectors)
 
-    for at, acts in zip(BESIDE, rounds):
-
-        @pl.when(i == at)
-        def _(acts=acts):
-            for act in acts:
-                act()
+    beside(i, BESIDE_BACKWARD, rounds)
 
     @pl.when(i < parts)
     def _():
@@ -918,7 +968,7 @@
         pack_rows(g_vec.at[FIRST_B : FIRST_B + 1, :], 2 * ndp, row, g_small, 0)
         row += rows_for(g_vec.shape[1] // (2 * ndp))
         pack_rows(g_second_b, 2 * ndp, row, g_small, 0)
-        for acts in rounds[len(BESIDE) :] + [sent]:
+        for acts in rounds[len(BESIDE_BACKWARD) :] + [sent]:
             for act in acts:
                 act()
 
@@ -960,7 +1010,7 @@
         def logits_of(shut):
             return wide(table_ref[:slots, :]) + shut, wide(table_ref[slots:, :]) + shut
 
-        forward_heads(i, length_ref[0], v_ref, c_ref, probs_ref.at[i], logits_of, True)
+        forward_heads(i, length_ref[lax.axis_index("segment"), 0], v_ref, c_ref, probs_ref.at[i], logits_of, True)
 
     @pl.when(i == pairs - 1)
     def _():
@@ -1033,7 +1083,7 @@
     return rows, width, HEADS // 2, parts, w.inner.shape[2] // parts
 
 
-def forward(x, length, w):
+def forward(x, lengths, w, host=None, late=()):
     rows, width, pairs, parts, part = sizes_of(x, w)
     slots = rows
 
@@ -1043,7 +1093,7 @@
     def piece(i):
         return jnp.maximum(i - pairs, 0)
 
-    ins = [length, x, w.small, w.value, w.out, w.first, w.second, w.inner, w.outer]
+    ins = [lengths, x, w.small, w.value, w.out, w.first, w.second, w.inner, w.outer] + list(late)
     specs = [
         pl.BlockSpec(memory_space=pltpu.SMEM),
         whole(x.shape, 0),
@@ -1054,19 +1104,21 @@
         pl.BlockSpec((width, 2 * slots), lambda i: (0, pair(i))),
         pl.BlockSpec((1, width, part), lambda i: (0, 0, piece(i))),
         pl.BlockSpec((1, part, width), lambda i: (0, piece(i), 0)),
-    ]
+    ] + [FAR] * len(late)
+    table = [like((2, host[1], 2, 2) + t.shape) for t in late]
     half_rows = like((rows, width))
     kept = [half_rows] * 6 + [like((rows, width), jnp.float32)]
     hidden_block = pl.BlockSpec((rows, part), lambda i: (0, piece(i)))
     y, *saved = pl.pallas_call(
-        functools.partial(forward_kernel, pairs, parts),
+        functools.partial(forward_kernel, pairs, parts, host),
         grid=(pairs + parts,),
-        out_shape=[like(x.shape)] + kept + [like((pairs, rows, 2 * slots))] + [like((rows, part * parts))] * 2,
+        out_shape=[like(x.shape)] + kept + [like((pairs, rows, 2 * slots))] + [like((rows, part * parts))] * 2 + table,
         in_specs=specs,
         out_specs=[whole_out(x.shape, 0)]
         + [FAR] * 7
         + [pl.BlockSpec((1, rows, 2 * slots), lambda i: (pair(i), 0, 0))]
-        + [hidden_block] * 2,
+        + [hidden_block] * 2
+        + [FAR] * len(table),
         scratch_shapes=[pltpu.VMEM(k.shape, k.dtype) for k in kept]
         + [
             pltpu.VMEM((rows, width), jnp.float32),
@@ -1075,14 +1127,19 @@
             pltpu.VMEM((1, width), jnp.float32),
             pltpu.VMEM((1, w.second.shape[1]), jnp.float32),
             pltpu.SemaphoreType.DMA((7,)),
-        ],
-        compiler_params=pltpu.CompilerParams(vmem_limit_bytes=62 * 2**20),
+        ]
+        + [pltpu.VMEM(t.shape, t.dtype) for t in late]
+        + [pltpu.VMEM(t.shape, jnp.bfloat16) for t in late]
+        + ([pltpu.SemaphoreType.DMA((1,))] + gather_sems(*host) if host else []),
+        compiler_params=pltpu.CompilerParams(
+            vmem_limit_bytes=62 * 2**20, **(dict(collective_id=3, has_side_effects=True) if host else {})
+        ),
         name="forward_0",
     )(*ins)
-    return y, saved
-
-
-def backward(g, x, saved, w, before, small1, host=None, early=()):
+    return y, saved[:10], saved[10:]
+
+
+def backward(g, x, saved, w, before, small1, host=None, early=(), ys=()):
     rows, width, pairs, parts, part = sizes_of(x, w)
     slots = rows
     a, v, p, first_slope, c, b, hid, probs, q, slope = saved
@@ -1103,8 +1160,8 @@
     specs += [pl.BlockSpec((1, rows, 2 * slots), lambda i: (pair(i), 0, 0)), inner_block, outer_block, second_block]
     specs += [FAR] * 10
     aliases = {len(ins) + j: 2 + j for j in range(3)}
-    ins += list(before) + list(early)
-    specs += [FAR] * (3 + len(early))
+    ins += list(before) + list(early) + list(ys)
+    specs += [FAR] * (3 + len(early) + len(ys))
     outs = [like((rows, width)), like(w.outer.shape[1:])] + [like(k.shape, k.dtype) for k in before]
     out_specs = [whole_out((rows, width)), pl.BlockSpec((part, width), lambda i: (piece(i), 0)), inner_block]
     out_specs += [whole_out(w.out.shape, 0), whole_out(w.value.shape, 0)]
@@ -1114,9 +1171,9 @@
     gx, *grads = pl.pallas_call(
         functools.partial(backward_kernel, pairs, parts, host),
         grid=(pairs + parts,),
-        out_shape=outs + sums_of,
+        out_shape=outs + sums_of + [like(y.shape[1:]) for y in ys],
         in_specs=specs,
-        out_specs=out_specs + [whole_out(e.shape) for e in sums_of],
+        out_specs=out_specs + [whole_out(e.shape) for e in sums_of] + [FAR] * len(ys),
         scratch_shapes=[pltpu.VMEM(k.shape[-2:], k.dtype) for k in far]
         + [pltpu.VMEM((rows, width), jnp.float32)] * 2
         + [pltpu.VMEM((rows, width), jnp.bfloat16)] * 3
@@ -1124,7 +1181,7 @@
         + [pltpu.VMEM((8, width), jnp.float32)] * 2
         + [pltpu.VMEM((1, part * parts), jnp.float32), pltpu.VMEM((1, w.second.shape[1]), jnp.float32)]
         + [pltpu.SemaphoreType.DMA((10,))]
-        + (sum_scratch(host[0], early, host[1]) if host else []),
+        + (sum_scratch(host[0], early, host[1]) + [pltpu.SemaphoreType.DMA((2,))] if host else []),
         input_output_aliases=aliases,
         compiler_params=pltpu.CompilerParams(
             vmem_limit_bytes=63 * 2**20, **(dict(collective_id=2, has_side_effects=True) if host else {})
@@ -1134,7 +1191,7 @@
     return gx, grads[:7], grads[7:]
 
 
-def both_ways(x, g, length, w):
+def both_ways(x, g, lengths, w):
     rows, width, pairs, parts, part = sizes_of(x, w)
     slots = rows
 
@@ -1151,7 +1208,7 @@
     def late(i):
         return parts - 1 - jnp.clip(i - pairs - parts, 0, parts - 1)
 
-    ins = [length, x, g, w.small, w.value, w.out, w.table, w.inner, w.outer]
+    ins = [lengths, x, g, w.small, w.value, w.out, w.table, w.inner, w.outer]
     specs = [pl.BlockSpec(memory_space=pltpu.SMEM), whole(x.shape, 0), whole(g.shape, 1)]
     specs += [whole(w.small.shape), whole(w.value.shape, 1), whole(w.out.shape, 1)]
     specs += [
@@ -1194,32 +1251,28 @@
 MATRICES = (2, 4, 8, 10, 12, 14, 16)
 SMALL = 17
 GATHER = (
-    (8, 0, "xzy", 2),
-    (SMALL, None, "xzy", 3),
-    (10, 1, "zyx", 1),
-    (2, None, "zyx", 0),
-    (16, 0, "zxy", 1),
-    (10, 0, "yzx", 2),
-    (12, None, "zyx", 0),
-    (16, 1, "xzy", 0),
-    (8, 1, "yzx", 2),
-    (4, None, "zyx", 0),
-    (14, 0, "xzy", 2),
-    (14, 1, "xzy", 0),
+    (12, None, "zyx", 2),
+    (4, None, "zyx", 2),
+    (14, 0, "xzy", 3),
+    (SMALL, None, "zyx", 3),
+    (2, None, "xzy", 0),
+    (14, 1, "yzx", 2),
+    (10, None, "xzy", 1),
+    (8, None, "zyx", 0),
 )
+LATE = ((16, 0, "zyx", 0), (16, 1, "xzy", 0))
+BESIDE_FORWARD = (0, 1, 3, 5, 7, 9)
 EARLY = ((10, 1, "yzx", 1, 1), (10, 0, "yzx", 0, 1), (16, 1, "yxz", 1, None), (16, 0, "xzy", 1, None))
-BESIDE = (0, 0, 1, 3, 4, 7, 9)
+BESIDE_BACKWARD = (0, 0, 1, 3, 4, 7, 9)
 SUM = (
-    (8, 1, "yzx", 4, None),
-    (14, 1, "yxz", 5, None),
-    (10, 1, "yzx", 2, 0),
-    (12, None, "xzy", 2, None),
-    (8, 0, "xyz", 3, None),
     (4, None, "yzx", 0, None),
-    (10, 0, "yzx", 2, 0),
-    (2, None, "xzy", 2, None),
-    (SMALL, None, "xyz", 5, None),
-    (14, 0, "xzy", 4, None),
+    (14, 1, "yzx", 1, None),
+    (10, None, "yzx", 2, 0),
+    (2, None, "yzx", 3, None),
+    (12, None, "yxz", 2, None),
+    (14, 0, "xzy", 1, None),
+    (8, None, "xyz", 2, None),
+    (SMALL, None, "xzy", 2, None),
 )
 
 
@@ -1246,30 +1299,37 @@
 def per_device(mesh, boundary, lengths, *parts):
     nx, ndp = mesh.shape["segment"], mesh.shape["dp"]
     devices = nx * ndp
-    first = lax.axis_index("segment") == 0
-    length = jnp.where(first, lengths[0], lengths[1])
+    fast = nx == 2 and ndp == 16
     sizes = [parts[k].size for k in VECTORS]
 
     shards = {k: parts[k].reshape(parts[k].shape[-2:]) for k in MATRICES}
     shards[SMALL] = [parts[k].reshape(1, -1) for k in VECTORS]
     full, pair = planned(gather_all, GATHER, shards, mesh, boundary[0, :, 0])
-    for k in MATRICES:
+    if not fast:
+        full[16] = lax.all_gather(half(shards[16]), AXES, axis=0)
+    for k in full:
+        if k == SMALL:
+            continue
         g = full[k]
         full[k] = g.reshape((nx, ndp * g.shape[1]) + g.shape[2:]) if k < 12 else g.reshape(-1, g.shape[2])
-    w = Weights(full[SMALL], full[2], full[4], full[8], full[10], full[12], full[14], full[16])
-
-    outs, saved = forward(pair, length, w)
-    outs, gin1, (g_outer1, *both, g_small, g_table) = both_ways(outs, pair, length, w)
-    other_outs = from_other(outs[0], outs[1])
+    w = Weights(full[SMALL], full[2], full[4], full[8], full[10], full[12], full[14], full.get(16))
+
+    if fast:
+        outs, saved, (table,) = forward(pair, lengths, w, (numbered(LATE)[1], ndp // 4), [shards[16]])
+        w = w._replace(table=table.reshape(-1, table.shape[-1]))
+    else:
+        outs, saved, _ = forward(pair, lengths, w)
+    outs, gin1, (g_outer1, *both, g_small, g_table) = both_ways(outs, pair, lengths, w)
     early = {16: g_table.reshape((devices,) + parts[16].shape), 10: g_outer1.reshape((ndp,) + parts[10].shape[1:])}
     names, plan = numbered(EARLY)
     early = [early[k] for k in names]
-    if nx == 2 and ndp == 16:
+    if fast:
         host, hosted = (plan, ndp // 4), by_chip(early, plan, ndp // 4)
-        gin0, grads, sums_early = backward(gin1, pair, saved, w, both, g_small, host, hosted)
+        gin0, grads, (*sums_early, other_outs) = backward(gin1, pair, saved, w, both, g_small, host, hosted, [outs])
     else:
         gin0, grads, _ = backward(gin1, pair, saved, w, both, g_small)
         sums_early = plain_sums(early, plan)
+        other_outs = from_other(outs[0], outs[1])
     sums_early = dict(zip(names, sums_early))
 
     g_outer0, g_inner, g_out, g_value, g_small, g_first, g_second = grads

time: 452 us -> 434 us (0.960); the launches traced: 445 us -> 434 us
  Pallas kernels: 439 us -> 431 us
    pallas_call x1, Pallas kernels: 160 us -> 140 us  [gather_all(): pl.pallas_call(functools.partial(gather_kernel, plan, nz, small_at, count...]
    pallas_call x1, Pallas kernels: 30.4 us -> 42.8 us  [forward(): pl.pallas_call(functools.partial(forward_kernel, pairs, parts, host), gri...]
  transfers between devices with their start and end apart: 1 -> 0, of which waited for: 0 -> 0; matrix products, arithmetic and copies ran while one was open for 0% -> 0% of each run, Pallas kernels for 43% -> 0%
where the time goes in v7:
time: 434 us
  Pallas kernels  431 us (99%)
    pallas_call x1, Pallas kernels, gather_all(): pl.pallas_call(functools.partial(gather_kernel, plan, nz, small_at, count...  140 us
    pallas_call x1, Pallas kernels, scatter_all(): pl.pallas_call(functools.partial(scatter_kernel, plan, nz), out_shape=[ja...  120 us
    pallas_call x1, Pallas kernels, backward(): pl.pallas_call(functools.partial(backward_kernel, pairs, parts, host), gr...  72.7 us
    pallas_call x1, Pallas kernels, both_ways(): pl.pallas_call(functools.partial(both_kernel, pairs, parts), grid=(2 * pa...  49.9 us
    pallas_call x1, Pallas kernels, forward(): pl.pallas_call(functools.partial(forward_kernel, pairs, parts, host), gri...  42.8 us

profile of v7, /device:TPU:0, one launch (start us, length us, event | category | flops | bytes accessed | tf_op | source)
XLA Modules:
  0.0 433.5 jit_solution(17672822570782725135)
XLA Ops:
  0.7 1.3 copy.43.length_ref
  2.0 139.8 %gather_weights.1 = (bf16[2,4,2,2,24,768]{5,4,3,2,1,0:T(8,128)(2,1)}, bf16[2,4,2,2,48,768]{5,4,3,2,1,0:T(8,128)(2,1)}, bf16[2,4,2,2,24,6144]{5,4,3,2,1,0:T(8,128...) custom-call(f32[24,768]{1,0:T(8,128)} %refs_0_.2, ...), custom_call_target="tpu_custom_call" | custom-call | tf_op jit(solution)/shard_map/gather_weights/pallas_call | solution.py:271
  141.8 42.8 %forward_0.1 = (bf16[2,512,768]{2,1,0:T(8,128)(2,1)}, bf16[512,768]{1,0:T(8,128)(2,1)}, bf16[512,768]{1,0:T(8,128)(2,1)}, bf16[512,768]{1,0:T(8,128)(2,1)}, bf16...) custom-call(s32[2,1]{1,0:T(2,128)} %copy.43.length_ref, ...), custom_call_target="tpu_custom_call" | custom-call | tf_op jit(solution)/shard_map/forward_0/pallas_call | solution.py:1112
  184.6 49.9 %forward_backward_1.1 = (bf16[2,512,768]{2,1,0:T(8,128)(2,1)}, bf16[512,768]{1,0:T(8,128)(2,1)}, bf16[3072,768]{1,0:T(8,128)(2,1)}, bf16[2,768,3072]{2,1,0:T(8,1...) custom-call(s32[2,1]{1,0:T(2,128)} %copy.43.length_ref, ...), custom_call_target="tpu_custom_call", output_to_operand_aliasing={{0}: (1, {})} | custom-call | tf_op jit(solution)/shard_map/forward_backward_1/pallas_call | solution.py:1230
  234.5 72.7 %backward_0.1 = (bf16[512,768]{1,0:T(8,128)(2,1)}, bf16[3072,768]{1,0:T(8,128)(2,1)}, bf16[2,768,3072]{2,1,0:T(8,128)(2,1)}, bf16[2,768,768]{2,1,0:T(8,128)(2,1)...) custom-call(bf16[512,768]{1,0:T(8,128)(2,1)} %get-tuple-element.96.g, ...), custom_call_target="tpu_custom_call", output_to_operand_aliasing={{2}: (20, {}), {3}: (21, {}), {4}: (22, {})} | custom-call | tf_op jit(solution)/shard_map/backward_0/pallas_call | solution.py:1171
  307.2 119.9 %sum_gradients.1 = (f32[48,768]{1,0:T(8,128)}, f32[24,6144]{1,0:T(8,128)}, f32[192,768]{1,0:T(8,128)}, f32[48,768]{1,0:T(8,128)}, f32[24,768]{1,0:T(8,128)}, /*i...) custom-call(bf16[2,4,2,2,48,768]{5,4,3,2,1,0:T(8,128)(2,1)} %bitcast.52, ...), custom_call_target="tpu_custom_call" | custom-call | tf_op jit(solution)/shard_map/sum_gradients/pallas_call | solution.py:563
  427.1 6.2 %finish.1 = (bf16[2,512,768]{2,1,0:T(8,128)(2,1)}, bf16[2,512,768]{2,1,0:T(8,128)(2,1)}, f32[48,768]{1,0:T(8,128)}, f32[48,768]{1,0:T(8,128)}, f32[48,3072]{1,0:...) custom-call(bf16[2,512,768]{2,1,0:T(8,128)(2,1)} %get-tuple-element., ...), custom_call_target="tpu_custom_call" | custom-call | tf_op jit(solution)/shard_map/finish/pallas_call | solution.py:528

commit v8 on v7

--- a/solution.py
+++ b/solution.py
@@ -974,9 +974,9 @@
 
 
 def both_kernel(pairs, parts, length_ref, x_ref, g_ref, small, value_ref, out_ref, table_ref, inner_ref, outer_ref, *refs):
-    y_ref, gx_ref, g_outer, g_inner, g_out, g_value, g_small, g_table = refs[:8]
+    y_ref, gx_ref, g_outer, g_inner, far_g_out, g_value, g_small, g_table = refs[:8]
     acc, hid_ref, ghid, a_ref, v_ref, c_ref, b_ref, gatt, gc_ref, gv_ref, probs_ref, q_ref, slope_ref, db, gz_ref, *refs = refs[8:]
-    vectors, inner_b, g_vec, g_inner_b = refs
+    vectors, inner_b, g_vec, g_inner_b, near_g, near_out, g_out, sem = refs
     i = pl.program_id(0)
     slots = probs_ref.shape[2] // 2
     j = i - pairs
@@ -994,13 +994,19 @@
     def hidden(ref, k):
         return ref.at[:, pl.ds(pl.multiple_of(k * part, part), part)]
 
-    x_ref, g_ref, y_ref = (ref.at[0] for ref in (x_ref, g_ref, y_ref))
+    load_out = pltpu.make_async_copy(out_ref.at[1], near_out, sem.at[0])
+    load_g = pltpu.make_async_copy(g_ref.at[1], near_g, sem.at[1])
+    store_out = pltpu.make_async_copy(g_out, far_g_out.at[1], sem.at[2])
+    x_ref, y_ref = x_ref.at[0], y_ref.at[0]
+    g_ref, out_ref = near_g, near_out
 
     def read(r):
         return wide(x_ref[r, :])
 
     @pl.when(i == 0)
     def _():
+        load_out.start()
+        load_g.start()
         unpack_vectors(small, ndp, ndp, vectors)
         unpack_rows(small, ndp, ndp, VECTOR_ROWS, inner_b)
         forward_start(read, vec, value_ref.at[0], a_ref, v_ref)
@@ -1014,7 +1020,9 @@
 
     @pl.when(i == pairs - 1)
     def _():
-        forward_middle(read, vec, out_ref.at[0], c_ref, hid_ref, b_ref)
+        load_out.wait()
+        load_g.wait()
+        forward_middle(read, vec, out_ref, c_ref, hid_ref, b_ref)
 
     @pl.when((j >= 0) & (j < parts))
     def _():
@@ -1031,7 +1039,8 @@
 
     @pl.when(k == parts - 1)
     def _():
-        backward_middle(vec, put, g_ref, hid_ref, c_ref, out_ref.at[0], acc, ghid, gatt, gc_ref, g_out.at[0])
+        backward_middle(vec, put, g_ref, hid_ref, c_ref, out_ref, acc, ghid, gatt, gc_ref, g_out)
+        store_out.start()
 
     @pl.when(n >= 0)
     def _():
@@ -1045,6 +1054,7 @@
         g_small[...] = jnp.zeros_like(g_small)
         pack_vectors(g_vec, ndp, g_small, 0)
         pack_rows(g_inner_b, ndp, VECTOR_ROWS, g_small, 0)
+        store_out.wait()
 
 
 class Weights(NamedTuple):
@@ -1209,8 +1219,8 @@
         return parts - 1 - jnp.clip(i - pairs - parts, 0, parts - 1)
 
     ins = [lengths, x, g, w.small, w.value, w.out, w.table, w.inner, w.outer]
-    specs = [pl.BlockSpec(memory_space=pltpu.SMEM), whole(x.shape, 0), whole(g.shape, 1)]
-    specs += [whole(w.small.shape), whole(w.value.shape, 1), whole(w.out.shape, 1)]
+    specs = [pl.BlockSpec(memory_space=pltpu.SMEM), whole(x.shape, 0), FAR]
+    specs += [whole(w.small.shape), whole(w.value.shape, 1), FAR]
     specs += [
         pl.BlockSpec((2 * slots, slots), lambda i: (there(i), 0)),
         pl.BlockSpec((1, width, part), lambda i: (1, 0, piece(i))),
@@ -1222,7 +1232,7 @@
     grad_specs = [
         pl.BlockSpec((part, width), lambda i: (late(i), 0)),
         pl.BlockSpec((1, width, part), lambda i: (1, 0, late(i))),
-        whole_out(w.out.shape, 1),
+        FAR,
         whole_out(w.value.shape, 1),
         whole_out(small),
         pl.BlockSpec((2 * slots, slots), lambda i: (back(i), 0)),
@@ -1238,7 +1248,10 @@
         + [pltpu.VMEM((pairs, rows, 2 * slots), jnp.bfloat16)]
         + [pltpu.VMEM((parts, rows, part), jnp.bfloat16)] * 2
         + [pltpu.VMEM((rows, 2 * slots), jnp.bfloat16), pltpu.VMEM((rows, part), jnp.bfloat16)]
-        + [pltpu.VMEM((8, width), jnp.float32), pltpu.VMEM((1, part * parts), jnp.float32)] * 2,
+        + [pltpu.VMEM((8, width), jnp.float32), pltpu.VMEM((1, part * parts), jnp.float32)] * 2
+        + [pltpu.VMEM((rows, width), jnp.bfloat16)]
+        + [pltpu.VMEM(w.out.shape[1:], jnp.bfloat16)] * 2
+        + [pltpu.SemaphoreType.DMA((3,))],
         input_output_aliases={1: 0},
         compiler_params=pltpu.CompilerParams(vmem_limit_bytes=62 * 2**20),
         name="forward_backward_1",
@@ -1263,7 +1276,7 @@
 LATE = ((16, 0, "zyx", 0), (16, 1, "xzy", 0))
 BESIDE_FORWARD = (0, 1, 3, 5, 7, 9)
 EARLY = ((10, 1, "yzx", 1, 1), (10, 0, "yzx", 0, 1), (16, 1, "yxz", 1, None), (16, 0, "xzy", 1, None))
-BESIDE_BACKWARD = (0, 0, 1, 3, 4, 7, 9)
+BESIDE_BACKWARD = (0, 0, 1, 3, 4, 8)
 SUM = (
     (4, None, "yzx", 0, None),
     (14, 1, "yzx", 1, None),

time: 434 us -> 431 us (level)
  no operation moved by 1% of the time
where the time goes in v8:
time: 431 us
  Pallas kernels  429 us (100%)
    pallas_call x1, Pallas kernels, gather_all(): pl.pallas_call(functools.partial(gather_kernel, plan, nz, small_at, count...  140 us
    pallas_call x1, Pallas kernels, scatter_all(): pl.pallas_call(functools.partial(scatter_kernel, plan, nz), out_shape=[ja...  121 us
    pallas_call x1, Pallas kernels, backward(): pl.pallas_call(functools.partial(backward_kernel, pairs, parts, host), gr...  70.2 us
    pallas_call x1, Pallas kernels, both_ways(): pl.pallas_call(functools.partial(both_kernel, pairs, parts), grid=(2 * pa...  48.9 us
    pallas_call x1, Pallas kernels, forward(): pl.pallas_call(functools.partial(forward_kernel, pairs, parts, host), gri...  42.8 us

profile of v8, /device:TPU:0, one launch (start us, length us, event | category | flops | bytes accessed | tf_op | source)
XLA Modules:
  0.0 431.0 jit_solution(13843861635423739146)
XLA Ops:
  0.7 1.3 copy.43.length_ref
  2.0 139.8 %gather_weights.1 = (bf16[2,4,2,2,24,768]{5,4,3,2,1,0:T(8,128)(2,1)}, bf16[2,4,2,2,48,768]{5,4,3,2,1,0:T(8,128)(2,1)}, bf16[2,4,2,2,24,6144]{5,4,3,2,1,0:T(8,128...) custom-call(f32[24,768]{1,0:T(8,128)} %refs_0_.2, ...), custom_call_target="tpu_custom_call" | custom-call | tf_op jit(solution)/shard_map/gather_weights/pallas_call | solution.py:271
  141.8 42.8 %forward_0.1 = (bf16[2,512,768]{2,1,0:T(8,128)(2,1)}, bf16[512,768]{1,0:T(8,128)(2,1)}, bf16[512,768]{1,0:T(8,128)(2,1)}, bf16[512,768]{1,0:T(8,128)(2,1)}, bf16...) custom-call(s32[2,1]{1,0:T(2,128)} %copy.43.length_ref, ...), custom_call_target="tpu_custom_call" | custom-call | tf_op jit(solution)/shard_map/forward_0/pallas_call | solution.py:1122
  184.6 48.9 %forward_backward_1.1 = (bf16[2,512,768]{2,1,0:T(8,128)(2,1)}, bf16[512,768]{1,0:T(8,128)(2,1)}, bf16[3072,768]{1,0:T(8,128)(2,1)}, bf16[2,768,3072]{2,1,0:T(8,1...) custom-call(s32[2,1]{1,0:T(2,128)} %copy.43.length_ref, ...), custom_call_target="tpu_custom_call", output_to_operand_aliasing={{0}: (1, {})} | custom-call | tf_op jit(solution)/shard_map/forward_backward_1/pallas_call | solution.py:1240
  233.5 70.2 %backward_0.1 = (bf16[512,768]{1,0:T(8,128)(2,1)}, bf16[3072,768]{1,0:T(8,128)(2,1)}, bf16[2,768,3072]{2,1,0:T(8,128)(2,1)}, bf16[2,768,768]{2,1,0:T(8,128)(2,1)...) custom-call(bf16[512,768]{1,0:T(8,128)(2,1)} %get-tuple-element.96.g, ...), custom_call_target="tpu_custom_call", output_to_operand_aliasing={{2}: (20, {}), {3}: (21, {}), {4}: (22, {})} | custom-call | tf_op jit(solution)/shard_map/backward_0/pallas_call | solution.py:1181
  303.6 120.9 %sum_gradients.1 = (f32[48,768]{1,0:T(8,128)}, f32[24,6144]{1,0:T(8,128)}, f32[192,768]{1,0:T(8,128)}, f32[48,768]{1,0:T(8,128)}, f32[24,768]{1,0:T(8,128)}, /*i...) custom-call(bf16[2,4,2,2,48,768]{5,4,3,2,1,0:T(8,128)(2,1)} %bitcast.52, ...), custom_call_target="tpu_custom_call" | custom-call | tf_op jit(solution)/shard_map/sum_gradients/pallas_call | solution.py:563
  424.6 6.2 %finish.1 = (bf16[2,512,768]{2,1,0:T(8,128)(2,1)}, bf16[2,512,768]{2,1,0:T(8,128)(2,1)}, f32[48,768]{1,0:T(8,128)}, f32[48,768]{1,0:T(8,128)}, f32[48,3072]{1,0:...) custom-call(bf16[2,512,768]{2,1,0:T(8,128)(2,1)} %get-tuple-element., ...), custom_call_target="tpu_custom_call" | custom-call | tf_op jit(solution)/shard_map/finish/pallas_call | solution.py:528
